TPU v7x, 512 devices: a whole 4x4x16 slice. The times are simulated.
512 devices in a mesh: tiles: 32 (over z, core), sub: 16 (over y, x).
Axes of the slice: x: 4, y: 4, z: 16, core: 2. Of those that a mesh axis runs over, the one named last changes fastest.
Arguments:
- strips: bfloat16 [64, 4, 128, 32, 256], P('tiles', None, 'sub'), may hold values from -16 to 16
- pair_tiles: int32 [108, 2], replicated, may hold values from 0 to 63, as said below
- pair_owner: int32 [108], replicated, may hold values from 0 to 31, as said below
- pair_offset: int32 [108, 3], replicated, may hold values from -5 to 5
Outputs:
- windows: float32 [192, 729], P('tiles')
- normal_matrix: float32 [64, 64], replicated
- normal_rhs: float32 [64, 3], replicated
Inputs may be any that keep to these rules, and one draw needn't show every extreme that they name: `pair_tiles`: tiles are numbered row by row in rows of 4; each row names a = the left or upper tile and b = a + 1 in the same row or b = a + 4; every adjacent pair is listed exactly once. `pair_owner`: tile t lies on index t // 2 of tiles; the owner of a pair is the index that holds tile a or the index that holds tile b; no index owns more than 6 pairs, and some index owns exactly 6.
All inputs are finite; a program needn't handle non-finite values.
Results may differ from a plain program's by a relative error of at most 0.0003.
Values may be sent and summed in bfloat16 or wider, within the bound.
No kernel may reach another device: no remote copies, remote signals or barrier semaphores. Data moves between devices by JAX's collectives and lax.ppermute only.
A program may use at most 64 MiB of HBM per device.

v0:
```python
import jax
import jax.numpy as jnp
from jax import lax
from jax.sharding import PartitionSpec as P

REACH = 4
WIN = 9


HIGHEST_PREC = lax.Precision.HIGHEST
EPSILON = 1e-06
FLOOR_SHARE = 0.05


def swapped(block, axis, bit):
    count = lax.axis_size(axis)
    route = []
    for low in range(count):
        high = low | 1 << bit
        if high != low and high < count:
            route += [(low, high), (high, low)]
    return lax.ppermute(block, axis, route)


def from_behind(shard, axis, by):
    count = lax.axis_size(axis)
    pairs = [(i, i + by) for i in range(count) if 0 <= i + by < count]
    return lax.ppermute(shard, axis, pairs)


def twiddle(length, row_index, col_index):
    residue = row_index[:, None] * col_index[None, :] % length
    radians = residue.astype(jnp.float32) * (2.0 * jnp.pi / length)
    return (jnp.cos(radians), jnp.sin(radians))


def spectrum(batch_in):
    planes = batch_in.shape[1]
    across = batch_in.shape[2]
    along_len = batch_in.shape[3]
    depth_full = planes * lax.axis_size("sub")
    voxels = batch_in.astype(jnp.float32)
    along_pos = jnp.arange(along_len, dtype=jnp.int32)
    cos_along, sin_along = twiddle(along_len, along_pos, along_pos)
    real_one = jnp.einsum("nzab,bk->nkaz", voxels, cos_along, precision=HIGHEST_PREC)
    imag_one = -jnp.einsum("nzab,bk->nkaz", voxels, sin_along, precision=HIGHEST_PREC)
    across_freq = jnp.arange(across, dtype=jnp.int32)
    cos_across, sin_across = twiddle(across, across_freq, across_freq)
    real_two = jnp.einsum(
        "nkaz,ac->nkcz", real_one, cos_across, precision=HIGHEST_PREC
    ) + jnp.einsum("nkaz,ac->nkcz", imag_one, sin_across, precision=HIGHEST_PREC)
    imag_two = jnp.einsum(
        "nkaz,ac->nkcz", imag_one, cos_across, precision=HIGHEST_PREC
    ) - jnp.einsum("nkaz,ac->nkcz", real_one, sin_across, precision=HIGHEST_PREC)
    gathered = lax.all_to_all(
        jnp.stack([real_two, imag_two], axis=1), "sub", split_axis=2, concat_axis=4, tiled=True
    )
    depth_freq = jnp.arange(depth_full, dtype=jnp.int32)
    cos_depth, sin_depth = twiddle(depth_full, depth_freq, depth_freq)
    real_three = jnp.einsum(
        "nkaz,zw->nkaw", gathered[:, 0], cos_depth, precision=HIGHEST_PREC
    ) + jnp.einsum("nkaz,zw->nkaw", gathered[:, 1], sin_depth, precision=HIGHEST_PREC)
    imag_three = jnp.einsum(
        "nkaz,zw->nkaw", gathered[:, 1], cos_depth, precision=HIGHEST_PREC
    ) - jnp.einsum("nkaz,zw->nkaw", gathered[:, 0], sin_depth, precision=HIGHEST_PREC)
    return jnp.stack([real_three, imag_three], axis=1)


def window_part(pair_data, offset, freq_start):
    along_share, across, depth_full = (pair_data.shape[2], pair_data.shape[3], pair_data.shape[4])
    along_len = along_share * lax.axis_size("sub") * 1
    voxel_count = along_len * across * depth_full
    along_freq = freq_start + jnp.arange(along_share, dtype=jnp.int32)
    weights = jnp.ones((along_share,), jnp.float32)
    first_real, first_imag = (pair_data[0, 0], pair_data[0, 1])
    second_real, second_imag = (pair_data[1, 0], pair_data[1, 1])
    cross_real = first_real * second_real + first_imag * second_imag
    cross_imag = first_imag * second_real - first_real * second_imag
    normal_factor = lax.rsqrt(
        cross_real * cross_real + cross_imag * cross_imag + (FLOOR_SHARE * voxel_count) ** 2
    )
    phase_real = cross_real * normal_factor
    phase_imag = cross_imag * normal_factor
    window_steps = jnp.arange(WIN, dtype=jnp.int32) - REACH
    cos_depth, sin_depth = twiddle(
        depth_full, jnp.arange(depth_full, dtype=jnp.int32), offset[0] + window_steps
    )
    one_real = jnp.einsum(
        "kaz,zw->kaw", phase_real, cos_depth, precision=HIGHEST_PREC
    ) - jnp.einsum("kaz,zw->kaw", phase_imag, sin_depth, precision=HIGHEST_PREC)
    one_imag = jnp.einsum(
        "kaz,zw->kaw", phase_real, sin_depth, precision=HIGHEST_PREC
    ) + jnp.einsum("kaz,zw->kaw", phase_imag, cos_depth, precision=HIGHEST_PREC)
    cos_across, sin_across = twiddle(
        across, jnp.arange(across, dtype=jnp.int32), offset[1] + window_steps
    )
    two_real = jnp.einsum("kaw,av->kvw", one_real, cos_across, precision=HIGHEST_PREC) - jnp.einsum(
        "kaw,av->kvw", one_imag, sin_across, precision=HIGHEST_PREC
    )
    two_imag = jnp.einsum("kaw,av->kvw", one_real, sin_across, precision=HIGHEST_PREC) + jnp.einsum(
        "kaw,av->kvw", one_imag, cos_across, precision=HIGHEST_PREC
    )
    cos_along, sin_along = twiddle(along_len, along_freq, offset[2] + window_steps)
    cos_along = cos_along * weights[:, None]
    sin_along = sin_along * weights[:, None]
    partial_sum = jnp.einsum(
        "kvw,ku->wvu", two_real, cos_along, precision=HIGHEST_PREC
    ) - jnp.einsum("kvw,ku->wvu", two_imag, sin_along, precision=HIGHEST_PREC)
    return partial_sum.reshape(-1) / voxel_count


def fetch(source_kind, position, tables):

    def take_from(source_table):
        return lambda: lax.dynamic_index_in_dim(source_table, position, 0, keepdims=False)

    return lax.switch(source_kind, [take_from(source_table) for source_table in tables])


def local(strips, pair_tiles, pair_owner, pair_offset):
    tile_dev = strips.shape[0]
    owner_index = lax.axis_index("tiles")
    devices = lax.axis_size("tiles")
    tiles_all = tile_dev * devices
    capacity = 3 * tile_dev
    left_half = owner_index % 2 == 0
    first_tile = pair_tiles[:, 0]
    second_tile = pair_tiles[:, 1]
    across_seam = second_tile - first_tile == 1
    side_first = jnp.where(across_seam, 1, 3)
    side_second = jnp.where(across_seam, 0, 2)
    owned_here = pair_owner == owner_index
    pair_count = pair_owner.shape[0]
    before = jnp.arange(pair_count)[:, None] > jnp.arange(pair_count)[None, :]
    ordinal = jnp.sum(before & owned_here[None, :], axis=1)
    chosen = (owned_here[None, :] & (ordinal[None, :] == jnp.arange(capacity)[:, None])).astype(
        jnp.int32
    )
    filled = jnp.sum(chosen, axis=1).astype(jnp.float32)
    slot_first = jnp.sum(chosen * first_tile[None, :], axis=1)
    slot_second = jnp.sum(chosen * second_tile[None, :], axis=1)
    slot_side_first = jnp.sum(chosen * side_first[None, :], axis=1)
    slot_side_second = jnp.sum(chosen * side_second[None, :], axis=1)
    slot_offset = jnp.sum(chosen[:, :, None] * pair_offset[None, :, :], axis=1)

    def locate(tile_number, side_code):
        at_home = tile_number // tile_dev == owner_index
        remote = jnp.select([side_code == 1, side_code == 0, side_code == 3], [1, 2, 3], 4)
        source_kind = jnp.where(at_home, 0, remote)
        position = jnp.where(
            at_home,
            tile_number % tile_dev * 4 + side_code,
            jnp.where(side_code >= 2, tile_number % tile_dev, 0),
        )
        return (source_kind, position)

    kind_first, pos_first = locate(slot_first, slot_side_first)
    kind_second, pos_second = locate(slot_second, slot_side_second)
    along_share = strips.shape[4] // lax.axis_size("sub") // 1
    freq_start = lax.axis_index("sub") * along_share
    slot_data = (kind_first, pos_first, kind_second, pos_second, slot_offset)

    def per_tile(carried, tile_sides):
        return (carried, spectrum(tile_sides))

    ignored, spectra = lax.scan(per_tile, 0, strips)
    spectra = spectra.reshape((tile_dev * 4,) + spectra.shape[2:])
    seam_piece = jnp.where(left_half, spectra[-3:-2], spectra[0:1])
    partner = swapped(seam_piece.astype(jnp.bfloat16), "tiles", 0).astype(seam_piece.dtype)
    from_above = from_behind(spectra[3::4].astype(jnp.bfloat16), "tiles", 2).astype(jnp.float32)
    from_below = from_behind(spectra[2::4].astype(jnp.bfloat16), "tiles", -2).astype(jnp.float32)
    tables = (spectra, partner, partner, from_above, from_below)

    def per_slot(carried, slot_items):
        pair_data = jnp.stack(
            [
                fetch(slot_items[0], slot_items[1], tables),
                fetch(slot_items[2], slot_items[3], tables),
            ]
        )
        return (carried, window_part(pair_data, slot_items[4], freq_start))

    ignored, partials = lax.scan(per_slot, 0, slot_data)
    windows = lax.psum(partials, "sub") * filled[:, None]
    win_index = jnp.arange(WIN * WIN * WIN, dtype=jnp.int32)
    displace = (
        jnp.stack([win_index // (WIN * WIN), win_index // WIN % WIN, win_index % WIN], axis=1)
        - REACH
    )
    squares = windows * windows
    energy = jnp.sum(squares, axis=1)
    estimate = (
        slot_offset.astype(jnp.float32)
        + jnp.dot(squares, displace.astype(jnp.float32), precision=HIGHEST_PREC)
        / (energy + EPSILON)[:, None]
    )
    tile_ids = jnp.arange(tiles_all, dtype=jnp.int32)
    incidence = (
        (slot_first[:, None] == tile_ids[None, :]).astype(jnp.float32)
        - (slot_second[:, None] == tile_ids[None, :]).astype(jnp.float32)
    ) * filled[:, None]
    weighted = incidence * energy[:, None]
    matrix_part = jnp.dot(weighted.T, incidence, precision=HIGHEST_PREC)
    load_part = jnp.dot(weighted.T, estimate, precision=HIGHEST_PREC)
    normal_matrix, normal_rhs = lax.psum((matrix_part, load_part), "tiles")
    return (windows, normal_matrix, normal_rhs)


def solution(mesh):
    in_specs = (P("tiles", None, "sub", None, None), P(), P(), P())
    out_specs = (P("tiles", None), P(), P())
    return jax.shard_map(local, mesh=mesh, in_specs=in_specs, out_specs=out_specs, check_vma=False)
```

profile of v0, /device:TPU:1, one launch (start us, length us, event | category | flops | bytes accessed | tf_op | source)
XLA Modules:
  0.0 545.1 jit_solution(7130668344387919780)
XLA Ops:
  0.7 222.9 %while.26 = (s32[]{:T(128)}, f32[2,4,2,16,32,128]{5,4,3,2,1,0:T(8,128)}, bf16[2,4,8,32,256]{4,3,2,1,0:T(8,128)(2,1)}, s32[]{:T(128)}, f32[]{:T(128)}) while((s32[]{:T(128)}, f32[2,4,2,16,32,128]{5,4,3,2,1,0:T(8,128)}, bf16[2,4,8,32,256]{4,3,2,1,0:T(8,128)(2,1)}, s32[]{:T(128)}, f32[]{:T(128)}) %tuple.220), condition=%wide.region_9.10_spmd, body=%wide.region_8.9_spmd.sunk | while | flops 3629047808 | bytes 114294984 | solution.py:166
  10.7 7.5 %copy.82 = f32[4,2,256,32,8]{3,4,0,1,2:T(8,128)} copy(f32[4,2,256,32,8]{2,3,4,0,1:T(8,128)S(1)} %pad_maximum_fusion.2) | data formatting | bytes 4194304 | tf_op jit(solution)/shard_map/while/body/eval_jaxpr/stack | solution.py:56
  18.3 8.6 %reshape.300 = f32[16,1,32768]{2,1,0:T(1,128)} reshape(f32[256,2,4,8,32]{4,3,2,1,0:T(8,128)} %bitcast.313) | data formatting | bytes 4194304 | tf_op jit(solution)/shard_map/while
  26.8 8.1 %all-to-all-start = ((f32[16,1,32768]{2,1,0:T(1,128)}), f32[16,1,32768]{2,1,0:T(1,128)S(1)}, u32[]{:S(2)}, u32[]{:S(2)}) async-start(f32[16,1,32768]{2,1,0:T(1,128)} %reshape.300), calls=%async_computation | async-start | bytes 4194304 | tf_op jit(solution)/shard_map/while/body/eval_jaxpr/all_to_all | solution.py:55
  34.9 25.2 %all-to-all-done = f32[16,1,32768]{2,1,0:T(1,128)S(1)} async-done(((f32[16,1,32768]{2,1,0:T(1,128)}), f32[16,1,32768]{2,1,0:T(1,128)S(1)}, u32[]{:S(2)}, u32[]{:S(2)}) %all-to-all-start) | async-done | bytes 2097184 | tf_op jit(solution)/shard_map/while/body/eval_jaxpr/all_to_all | solution.py:55
  62.0 7.3 %reduce.33 = f32[16,32768]{1,0:T(8,128)S(1)} reduce(f32[16,1,32768]{2,1,0:T(1,128)} %copy-done, f32[]{:T(128)} %broadcast.786), dimensions={1}, to_apply=%all_to_all.25.reduce_sub_computation | reduce | bytes 4194308 | tf_op jit(solution)/shard_map/while/body/eval_jaxpr/all_to_all | solution.py:55
  78.7 6.7 %fusion.319 = f32[4,16,32,128]{3,2,1,0:T(8,128)S(1)} fusion(f32[4,2,16,32,128]{3,4,2,1,0:T(8,128)S(1)} %bitcast.309), kind=kOutput, calls=%fused_computation.4.clone.1 | convolution fusion | flops 402882560 | bytes 5242880 | tf_op jit(solution)/shard_map/while/body/eval_jaxpr/nkaz,zw->nkaw/dot_general | solution.py:60
  85.5 6.7 %fusion.317 = f32[4,16,32,128]{3,2,1,0:T(8,128)S(1)} fusion(f32[4,2,16,32,128]{3,4,2,1,0:T(8,128)S(1)} %bitcast.310), kind=kOutput, calls=%fused_computation.3.clone.1 | convolution fusion | flops 402882560 | bytes 5242880 | tf_op jit(solution)/shard_map/while/body/eval_jaxpr/nkaz,zw->nkaw/dot_general | solution.py:65
  92.2 7.0 %fusion.320 = f32[4,1,16,32,128]{4,3,2,0,1:T(8,128)S(1)} fusion(f32[4,16,32,128]{3,2,1,0:T(8,128)S(1)} %fusion.319, f32[4,2,16,32,128]{3,4,2,1,0:T(8,128)S(1)} %bitcast.311), kind=kOutput, calls=%fused_computation.11.clone.1 | convolution fusion | flops 403144704 | bytes 6291456 | tf_op jit(solution)/shard_map/while/body/eval_jaxpr/nkaz,zw->nkaw/dot_general | solution.py:62
  99.2 6.7 %fusion.318 = f32[4,1,16,32,128]{4,3,2,0,1:T(8,128)S(1)} fusion(f32[4,16,32,128]{3,2,1,0:T(8,128)S(1)} %fusion.317, f32[4,2,16,32,128]{3,4,2,1,0:T(8,128)S(1)} %bitcast.312), kind=kOutput, calls=%fused_computation.13.clone.1 | convolution fusion | flops 403144704 | bytes 6291456 | tf_op jit(solution)/shard_map/while/body/eval_jaxpr/nkaz,zw->nkaw/dot_general | solution.py:63
  118.4 7.5 %copy.82 = f32[4,2,256,32,8]{3,4,0,1,2:T(8,128)} copy(f32[4,2,256,32,8]{2,3,4,0,1:T(8,128)S(1)} %pad_maximum_fusion.2) | data formatting | bytes 4194304 | tf_op jit(solution)/shard_map/while/body/eval_jaxpr/stack | solution.py:56
  125.9 8.6 %reshape.300 = f32[16,1,32768]{2,1,0:T(1,128)} reshape(f32[256,2,4,8,32]{4,3,2,1,0:T(8,128)} %bitcast.313) | data formatting | bytes 4194304 | tf_op jit(solution)/shard_map/while
  134.5 7.6 %all-to-all-start = ((f32[16,1,32768]{2,1,0:T(1,128)}), f32[16,1,32768]{2,1,0:T(1,128)S(1)}, u32[]{:S(2)}, u32[]{:S(2)}) async-start(f32[16,1,32768]{2,1,0:T(1,128)} %reshape.300), calls=%async_computation | async-start | bytes 4194304 | tf_op jit(solution)/shard_map/while/body/eval_jaxpr/all_to_all | solution.py:55
  142.1 27.4 %all-to-all-done = f32[16,1,32768]{2,1,0:T(1,128)S(1)} async-done(((f32[16,1,32768]{2,1,0:T(1,128)}), f32[16,1,32768]{2,1,0:T(1,128)S(1)}, u32[]{:S(2)}, u32[]{:S(2)}) %all-to-all-start) | async-done | bytes 2097184 | tf_op jit(solution)/shard_map/while/body/eval_jaxpr/all_to_all | solution.py:55
  171.4 7.3 %reduce.33 = f32[16,32768]{1,0:T(8,128)S(1)} reduce(f32[16,1,32768]{2,1,0:T(1,128)} %copy-done, f32[]{:T(128)} %broadcast.786), dimensions={1}, to_apply=%all_to_all.25.reduce_sub_computation | reduce | bytes 4194308 | tf_op jit(solution)/shard_map/while/body/eval_jaxpr/all_to_all | solution.py:55
  188.2 6.7 %fusion.319 = f32[4,16,32,128]{3,2,1,0:T(8,128)S(1)} fusion(f32[4,2,16,32,128]{3,4,2,1,0:T(8,128)S(1)} %bitcast.309), kind=kOutput, calls=%fused_computation.4.clone.1 | convolution fusion | flops 402882560 | bytes 5242880 | tf_op jit(solution)/shard_map/while/body/eval_jaxpr/nkaz,zw->nkaw/dot_general | solution.py:60
  194.9 6.7 %fusion.317 = f32[4,16,32,128]{3,2,1,0:T(8,128)S(1)} fusion(f32[4,2,16,32,128]{3,4,2,1,0:T(8,128)S(1)} %bitcast.310), kind=kOutput, calls=%fused_computation.3.clone.1 | convolution fusion | flops 402882560 | bytes 5242880 | tf_op jit(solution)/shard_map/while/body/eval_jaxpr/nkaz,zw->nkaw/dot_general | solution.py:65
  201.7 7.1 %fusion.320 = f32[4,1,16,32,128]{4,3,2,0,1:T(8,128)S(1)} fusion(f32[4,16,32,128]{3,2,1,0:T(8,128)S(1)} %fusion.319, f32[4,2,16,32,128]{3,4,2,1,0:T(8,128)S(1)} %bitcast.311), kind=kOutput, calls=%fused_computation.11.clone.1 | convolution fusion | flops 403144704 | bytes 6291456 | tf_op jit(solution)/shard_map/while/body/eval_jaxpr/nkaz,zw->nkaw/dot_general | solution.py:62
  208.8 6.7 %fusion.318 = f32[4,1,16,32,128]{4,3,2,0,1:T(8,128)S(1)} fusion(f32[4,16,32,128]{3,2,1,0:T(8,128)S(1)} %fusion.317, f32[4,2,16,32,128]{3,4,2,1,0:T(8,128)S(1)} %bitcast.312), kind=kOutput, calls=%fused_computation.13.clone.1 | convolution fusion | flops 403144704 | bytes 6291456 | tf_op jit(solution)/shard_map/while/body/eval_jaxpr/nkaz,zw->nkaw/dot_general | solution.py:63
  224.8 6.2 %collective-permute-start = (bf16[1,2,16,32,128]{4,3,2,1,0:T(8,128)(2,1)S(1)}, bf16[1,2,16,32,128]{4,3,2,1,0:T(8,128)(2,1)S(1)}, u32[]{:S(2)}, u32[]{:S(2)}) collective-permute-start(bf16[1,2,16,32,128]{4,3,2,1,0:T(8,128)(2,1)S(1)} %fusion.208), channel_id=1, source_target_pairs={{0,16},{16,0},{32,48},{48,32},{64,80},{80,64},{96,112},{112,96},{1... | collective-permute-start | bytes 786440 | tf_op jit(solution)/shard_map/ppermute | solution.py:22
  243.0 8.0 %collective-permute-done.1 = bf16[2,2,16,32,128]{4,3,2,1,0:T(8,128)(2,1)S(1)} collective-permute-done((bf16[2,2,16,32,128]{4,3,2,1,0:T(8,128)(2,1)S(1)}, bf16[2,2,16,32,128]{4,3,2,1,0:T(8,128)(2,1)S(1)}, u32[]{:S(2)}, u32[]{:S(2)}) %collective-permute-start.1) | collective-permute-done | bytes 524320 | tf_op jit(solution)/shard_map/ppermute | solution.py:28
  256.3 114.6 %while.27 = (s32[]{:T(128)}, f32[6,729]{1,0:T(8,128)S(1)}, s32[]{:T(128)}, s32[6,3]{0,1:T(4,128)S(1)}, s32[6]{0:T(128)S(1)}, /*index=5*/s32[6]{0:T(128)S(1)}, f3...) while((s32[]{:T(128)}, f32[6,729]{1,0:T(8,128)S(1)}, ...), condition=%wide.region_21.22_spmd, body=%wide.region_10.21_spmd.sunk | while | flops 32384096 | bytes 6020353 | solution.py:183
  370.9 55.9 %psum.21 = f32[6,729]{1,0:T(8,128)S(1)} all-reduce(f32[6,729]{1,0:T(8,128)S(1)} %get-tuple-element.437), channel_id=1, replica_groups=mesh['tiles'=32,'sub'=16] {'sub'}, use_global_device_ids=true, to_apply=%region_22.23 | all-reduce | flops 4374 | bytes 34992 | tf_op jit(solution)/shard_map/psum | solution.py:184
  427.7 117.2 %all-reduce = (f32[64,64]{1,0:T(8,128)}, f32[64,3]{0,1:T(4,128)}) all-reduce(f32[64,64]{1,0:T(8,128)S(1)} %fusion.220, f32[64,3]{0,1:T(4,128)S(1)} %fusion.218), channel_id=1, replica_groups=mesh['tiles'=32,'sub'=16] {'tiles'}, use_global_device_ids=true, to_apply=%region_25.26 | all-reduce | flops 4288 | bytes 34304 | tf_op jit(solution)/shard_map/psum | solution.py:205
  (244 shorter events, 178.6 us)
Async XLA Ops:
  26.8 33.3 %all-to-all-start = ((f32[16,1,32768]{2,1,0:T(1,128)}), f32[16,1,32768]{2,1,0:T(1,128)S(1)}, u32[]{:S(2)}, u32[]{:S(2)}) async-start(f32[16,1,32768]{2,1,0:T(1,128)} %reshape.300), calls=%async_computation | async-start | bytes 4194304 | tf_op jit(solution)/shard_map/while/body/eval_jaxpr/all_to_all | solution.py:55
  60.1 1.4 copy-start
  99.2 6.8 %copy-start.1 = (f32[2,4,2,16,32,128]{5,4,3,2,1,0:T(8,128)S(1)}, f32[2,4,2,16,32,128]{5,4,3,2,1,0:T(8,128)}, u32[]{:S(2)}) copy-start(f32[2,4,2,16,32,128]{5,4,3,2,1,0:T(8,128)} %get-tuple-element.613) | copy-start | bytes 12582916 | tf_op jit(solution)/shard_map/while
  106.2 2.0 copy-start.2
  134.5 35.0 %all-to-all-start = ((f32[16,1,32768]{2,1,0:T(1,128)}), f32[16,1,32768]{2,1,0:T(1,128)S(1)}, u32[]{:S(2)}, u32[]{:S(2)}) async-start(f32[16,1,32768]{2,1,0:T(1,128)} %reshape.300), calls=%async_computation | async-start | bytes 4194304 | tf_op jit(solution)/shard_map/while/body/eval_jaxpr/all_to_all | solution.py:55
  169.5 1.4 copy-start
  208.8 6.8 %copy-start.1 = (f32[2,4,2,16,32,128]{5,4,3,2,1,0:T(8,128)S(1)}, f32[2,4,2,16,32,128]{5,4,3,2,1,0:T(8,128)}, u32[]{:S(2)}) copy-start(f32[2,4,2,16,32,128]{5,4,3,2,1,0:T(8,128)} %get-tuple-element.613) | copy-start | bytes 12582916 | tf_op jit(solution)/shard_map/while
  215.8 2.0 copy-start.2
  224.8 16.3 %copy-start.4 = (s32[108,2]{0,1:T(2,128)S(1)}, s32[108,2]{0,1:T(2,128)}, u32[]{:S(2)}) copy-start(s32[108,2]{0,1:T(2,128)} %param.19) | copy-start | bytes 2596
  224.8 16.3 %copy-start.6 = (s32[108]{0:T(128)S(1)}, s32[108]{0:T(128)}, u32[]{:S(2)}) copy-start(s32[108]{0:T(128)} %param.20) | copy-start | bytes 1300
  224.8 16.7 %copy-start.5 = (s32[108,3]{0,1:T(4,128)S(1)}, s32[108,3]{0,1:T(4,128)}, u32[]{:S(2)}) copy-start(s32[108,3]{0,1:T(4,128)} %param.21) | copy-start | bytes 3892
  224.8 18.1 %collective-permute-start = (bf16[1,2,16,32,128]{4,3,2,1,0:T(8,128)(2,1)S(1)}, bf16[1,2,16,32,128]{4,3,2,1,0:T(8,128)(2,1)S(1)}, u32[]{:S(2)}, u32[]{:S(2)}) collective-permute-start(bf16[1,2,16,32,128]{4,3,2,1,0:T(8,128)(2,1)S(1)} %fusion.208), channel_id=1, source_target_pairs={{0,16},{16,0},{32,48},{48,32},{64,80},{80,64},{96,112},{112,96},{1... | collective-permute-start | bytes 786440 | tf_op jit(solution)/shard_map/ppermute | solution.py:22
  233.9 17.2 %collective-permute-start.1 = (bf16[2,2,16,32,128]{4,3,2,1,0:T(8,128)(2,1)S(1)}, bf16[2,2,16,32,128]{4,3,2,1,0:T(8,128)(2,1)S(1)}, u32[]{:S(2)}, u32[]{:S(2)}) collective-permute-start(bf16[2,2,16,32,128]{4,3,2,1,0:T(8,128)(2,1)S(1)} %get-tuple-element.487), channel_id=1, source_target_pairs={{0,32},{16,48},{32,64},{48,80},{64,96},{80,112},{96,128},{112,144}... | collective-permute-start | bytes 1572872 | tf_op jit(solution)/shard_map/ppermute | solution.py:28
  239.8 15.4 %collective-permute-start.2 = (bf16[2,2,16,32,128]{4,3,2,1,0:T(8,128)(2,1)S(1)}, bf16[2,2,16,32,128]{4,3,2,1,0:T(8,128)(2,1)S(1)}, u32[]{:S(2)}, u32[]{:S(2)}) collective-permute-start(bf16[2,2,16,32,128]{4,3,2,1,0:T(8,128)(2,1)S(1)} %get-tuple-element.486), channel_id=1, source_target_pairs={{32,0},{48,16},{64,32},{80,48},{96,64},{112,80},{128,96},{144,112}... | collective-permute-start | bytes 1572872 | tf_op jit(solution)/shard_map/ppermute | solution.py:28
  427.0 117.9 %copy-start.3 = (f32[6,729]{1,0:T(8,128)}, f32[6,729]{1,0:T(8,128)S(1)}, u32[]{:S(2)}) copy-start(f32[6,729]{1,0:T(8,128)S(1)} %get-tuple-element.476) | copy-start | bytes 52492
where the time goes:
time: 548 us; the launch traced here: 545 us
  blocking collectives  173 us (32%)
  matrix products  128 us (23%)
  local copies, waits for them, and re-layouts  87.2 us (16%)
  waiting for transfers between devices  64.7 us (12%)
  other arithmetic  34.6 us (6%)
  starting transfers between devices  29.1 us (5%)
  loops' own time  27.6 us (5%)
    psum x1, blocking collectives, local(): normal_matrix, normal_rhs = lax.psum((matrix_part, load_part), 'tiles')  117 us
    psum x1, blocking collectives, local(): windows = lax.psum(partials, 'sub') * filled[:, None]  55.9 us
    all_to_all x2, waiting for transfers between devices, spectrum(): lax.all_to_all(jnp.stack([real_two, imag_two], axis=1), 'sub', split_axis...  52.6 us
    while x16, local copies, waits for them, and re-layouts  33.6 us
    all_to_all x2, starting transfers between devices, spectrum(): lax.all_to_all(jnp.stack([real_two, imag_two], axis=1), 'sub', split_axis...  15.7 us
    dynamic_slice x30, local copies, waits for them, and re-layouts, local(): ignored, partials = lax.scan(per_slot, 0, slot_data)  15.5 us
    another operation x2, local copies, waits for them, and re-layouts, spectrum(): jnp.stack([real_two, imag_two], axis=1)  15 us
    all_to_all x2, other arithmetic, spectrum(): lax.all_to_all(jnp.stack([real_two, imag_two], axis=1), 'sub', split_axis...  14.6 us
  transfers between devices with their start and end apart: 5, of which 4 were waited for; matrix products, arithmetic and copies ran while one was open for 1% of the time, Pallas kernels for 0%

commit v1 on v0

v1 whole, which is shorter than its diff:
```python
import jax
import jax.numpy as jnp
import ml_dtypes
import numpy as np
from jax import lax
from jax.experimental import pallas as pl
from jax.experimental.pallas import tpu as pltpu
from jax.sharding import Mesh, PartitionSpec as P

REACH = 4
WIN = 9
EPSILON = 1e-06
FLOOR_SHARE = 0.05
ROW = 4
PLANES = 16
SUBS = 16
DEPTH, ACROSS, ALONG = 128, 32, 256
LOCAL = DEPTH // SUBS
HALF = ALONG // 2
VOXELS = DEPTH * ACROSS * ALONG
MAX_OFF = 5
OFFS = 2 * MAX_OFF + 1
SLOTS = 7
BF = jnp.bfloat16
F32 = jnp.float32


def split_np(table):
    high = table.astype(ml_dtypes.bfloat16)
    low = (table - high.astype(np.float64)).astype(ml_dtypes.bfloat16)
    return high, low


def angles(rows, cols, length):
    return (np.outer(rows, cols) % length) * (2.0 * np.pi / length)


def across_freq(half, sub):
    if half == 0:
        return sub
    return ACROSS // 2 if sub == 0 else ACROSS - sub


def across_table():
    table = np.zeros((2, 2, SUBS, LOCAL, LOCAL, ACROSS))
    for half in range(2):
        for sub in range(SUBS):
            theta = angles([across_freq(half, sub)], np.arange(ACROSS), ACROSS)[0]
            for plane in range(LOCAL):
                table[half, 0, sub, plane, plane] = np.cos(theta)
                table[half, 1, sub, plane, plane] = -np.sin(theta)
    return table.reshape(2, 2 * SUBS * LOCAL, LOCAL * ACROSS)


def along_table():
    table = np.zeros((2, 2, ALONG, 2, HALF))
    for half in range(2):
        theta = angles(np.arange(ALONG), np.arange(HALF) + half, ALONG)
        table[half, 0, :, 0] = np.cos(theta)
        table[half, 0, :, 1] = -np.sin(theta)
        table[half, 1, :, 0] = np.sin(theta)
        table[half, 1, :, 1] = np.cos(theta)
    return table.reshape(2, 2 * ALONG, 2 * HALF)


def extra_table():
    table = np.zeros((2, ALONG, HALF))
    table[0, :, 0] = np.where(np.arange(ALONG) % 2 == 0, 1.0, -1.0)
    table[1, :, HALF - 1] = 1.0
    return table


def depth_table():
    theta = angles(np.arange(DEPTH), np.arange(DEPTH), DEPTH).reshape(DEPTH, SUBS, LOCAL)
    table = np.zeros((2, 2, DEPTH, SUBS, 2, LOCAL))
    for half in range(2):
        table[0, half, :, :, half, :] = np.cos(theta)
        table[1, half, :, :, half, :] = np.sin(theta)
    return table.reshape(4 * DEPTH, 2 * DEPTH)


def window_table():
    freq = np.arange(DEPTH)
    table = np.zeros((OFFS, 6, 16, DEPTH))
    low, high = (freq >= 1) & (freq < 64), freq > 64
    for index in range(OFFS):
        steps = np.arange(WIN) - REACH + index - MAX_OFF
        theta = angles(steps, freq, DEPTH)
        cos, sin = np.cos(theta), np.sin(theta)
        edge = 0.5 * cos * ((freq == 0) | (freq == 64))
        table[index, 0, :WIN] = cos
        table[index, 1, :WIN] = sin
        table[index, 2, :WIN] = cos * low + edge
        table[index, 3, :WIN] = sin * low
        table[index, 4, :WIN] = cos * high
        table[index, 5, :WIN] = edge - sin * high
    return table.reshape(OFFS, 96, DEPTH)


def plane_table():
    table = np.zeros((SUBS, 2, 2, HALF, 128))
    step = np.arange(WIN) - REACH
    ones = np.ones(WIN)
    for sub in range(SUBS):
        for half in range(2):
            freq = np.arange(HALF) + half
            theta_x = angles(freq, step, ALONG)
            theta_y = angles([across_freq(half, sub)], step, ACROSS)[0]
            theta = theta_y[None, :, None] + theta_x[:, None, :]
            table[sub, half, 0, :, : WIN * WIN] = np.cos(theta).reshape(HALF, -1)
            table[sub, half, 1, :, : WIN * WIN] = -np.sin(theta).reshape(HALF, -1)
    sign = np.where(step % 2 == 0, 1.0, -1.0)
    table[0, 0, 1, 0, : WIN * WIN] = np.outer(ones, sign).reshape(-1)
    table[0, 1, 1, HALF - 1, : WIN * WIN] = np.outer(sign, ones).reshape(-1)
    return table.reshape(SUBS, 4 * HALF, 128) * (2.0 / VOXELS)


def shift_table():
    table = np.zeros((2, 2, 16, HALF))
    for half in range(2):
        theta = angles(np.arange(OFFS) - MAX_OFF, np.arange(HALF) + half, ALONG)
        table[half, 0, :OFFS] = np.cos(theta)
        table[half, 1, :OFFS] = np.sin(theta)
    return table.reshape(4, 16, HALF).astype(np.float32)


def circle_table():
    theta = np.arange(ACROSS) * (2.0 * np.pi / ACROSS)
    return np.stack([np.cos(theta), np.sin(theta)]).astype(np.float32)


def graph_table():
    table = np.zeros((PLANES, 8, ROW * PLANES), np.float32)
    for plane in range(PLANES):
        base = ROW * plane
        pairs = [(base, base + 1), (base + 2, base + 3), (base + 1, base + 2)]
        pairs += [(base - ROW + col, base + col) for col in range(ROW)]
        for slot, (first, second) in enumerate(pairs):
            if first >= 0:
                table[plane, slot, first] = 1.0
                table[plane, slot, second] = -1.0
    return table.reshape(PLANES * 8, ROW * PLANES)


def dot(left, right):
    return jnp.dot(left, right, preferred_element_type=F32)


def split(value):
    high = value.astype(BF)
    return high, (value - high.astype(F32)).astype(BF)


def across_dft(strip, half, across_hi, across_lo):
    both = dot(across_hi[half], strip) + dot(across_lo[half], strip)
    rows = SUBS * LOCAL
    return jnp.concatenate([both[:rows], both[rows:]], axis=1)


def along_dft(value, half, along_hi, along_lo, extra, count):
    high, low = split(value)
    out = dot(high, along_hi[half]) + dot(low, along_hi[half]) + dot(high, along_lo[half])
    rows = SUBS * LOCAL
    edge_hi = jnp.concatenate([high[rows * k : rows * k + 16, :ALONG] for k in range(count)], axis=0)
    edge_lo = jnp.concatenate([low[rows * k : rows * k + 16, :ALONG] for k in range(count)], axis=0)
    more = dot(edge_hi, extra[half]) + dot(edge_lo, extra[half])
    pieces = []
    for k in range(count):
        block = out[rows * k : rows * (k + 1)]
        head = block[:LOCAL]
        head = jnp.concatenate(
            [head[:, :HALF], head[:, HALF:] + more[16 * k : 16 * k + LOCAL]], axis=1
        )
        pieces.append(jnp.concatenate([head, block[LOCAL:]], axis=0).reshape(SUBS, LOCAL, 2 * HALF))
    return pieces


def local_kernel(strips, ahi, alo, bhi, blo, extra, out):
    chosen = (1, 4, 2, 6)
    parts = []
    for half in range(2):
        stack = [across_dft(strips[k], half, ahi, alo) for k in chosen]
        parts.append(along_dft(jnp.concatenate(stack, axis=0), half, bhi, blo, extra, 4))
    for k in range(4):
        out[:, 16 * k : 16 * k + 16, :] = jnp.concatenate(
            [parts[0][k], parts[1][k]], axis=1
        ).astype(BF)


def remote_kernel(core, below, own, other, ahi, alo, bhi, blo, extra, ignored, out):
    del ignored
    parts = []
    for half in range(2):
        stack = [across_dft(below[k], half, ahi, alo) for k in range(2)]
        parts.append(along_dft(jnp.concatenate(stack, axis=0), half, bhi, blo, extra, 2))
    for k in range(2):
        out[:, 16 * k : 16 * k + 16, :] = jnp.concatenate(
            [parts[0][k], parts[1][k]], axis=1
        ).astype(BF)
    me = core[0]
    is_left = me == 0
    mine, theirs = own[...], other[...]
    first = jnp.where(is_left, mine, theirs)
    second = jnp.where(is_left, theirs, mine)
    stack = [across_dft(strip, me, ahi, alo) for strip in (first, second)]
    seam = along_dft(jnp.concatenate(stack, axis=0), me, bhi, blo, extra, 2)
    out[:, 32:48, :] = jnp.concatenate(seam, axis=1).astype(BF)


def spectrum_of(block, lanes, mhi, mlo):
    both = dot(mhi, block) + dot(mlo, block)
    cos, sin = both[: 2 * DEPTH], both[2 * DEPTH :]
    cos_re, cos_im = cos[:, :HALF], cos[:, HALF:]
    sin_re, sin_im = sin[:, :HALF], sin[:, HALF:]
    low, high = lanes
    real = jnp.where(low, cos_re, jnp.where(high, cos_im, cos_re + sin_im))
    imag = jnp.where(low, -sin_re, jnp.where(high, -sin_im, cos_im - sin_re))
    return real, imag


def phase_of(first, second, edge):
    floor = (FLOOR_SHARE * VOXELS) ** 2
    first_re, first_im = first
    second_re, second_im = second
    straight, crossed = first_re * second_re, first_im * second_im
    real = straight + jnp.where(edge, 0.0, crossed)
    imag = jnp.where(edge, crossed, first_im * second_re - first_re * second_im)
    real_sq, imag_sq = real * real, imag * imag
    norm = lax.rsqrt(real_sq + jnp.where(edge, 0.0, imag_sq) + floor)
    norm_im = jnp.where(edge, lax.rsqrt(imag_sq + floor), norm)
    return real * norm, imag * norm_im


def window_kernel(meta, circle, sub, core, got, mhi, mlo, vhi, vlo, ehi, elo, shift, out):
    d, c = sub[0], core[0]
    row = lax.broadcasted_iota(jnp.int32, (2 * DEPTH, HALF), 0)
    lane = lax.broadcasted_iota(jnp.int32, (2 * DEPTH, HALF), 1)
    freq = lax.rem(row, DEPTH)
    nowhere = jnp.where(d == 0, 0, 2 * HALF)

    def special(half_of_row):
        held = lane == half_of_row * (HALF - 1) + nowhere
        low = held & (freq > 0) & (freq < 64)
        high = held & (freq > 64)
        edge = held & ((freq == 0) | (freq == 64))
        return (low, high), edge

    lanes, edge = special(row // DEPTH)
    mh, ml = mhi[...], mlo[...]

    def spectrum(slot, masks):
        block = got[:, 16 * slot : 16 * slot + 16, :].reshape(2 * DEPTH, 2 * HALF)
        return spectrum_of(block, masks, mh, ml)

    small_lane = lax.broadcasted_iota(jnp.int32, (16, HALF), 1)

    def window_rows(phase, half, slot):
        off_z, off_y, off_x = meta[slot, 0], meta[slot, 1], meta[slot, 2]
        both = jnp.concatenate(phase, axis=1)
        high, low = split(both)
        table_hi, table_lo = vhi[off_z + MAX_OFF], vlo[off_z + MAX_OFF]
        rows = dot(table_hi, high) + dot(table_lo, high) + dot(table_hi, low)
        part = [(rows[16 * k : 16 * k + 16, :HALF], rows[16 * k : 16 * k + 16, HALF:]) for k in range(6)]
        real = part[0][0] - part[1][1]
        imag = part[1][0] + part[0][1]
        held = small_lane == half * (HALF - 1) + nowhere
        sign = jnp.where(lax.rem(off_x + 6, 2) == 0, 1.0, -1.0).astype(F32)
        real = jnp.where(held, part[2][0] - part[3][1], real)
        imag = jnp.where(held, (part[4][0] + part[5][1]) * sign, imag)
        freq_y = jnp.where(half == 0, d, jnp.where(d == 0, ACROSS // 2, ACROSS - d))
        turn = lax.rem(freq_y * (off_y + ACROSS), ACROSS)
        cos_y, sin_y = circle[0, turn], circle[1, turn]
        cos_x = shift[2 * half, pl.ds(off_x + MAX_OFF, 1), :]
        sin_x = shift[2 * half + 1, pl.ds(off_x + MAX_OFF, 1), :]
        cos = cos_x * cos_y - sin_x * sin_y
        sin = sin_x * cos_y + cos_x * sin_y
        return jnp.concatenate([real * cos - imag * sin, real * sin + imag * cos], axis=1)

    pieces = []
    for first, second, slot in ((0, 1, c), (4, 2, 3 + 2 * c), (5, 3, 4 + 2 * c)):
        real, imag = phase_of(spectrum(first, lanes), spectrum(second, lanes), edge)
        halves = [
            window_rows((real[DEPTH * h : DEPTH * (h + 1)], imag[DEPTH * h : DEPTH * (h + 1)]), h, slot)
            for h in range(2)
        ]
        pieces.append(jnp.concatenate(halves, axis=1))
    seam_lanes, seam_edge = special(c)
    real, imag = spectrum(6, seam_lanes)
    phase = phase_of(
        (real[:DEPTH], imag[:DEPTH]), (real[DEPTH:], imag[DEPTH:]), seam_edge[:DEPTH]
    )
    seam = window_rows(phase, c, 2)
    empty = jnp.zeros_like(seam)
    pieces.append(
        jnp.concatenate([jnp.where(c == 0, seam, empty), jnp.where(c == 0, empty, seam)], axis=1)
    )
    terms = jnp.concatenate(pieces, axis=0)
    high, low = split(terms)
    table_hi, table_lo = ehi[0], elo[0]
    sums = dot(high, table_hi) + dot(low, table_hi) + dot(high, table_lo)
    packed = jnp.concatenate(
        [sums[16 * k : 16 * k + WIN] for k in range(4)] + [jnp.zeros((4, 128), F32)], axis=0
    )
    out[...] = jnp.broadcast_to(packed[None], out.shape)


def energy_kernel(core, got, offsets, windows, terms):
    left = got[0]
    right = got[SUBS]
    for k in range(1, SUBS):
        left = left + got[k]
        right = right + got[SUBS + k]
    blocks = [left[:WIN], right[:WIN], left[27:36] + right[27:36]]
    blocks += [left[9:18], left[18:27], right[9:18], right[18:27]]
    step_z = (lax.broadcasted_iota(jnp.int32, (WIN, 128), 0) - REACH).astype(F32)
    sums, sums_z = [], []
    for block in blocks:
        square = block * block
        sums.append(jnp.sum(square, axis=0, keepdims=True))
        sums_z.append(jnp.sum(square * step_z, axis=0, keepdims=True))
    zero = jnp.zeros((1, 128), F32)
    sums = jnp.concatenate(sums + [zero], axis=0)
    sums_z = jnp.concatenate(sums_z + [zero], axis=0)
    lane = lax.broadcasted_iota(jnp.int32, (8, 128), 1)
    step_y = (lane // WIN - REACH).astype(F32)
    step_x = (lane % WIN - REACH).astype(F32)
    energy = jnp.sum(sums, axis=1, keepdims=True)
    moments = [sums_z, sums * step_y, sums * step_x]
    moments = [jnp.sum(m, axis=1, keepdims=True) for m in moments]
    mixed = jnp.where(lane == 1, moments[0], jnp.where(lane == 2, moments[1], moments[2]))
    place = offsets[...] + mixed / (energy + EPSILON)
    value = jnp.where(lane == 0, energy, energy * place)
    value = jnp.where(lane < 4, value, 0.0)
    terms[...] = jnp.broadcast_to(value[None], terms.shape)
    is_left = core[0] == 0
    mine = [
        jnp.where(is_left, blocks[0], blocks[1]),
        blocks[2],
        jnp.where(is_left, blocks[3], blocks[5]),
        jnp.where(is_left, blocks[4], blocks[6]),
    ]
    for k in range(4):
        windows[k, :WIN, :] = mine[k]
        windows[k, WIN:, :] = jnp.zeros((16 - WIN, 128), F32)


def final_kernel(meta, mine, below, terms, graph, windows, matrix, rhs):
    slot = lax.broadcasted_iota(jnp.int32, (6, 128), 0)
    blocks = [mine[k] for k in range(4)] + [below[k] for k in range(2)]
    places = [slot == meta[9 + k, 0] for k in range(6)]
    for step in range(WIN):
        rows = jnp.zeros((6, 128), F32)
        for block, place in zip(blocks, places):
            rows = jnp.where(place, block[step : step + 1], rows)
        windows[:, WIN * WIN * step : WIN * WIN * (step + 1)] = rows[:, : WIN * WIN]
    table = graph[...]
    value = terms[...].reshape(PLANES * 8, 128)
    weighted = table * value[:, :1]
    over = (((0,), (0,)), ((), ()))
    matrix[...] = lax.dot_general(
        table, weighted, over, precision=lax.Precision.HIGHEST, preferred_element_type=F32
    )
    load = lax.dot_general(
        table, value, over, precision=lax.Precision.HIGHEST, preferred_element_type=F32
    )
    rhs[...] = load[:, 1:4]


def pair_facts(pair_tiles, pair_owner, pair_offset, plane, core):
    count = pair_owner.shape[0]
    key = pair_tiles[:, 0] * 2 + (pair_tiles[:, 1] - pair_tiles[:, 0] != 1)
    base = ROW * plane
    here = [base, base + 2, base + 1]
    up = [base - ROW + col for col in range(ROW)]
    down = [base + 2 * core, base + 2 * core + 1]
    wanted = jnp.stack([2 * t for t in here] + [2 * t + 1 for t in up + down])
    match = (wanted[:, None] == key[None, :]).astype(jnp.int32)
    owned = (pair_owner == 2 * plane + core).astype(jnp.int32)
    place = jnp.arange(count, dtype=jnp.int32)
    offset = jnp.sum(match[:, :, None] * pair_offset[None], axis=1)
    at = jnp.sum(match * place[None], axis=1)
    held = jnp.sum(match * owned[None], axis=1)
    ordinal = jnp.sum((place[None] < at[:, None]).astype(jnp.int32) * owned[None], axis=1)
    row = jnp.where(held > 0, ordinal, -1)
    mine = jnp.stack(
        [
            jnp.where(core == 0, row[0], row[1]),
            row[2],
            jnp.where(core == 0, row[3], row[5]),
            jnp.where(core == 0, row[4], row[6]),
            row[7],
            row[8],
        ]
    )
    facts = jnp.concatenate([offset, jnp.broadcast_to(mine[:, None], (6, 3))], axis=0)
    lanes = jnp.zeros((8, 128), F32).at[:7, 1:4].set(offset[:7].astype(F32))
    return facts, lanes


def call(kernel, shapes, operands, spaces, aliases=None, **params):
    specs = [pl.BlockSpec(memory_space=space) for space in spaces]
    outs = jax.tree.map(lambda _: pl.BlockSpec(memory_space=pltpu.VMEM), shapes)
    return pl.pallas_call(
        kernel,
        out_shape=shapes,
        in_specs=specs,
        out_specs=outs,
        compiler_params=pltpu.CompilerParams(vmem_limit_bytes=40 * 1024 * 1024),
        **params,
    )(*operands)


def local(strips, pair_tiles, pair_owner, pair_offset):
    plane, core, sub = (lax.axis_index(name) for name in ("z", "core", "sub"))
    ahi, alo = split_np(across_table())
    bhi, blo = split_np(along_table())
    extra = extra_table().astype(ml_dtypes.bfloat16)
    mhi, mlo = split_np(depth_table())
    vhi, vlo = split_np(window_table())
    ehi, elo = split_np(plane_table())
    vmem, smem = pltpu.VMEM, pltpu.SMEM
    core_arr = core.reshape(1).astype(jnp.int32)
    sub_arr = sub.reshape(1).astype(jnp.int32)

    tiles = strips.reshape(8, LOCAL * ACROSS, ALONG)
    from_above = lax.ppermute(
        jnp.stack([tiles[3], tiles[7]]), "z", [(k, k + 1) for k in range(PLANES - 1)]
    )
    own = jnp.where(core == 0, tiles[5], tiles[0])
    other = lax.ppermute(own, "core", [(0, 1), (1, 0)])
    facts, lanes = pair_facts(pair_tiles, pair_owner, pair_offset, plane, core)

    tables = (ahi, alo, bhi, blo, extra)
    here = call(
        local_kernel,
        jax.ShapeDtypeStruct((SUBS, 64, 2 * HALF), BF),
        (tiles,) + tables,
        (vmem,) * 6,
    )
    there = call(
        remote_kernel,
        jax.ShapeDtypeStruct((SUBS, 48, 2 * HALF), BF),
        (core_arr, from_above, own, other) + tables + (core_arr,),
        (smem,) + (vmem,) * 8 + (smem,),
    )
    sent = jnp.concatenate([here, there], axis=1)
    got = lax.all_to_all(sent, "sub", split_axis=0, concat_axis=0, tiled=True)

    ehi_here = lax.dynamic_slice_in_dim(jnp.asarray(ehi), sub, 1, 0)
    elo_here = lax.dynamic_slice_in_dim(jnp.asarray(elo), sub, 1, 0)
    partial = call(
        window_kernel,
        jax.ShapeDtypeStruct((2 * SUBS, 40, 128), F32),
        (facts, circle_table(), sub_arr, core_arr, got, mhi, mlo, vhi, vlo, ehi_here, elo_here, shift_table()),
        (smem,) * 4 + (vmem,) * 8,
    )
    shares = lax.all_to_all(partial, ("core", "sub"), split_axis=0, concat_axis=0, tiled=True)
    mine, terms = call(
        energy_kernel,
        (jax.ShapeDtypeStruct((4, 16, 128), F32), jax.ShapeDtypeStruct((PLANES, 8, 128), F32)),
        (core_arr, shares, lanes),
        (smem, vmem, vmem),
    )
    below = lax.ppermute(mine[2:], "z", [(k + 1, k) for k in range(PLANES - 1)])
    all_terms = lax.all_to_all(terms, "z", split_axis=0, concat_axis=0, tiled=True)
    return call(
        final_kernel,
        (
            jax.ShapeDtypeStruct((6, WIN * WIN * WIN), F32),
            jax.ShapeDtypeStruct((64, 64), F32),
            jax.ShapeDtypeStruct((64, 3), F32),
        ),
        (facts, mine, below, all_terms, graph_table()),
        (smem,) + (vmem,) * 4,
    )


def solution(mesh):
    grid = Mesh(mesh.devices.reshape(PLANES, 2, SUBS), ("z", "core", "sub"))
    tiles = ("z", "core")
    in_specs = (P(tiles, None, "sub", None, None), P(), P(), P())
    out_specs = (P(tiles, None), P(), P())
    return jax.shard_map(local, mesh=grid, in_specs=in_specs, out_specs=out_specs, check_vma=False)
```

time: 548 us -> 94.5 us (0.17)
  blocking collectives: 173 us -> 0 us
  matrix products: 128 us -> 0 us
  local copies, waits for them, and re-layouts: 87.2 us -> 10.6 us
  waiting for transfers between devices: 64.7 us -> 29.1 us
  other arithmetic: 34.6 us -> 4.44 us
  loops' own time: 27.6 us -> 0 us
  Pallas kernels: 0 us -> 9.64 us
  starting transfers between devices: 29.1 us -> 34.6 us
    psum x2 -> x0, blocking collectives: 173 us -> none  [the longest x1 117 us: local(): normal_matrix, normal_rhs = lax.psum((matrix_part, load_part), 'tiles')]
    dot_general x83 -> x0, matrix products: 128 us -> none  [the longest x2 14.1 us: spectrum(): jnp.einsum('nkaz,zw->nkaw', gathered[:, 1], sin_depth, precision=HIGHEST_...]
    while x16 -> x0, local copies, waits for them, and re-layouts: 33.6 us -> none
    another operation x14 -> x0, loops' own time: 27.6 us -> none  [the longest x12 12.5 us: fetch(): lax.switch(source_kind, [take_from(source_table) for source_table in tabl...]
    all_to_all x2 -> x3, waiting for transfers between devices: 52.6 us -> 25.5 us  [the longest x1 9.96 us: local(): lax.all_to_all(partial, ('core', 'sub'), split_axis=0, concat_axis=0, til...]
    dynamic_slice x36 -> x1, local copies, waits for them, and re-layouts: 22 us -> 0.99 us  [local(): elo_here = lax.dynamic_slice_in_dim(jnp.asarray(elo), sub, 1, 0)]
    all_to_all x2 -> x0, other arithmetic: 14.6 us -> none  [spectrum(): lax.all_to_all(jnp.stack([real_two, imag_two], axis=1), 'sub', split_axis...]
    another operation x3 -> x4, local copies, waits for them, and re-layouts: 15.1 us -> 1.38 us  [the longest x1 0.71 us: pair_facts(): jnp.stack([jnp.where(core == 0, row[0], row[1]), row[2], jnp.where(core =...]
  transfers between devices with their start and end apart: 5 -> 6, of which waited for: 4 -> 4; matrix products, arithmetic and copies ran while one was open for 1% -> 8% of each run, Pallas kernels for 0% -> 2%
where the time goes in v1:
time: 94.5 us; the launch traced here: 93.1 us
  starting transfers between devices  34.6 us (37%)
  waiting for transfers between devices  29.1 us (31%)
  local copies, waits for them, and re-layouts  10.6 us (11%)
  Pallas kernels  9.64 us (10%)
  between operations  4.75 us (5%)
  other arithmetic  4.44 us (5%)
    all_to_all x1, starting transfers between devices, local(): lax.all_to_all(terms, 'z', split_axis=0, concat_axis=0, tiled=True)  14 us
    all_to_all x1, waiting for transfers between devices, local(): lax.all_to_all(partial, ('core', 'sub'), split_axis=0, concat_axis=0, til...  9.96 us
    pallas_call x5, Pallas kernels, call(): pl.pallas_call(kernel, out_shape=shapes, in_specs=specs, out_specs=outs,...  9.64 us
    all_to_all x1, waiting for transfers between devices, local(): got = lax.all_to_all(sent, 'sub', split_axis=0, concat_axis=0, tiled=True)  8.76 us
    all_to_all x1, waiting for transfers between devices, local(): lax.all_to_all(terms, 'z', split_axis=0, concat_axis=0, tiled=True)  6.76 us
    ppermute x1, starting transfers between devices, local(): other = lax.ppermute(own, 'core', [(0, 1), (1, 0)])  5.71 us
    all_to_all x1, starting transfers between devices, local(): lax.all_to_all(partial, ('core', 'sub'), split_axis=0, concat_axis=0, til...  5.15 us
    unnamed x36, local copies, waits for them, and re-layouts  4.96 us
  transfers between devices with their start and end apart: 6, of which 4 were waited for; matrix products, arithmetic and copies ran while one was open for 8% of the time, Pallas kernels for 2%

profile of v1, /device:TPU:1, one launch (start us, length us, event | category | flops | bytes accessed | tf_op | source)
XLA Modules:
  0.0 93.1 jit_solution(11141734925839306558)
XLA Ops:
  0.7 1.2 %fusion = (bf16[256,256]{1,0:T(8,128)(2,1)S(1)}, bf16[1,256,256]{2,1,0:T(8,128)(2,1)S(1)}, bf16[1,256,256]{2,1,0:T(8,128)(2,1)S(1)}) fusion(bf16[8,256,256]{2,1,0:T(8,128)(2,1)} %bitcast.27, pred[]{:T(512)S(6)} %eq.32), kind=kLoop, calls=%fused_computation.3 | loop fusion | flops 65536 | bytes 917505 | tf_op jit(solution)/shard_map/jit(_where)/select_n | solution.py:429
  1.9 4.5 %collective-permute-start = (bf16[2,256,256]{2,1,0:T(8,128)(2,1)S(1)}, bf16[2,256,256]{2,1,0:T(8,128)(2,1)S(1)}, u32[]{:S(2)}, u32[]{:S(2)}) collective-permute-start(bf16[2,256,256]{2,1,0:T(8,128)(2,1)S(1)} %pad_maximum_fusion.1), channel_id=1, source_target_pairs={{0,32},{32,64},{64,96},{96,128},{128,160},{160,192},{192,224},{224... | collective-permute-start | bytes 786440 | tf_op jit(solution)/shard_map/ppermute | solution.py:426
  6.5 5.7 %collective-permute-start.1 = (bf16[256,256]{1,0:T(8,128)(2,1)S(1)}, bf16[256,256]{1,0:T(8,128)(2,1)S(1)}, u32[]{:S(2)}, u32[]{:S(2)}) collective-permute-start(bf16[256,256]{1,0:T(8,128)(2,1)S(1)} %get-tuple-element.30.own), channel_id=1, source_target_pairs={{0,16},{16,0},{1,17},{17,1},{2,18},{18,2},{3,19},{19,3},{4,20},{20... | collective-permute-start | bytes 393224 | tf_op jit(solution)/shard_map/ppermute | solution.py:430
  13.9 1.0 %copy-done.1 = bf16[2,512,256]{2,1,0:T(8,128)(2,1)S(1)} copy-done((bf16[2,512,256]{2,1,0:T(8,128)(2,1)S(1)}, bf16[2,512,256]{2,1,0:T(8,128)(2,1)}, u32[]{:S(2)}) %copy-start.1) | copy-done | bytes 524312
  14.9 1.0 %copy-done.3 = bf16[2,512,256]{2,1,0:T(8,128)(2,1)S(1)} copy-done((bf16[2,512,256]{2,1,0:T(8,128)(2,1)S(1)}, bf16[2,512,256]{2,1,0:T(8,128)(2,1)}, u32[]{:S(2)}) %copy-start.3) | copy-done | bytes 524312
  16.0 0.9 %copy-done.5 = bf16[2,256,256]{2,1,0:T(8,128)(2,1)S(1)} copy-done((bf16[2,256,256]{2,1,0:T(8,128)(2,1)S(1)}, bf16[2,256,256]{2,1,0:T(8,128)(2,1)}, u32[]{:S(2)}) %copy-start.5) | copy-done | bytes 262168
  16.9 0.9 %copy-done.7 = bf16[2,256,256]{2,1,0:T(8,128)(2,1)S(1)} copy-done((bf16[2,256,256]{2,1,0:T(8,128)(2,1)S(1)}, bf16[2,256,256]{2,1,0:T(8,128)(2,1)}, u32[]{:S(2)}) %copy-start.7) | copy-done | bytes 262168
  17.9 0.9 copy-done.9
  18.8 1.6 %shard_map.193 = bf16[16,64,256]{2,1,0:T(8,128)(2,1)S(1)} custom-call(bf16[8,256,256]{2,1,0:T(8,128)(2,1)S(1)} %bitcast.28, bf16[2,256,256]{2,1,0:T(8,128)(2,1)S(1)} %copy-done.5, bf16[2,256,256]{2,1,0:T(8,128)(2,1)S(1)} %copy-done.7, bf16[2,512,256]{2,1,0:T(8,128)(2,1)S(1)} %copy-done.1, bf16[2,512,256]{2,1,0:T(8,128)(2,1)S(1)} %copy-done.3, ...), custom_call_target="tpu_custom_call" | custom-call | tf_op jit(solution)/shard_map/pallas_call | solution.py:403
  20.7 1.6 %shard_map.194 = bf16[16,48,256]{2,1,0:T(8,128)(2,1)S(1)} custom-call(s32[1]{0:T(128)} %bitcast.19.core.ignored, bf16[2,256,256]{2,1,0:T(8,128)(2,1)S(1)} %collective-permute-done.below, bf16[256,256]{1,0:T(8,128)(2,1)S(1)} %get-tuple-element.30.own, bf16[256,256]{1,0:T(8,128)(2,1)S(1)} %collective-permute-done.1.other, bf16[2,256,256]{2,1,0:T(8,128)(2,1)S(1)} %copy-done.6, ...), custom_call_target="tpu_custom_call" | custom-call | tf_op jit(solution)/shard_map/pallas_call | solution.py:403
  22.3 1.0 %pad_maximum_fusion = bf16[16,112,256]{2,1,0:T(8,128)(2,1)} fusion(bf16[16,48,256]{2,1,0:T(8,128)(2,1)S(1)} %shard_map.194, bf16[16,64,256]{2,1,0:T(8,128)(2,1)S(1)} %shard_map.193), kind=kLoop, calls=%fused_computation | loop fusion | flops 1835008 | bytes 1835008 | tf_op jit(solution)/shard_map/concatenate | solution.py:446
  23.3 3.9 %all-to-all-start = ((bf16[16,112,256]{2,1,0:T(8,128)(2,1)}), bf16[16,112,256]{2,1,0:T(8,128)(2,1)S(1)}, u32[]{:S(2)}, u32[]{:S(2)}) async-start(bf16[16,112,256]{2,1,0:T(8,128)(2,1)} %pad_maximum_fusion), calls=%async_computation | async-start | bytes 1835008 | tf_op jit(solution)/shard_map/all_to_all | solution.py:447
  32.9 1.0 %constant_dynamic-slice_fusion = (bf16[1,512,128]{2,1,0:T(8,128)(2,1)S(1)}, bf16[1,512,128]{2,1,0:T(8,128)(2,1)S(1)}) fusion(bf16[16,512,128]{2,1,0:T(8,128)(2,1)} %constant.99.clone, s32[]{:T(128)S(6)} %select_n.35, bf16[16,512,128]{2,1,0:T(8,128)(2,1)} %constant.98.clone), kind=kLoop, calls=%fused_computation.19 | loop fusion | bytes 524292 | tf_op jit(solution)/shard_map/dynamic_slice | solution.py:450
  34.0 8.8 %all-to-all-done.got = bf16[16,112,256]{2,1,0:T(8,128)(2,1)S(1)} async-done(((bf16[16,112,256]{2,1,0:T(8,128)(2,1)}), bf16[16,112,256]{2,1,0:T(8,128)(2,1)S(1)}, u32[]{:S(2)}, u32[]{:S(2)}) %all-to-all-start) | async-done | bytes 917536 | tf_op jit(solution)/shard_map/all_to_all | solution.py:447
  42.8 4.1 %shard_map.195 = f32[32,40,128]{2,1,0:T(8,128)} custom-call(s32[15,3]{1,0:T(8,128)S(1)} %pad_add_fusion.meta, f32[2,32]{1,0:T(2,128)S(1)} %copy-done.16, s32[1]{0:T(128)} %bitcast.20.sub, s32[1]{0:T(128)} %bitcast.19.core.ignored, bf16[16,112,256]{2,1,0:T(8,128)(2,1)S(1)} %all-to-all-done.got, bf16[512,256]{1,0:T(8,128)(2,1)S(1)} %copy-done.12, ...), custom_call_target="tpu_custom_call" | custom-call | tf_op jit(solution)/shard_map/pallas_call | solution.py:403
  46.9 5.2 %all-to-all-start.1 = ((f32[32,40,128]{2,1,0:T(8,128)}), f32[32,40,128]{2,1,0:T(8,128)S(1)}, u32[]{:S(2)}, u32[]{:S(2)}) async-start(f32[32,40,128]{2,1,0:T(8,128)} %shard_map.195), calls=%async_computation.1 | async-start | bytes 1310720 | tf_op jit(solution)/shard_map/all_to_all | solution.py:457
  52.6 1.8 %scatter.4.offsets = f32[8,128]{1,0:T(8,128)S(1)} dynamic-update-slice(f32[8,128]{1,0:T(8,128)S(1)} %broadcast_in_dim.9, f32[7,3]{1,0:T(8,128)S(1)} %slice_convert_fusion, s32[]{:T(128)} %bitcast.23, s32[]{:T(128)} %bitcast.24) | dynamic-update-slice | bytes 172 | tf_op jit(solution)/shard_map/scatter | solution.py:396
  54.4 10.0 %all-to-all-done.1.got = f32[32,40,128]{2,1,0:T(8,128)S(1)} async-done(((f32[32,40,128]{2,1,0:T(8,128)}), f32[32,40,128]{2,1,0:T(8,128)S(1)}, u32[]{:S(2)}, u32[]{:S(2)}) %all-to-all-start.1) | async-done | bytes 655392 | tf_op jit(solution)/shard_map/all_to_all | solution.py:457
  64.4 0.8 shard_map.196
  65.2 14.0 %all-to-all-start.2 = ((f32[16,8,128]{2,1,0:T(8,128)}), f32[16,8,128]{2,1,0:T(8,128)S(1)}, u32[]{:S(2)}, u32[]{:S(2)}) async-start(f32[16,8,128]{2,1,0:T(8,128)} %get-tuple-element.18), calls=%async_computation.2 | async-start | bytes 131072 | tf_op jit(solution)/shard_map/all_to_all | solution.py:465
  79.2 1.3 %collective-permute-start.2 = (f32[2,16,128]{2,1,0:T(8,128)S(1)}, f32[2,16,128]{2,1,0:T(8,128)S(1)}, u32[]{:S(2)}, u32[]{:S(2)}) collective-permute-start(f32[2,16,128]{2,1,0:T(8,128)S(1)} %slice.93), channel_id=1, source_target_pairs={{32,0},{64,32},{96,64},{128,96},{160,128},{192,160},{224,192},{256... | collective-permute-start | bytes 49160 | tf_op jit(solution)/shard_map/ppermute | solution.py:464
  80.5 3.6 %collective-permute-done.2.below = f32[2,16,128]{2,1,0:T(8,128)S(1)} collective-permute-done((f32[2,16,128]{2,1,0:T(8,128)S(1)}, f32[2,16,128]{2,1,0:T(8,128)S(1)}, u32[]{:S(2)}, u32[]{:S(2)}) %collective-permute-start.2) | collective-permute-done | bytes 16416 | tf_op jit(solution)/shard_map/ppermute | solution.py:464
  84.1 6.8 %all-to-all-done.2.terms = f32[16,8,128]{2,1,0:T(8,128)S(1)} async-done(((f32[16,8,128]{2,1,0:T(8,128)}), f32[16,8,128]{2,1,0:T(8,128)S(1)}, u32[]{:S(2)}, u32[]{:S(2)}) %all-to-all-start.2) | async-done | bytes 65568 | tf_op jit(solution)/shard_map/all_to_all | solution.py:465
  90.9 1.6 %shard_map.197 = (f32[6,729]{1,0:T(8,128)}, f32[64,64]{1,0:T(8,128)}, f32[64,3]{1,0:T(8,128)S(1)}) custom-call(s32[15,3]{1,0:T(8,128)S(1)} %pad_add_fusion.meta, f32[4,16,128]{2,1,0:T(8,128)S(1)} %get-tuple-element.17.mine, f32[2,16,128]{2,1,0:T(8,128)S(1)} %collective-permute-done.2.below, f32[16,8,128]{2,1,0:T(8,128)S(1)} %all-to-all-done.2.terms, ...), custom_call_target="tpu_custom_call" | custom-call | tf_op jit(solution)/shard_map/pallas_call | solution.py:403
  (53 shorter events, 5.1 us)
Async XLA Ops:
  0.6 20.0 %copy-start.8 = (bf16[2,256,256]{2,1,0:T(8,128)(2,1)S(1)}, bf16[2,256,256]{2,1,0:T(8,128)(2,1)}, u32[]{:S(2)}) copy-start(bf16[2,256,256]{2,1,0:T(8,128)(2,1)} %constant.94.clone.alo) | copy-start | bytes 786436
  0.6 13.2 %copy-start = (bf16[2,4,8,32,256]{4,3,2,1,0:T(8,128)(2,1)S(1)}, bf16[2,4,8,32,256]{4,3,2,1,0:T(8,128)(2,1)}, u32[]{:S(2)}) copy-start(bf16[2,4,8,32,256]{4,3,2,1,0:T(8,128)(2,1)} %param.20) | copy-start | bytes 3145732
  1.9 18.7 %copy-start.6 = (bf16[2,256,256]{2,1,0:T(8,128)(2,1)S(1)}, bf16[2,256,256]{2,1,0:T(8,128)(2,1)}, u32[]{:S(2)}) copy-start(bf16[2,256,256]{2,1,0:T(8,128)(2,1)} %constant.93.clone.ahi) | copy-start | bytes 786436
  1.9 18.7 %collective-permute-start = (bf16[2,256,256]{2,1,0:T(8,128)(2,1)S(1)}, bf16[2,256,256]{2,1,0:T(8,128)(2,1)S(1)}, u32[]{:S(2)}, u32[]{:S(2)}) collective-permute-start(bf16[2,256,256]{2,1,0:T(8,128)(2,1)S(1)} %pad_maximum_fusion.1), channel_id=1, source_target_pairs={{0,32},{32,64},{64,96},{96,128},{128,160},{160,192},{192,224},{224... | collective-permute-start | bytes 786440 | tf_op jit(solution)/shard_map/ppermute | solution.py:426
  6.5 14.1 %collective-permute-start.1 = (bf16[256,256]{1,0:T(8,128)(2,1)S(1)}, bf16[256,256]{1,0:T(8,128)(2,1)S(1)}, u32[]{:S(2)}, u32[]{:S(2)}) collective-permute-start(bf16[256,256]{1,0:T(8,128)(2,1)S(1)} %get-tuple-element.30.own), channel_id=1, source_target_pairs={{0,16},{16,0},{1,17},{17,1},{2,18},{18,2},{3,19},{19,3},{4,20},{20... | collective-permute-start | bytes 393224 | tf_op jit(solution)/shard_map/ppermute | solution.py:430
  13.9 1.0 %copy-start.1 = (bf16[2,512,256]{2,1,0:T(8,128)(2,1)S(1)}, bf16[2,512,256]{2,1,0:T(8,128)(2,1)}, u32[]{:S(2)}) copy-start(bf16[2,512,256]{2,1,0:T(8,128)(2,1)} %constant.95.clone.bhi) | copy-start | bytes 1572868
  14.9 1.0 %copy-start.3 = (bf16[2,512,256]{2,1,0:T(8,128)(2,1)S(1)}, bf16[2,512,256]{2,1,0:T(8,128)(2,1)}, u32[]{:S(2)}) copy-start(bf16[2,512,256]{2,1,0:T(8,128)(2,1)} %constant.96.clone.blo) | copy-start | bytes 1572868
  16.0 0.9 %copy-start.5 = (bf16[2,256,256]{2,1,0:T(8,128)(2,1)S(1)}, bf16[2,256,256]{2,1,0:T(8,128)(2,1)}, u32[]{:S(2)}) copy-start(bf16[2,256,256]{2,1,0:T(8,128)(2,1)} %constant.93.clone.ahi) | copy-start | bytes 786436
  16.9 0.9 %copy-start.7 = (bf16[2,256,256]{2,1,0:T(8,128)(2,1)S(1)}, bf16[2,256,256]{2,1,0:T(8,128)(2,1)}, u32[]{:S(2)}) copy-start(bf16[2,256,256]{2,1,0:T(8,128)(2,1)} %constant.94.clone.alo) | copy-start | bytes 786436
  17.9 0.9 copy-start.9
  18.8 1.9 %copy-start.2 = (bf16[2,512,256]{2,1,0:T(8,128)(2,1)S(1)}, bf16[2,512,256]{2,1,0:T(8,128)(2,1)}, u32[]{:S(2)}) copy-start(bf16[2,512,256]{2,1,0:T(8,128)(2,1)} %constant.95.clone.bhi) | copy-start | bytes 1572868
  18.8 1.9 %copy-start.4 = (bf16[2,512,256]{2,1,0:T(8,128)(2,1)S(1)}, bf16[2,512,256]{2,1,0:T(8,128)(2,1)}, u32[]{:S(2)}) copy-start(bf16[2,512,256]{2,1,0:T(8,128)(2,1)} %constant.96.clone.blo) | copy-start | bytes 1572868
  22.3 10.4 %copy-start.17 = (s32[108,3]{0,1:T(4,128)S(1)}, s32[108,3]{0,1:T(4,128)}, u32[]{:S(2)}) copy-start(s32[108,3]{0,1:T(4,128)} %param.23) | copy-start | bytes 3892
  22.3 20.5 %copy-start.10 = (bf16[11,96,128]{2,1,0:T(8,128)(2,1)S(1)}, bf16[11,96,128]{2,1,0:T(8,128)(2,1)}, u32[]{:S(2)}) copy-start(bf16[11,96,128]{2,1,0:T(8,128)(2,1)} %constant.103.clone.vhi) | copy-start | bytes 811012
  22.3 20.5 %copy-start.11 = (bf16[11,96,128]{2,1,0:T(8,128)(2,1)S(1)}, bf16[11,96,128]{2,1,0:T(8,128)(2,1)}, u32[]{:S(2)}) copy-start(bf16[11,96,128]{2,1,0:T(8,128)(2,1)} %constant.104.clone.vlo) | copy-start | bytes 811012
  22.3 20.5 %copy-start.12 = (bf16[512,256]{1,0:T(8,128)(2,1)S(1)}, bf16[512,256]{1,0:T(8,128)(2,1)}, u32[]{:S(2)}) copy-start(bf16[512,256]{1,0:T(8,128)(2,1)} %constant.101.clone.mhi) | copy-start | bytes 786436
  22.3 20.5 %copy-start.13 = (bf16[512,256]{1,0:T(8,128)(2,1)S(1)}, bf16[512,256]{1,0:T(8,128)(2,1)}, u32[]{:S(2)}) copy-start(bf16[512,256]{1,0:T(8,128)(2,1)} %constant.102.clone.mlo) | copy-start | bytes 786436
  22.3 20.5 %copy-start.15 = (f32[4,16,128]{2,1,0:T(8,128)S(1)}, f32[4,16,128]{2,1,0:T(8,128)}, u32[]{:S(2)}) copy-start(f32[4,16,128]{2,1,0:T(8,128)} %constant.105.clone.shift) | copy-start | bytes 98308
  22.3 20.5 %copy-start.16 = (f32[2,32]{1,0:T(2,128)S(1)}, f32[2,32]{1,0:T(2,128)}, u32[]{:S(2)}) copy-start(f32[2,32]{1,0:T(2,128)} %constant.100.clone.circle) | copy-start | bytes 772
  23.3 19.4 %all-to-all-start = ((bf16[16,112,256]{2,1,0:T(8,128)(2,1)}), bf16[16,112,256]{2,1,0:T(8,128)(2,1)S(1)}, u32[]{:S(2)}, u32[]{:S(2)}) async-start(bf16[16,112,256]{2,1,0:T(8,128)(2,1)} %pad_maximum_fusion), calls=%async_computation | async-start | bytes 1835008 | tf_op jit(solution)/shard_map/all_to_all | solution.py:447
  42.8 48.0 %copy-start.14 = (f32[128,64]{1,0:T(8,128)S(1)}, f32[128,64]{1,0:T(8,128)}, u32[]{:S(2)}) copy-start(f32[128,64]{1,0:T(8,128)} %constant.106.clone.graph) | copy-start | bytes 98308
  46.9 17.5 %all-to-all-start.1 = ((f32[32,40,128]{2,1,0:T(8,128)}), f32[32,40,128]{2,1,0:T(8,128)S(1)}, u32[]{:S(2)}, u32[]{:S(2)}) async-start(f32[32,40,128]{2,1,0:T(8,128)} %shard_map.195), calls=%async_computation.1 | async-start | bytes 1310720 | tf_op jit(solution)/shard_map/all_to_all | solution.py:457
  65.2 25.7 %all-to-all-start.2 = ((f32[16,8,128]{2,1,0:T(8,128)}), f32[16,8,128]{2,1,0:T(8,128)S(1)}, u32[]{:S(2)}, u32[]{:S(2)}) async-start(f32[16,8,128]{2,1,0:T(8,128)} %get-tuple-element.18), calls=%async_computation.2 | async-start | bytes 131072 | tf_op jit(solution)/shard_map/all_to_all | solution.py:465
  79.2 4.9 %collective-permute-start.2 = (f32[2,16,128]{2,1,0:T(8,128)S(1)}, f32[2,16,128]{2,1,0:T(8,128)S(1)}, u32[]{:S(2)}, u32[]{:S(2)}) collective-permute-start(f32[2,16,128]{2,1,0:T(8,128)S(1)} %slice.93), channel_id=1, source_target_pairs={{32,0},{64,32},{96,64},{128,96},{160,128},{192,160},{224,192},{256... | collective-permute-start | bytes 49160 | tf_op jit(solution)/shard_map/ppermute | solution.py:464

commit v2 on v1

--- a/solution.py
+++ b/solution.py
@@ -31,6 +31,10 @@
     return high, low
 
 
+def lane_tiles(table):
+    return np.stack([table[..., :128], table[..., 128:]], axis=-3)
+
+
 def angles(rows, cols, length):
     return (np.outer(rows, cols) % length) * (2.0 * np.pi / length)
 
@@ -68,6 +72,37 @@
     table[0, :, 0] = np.where(np.arange(ALONG) % 2 == 0, 1.0, -1.0)
     table[1, :, HALF - 1] = 1.0
     return table
+
+
+HALF_ROWS = 2 * SUBS * LOCAL
+
+
+def plane_dft_tables():
+    across, along = split_np(across_table()), split_np(along_table())
+    extra = extra_table().astype(ml_dtypes.bfloat16)
+    pieces = [part[half] for half in range(2) for part in across]
+    pieces += [part[half] for half in range(2) for part in along]
+    pieces.append(np.concatenate([extra[0], extra[1]], axis=1))
+    return lane_tiles(np.concatenate(pieces, axis=0))
+
+
+def wide_rows(tables, start, count):
+    rows = pl.ds(pl.multiple_of(start, 256), count)
+    return jnp.concatenate([tables[0, rows, :], tables[1, rows, :]], axis=1)
+
+
+def across_rows(tables, half, low):
+    return wide_rows(tables, (2 * half + low) * HALF_ROWS, HALF_ROWS)
+
+
+def along_rows(tables, half, low):
+    start = 4 * HALF_ROWS + (2 * half + low) * 2 * ALONG
+    return wide_rows(tables, start, 2 * ALONG)
+
+
+def extra_rows(tables, half):
+    start = 4 * HALF_ROWS + 8 * ALONG
+    return tables[half, start : start + ALONG, :]
 
 
 def depth_table():
@@ -151,19 +186,21 @@
     return high, (value - high.astype(F32)).astype(BF)
 
 
-def across_dft(strip, half, across_hi, across_lo):
-    both = dot(across_hi[half], strip) + dot(across_lo[half], strip)
+def across_dft(strip, half, tables):
+    both = dot(across_rows(tables, half, 0), strip) + dot(across_rows(tables, half, 1), strip)
     rows = SUBS * LOCAL
     return jnp.concatenate([both[:rows], both[rows:]], axis=1)
 
 
-def along_dft(value, half, along_hi, along_lo, extra, count):
+def along_dft(value, half, tables, count):
     high, low = split(value)
-    out = dot(high, along_hi[half]) + dot(low, along_hi[half]) + dot(high, along_lo[half])
+    table_hi, table_lo = along_rows(tables, half, 0), along_rows(tables, half, 1)
+    out = dot(high, table_hi) + dot(low, table_hi) + dot(high, table_lo)
+    extra = extra_rows(tables, half)
     rows = SUBS * LOCAL
     edge_hi = jnp.concatenate([high[rows * k : rows * k + 16, :ALONG] for k in range(count)], axis=0)
     edge_lo = jnp.concatenate([low[rows * k : rows * k + 16, :ALONG] for k in range(count)], axis=0)
-    more = dot(edge_hi, extra[half]) + dot(edge_lo, extra[half])
+    more = dot(edge_hi, extra) + dot(edge_lo, extra)
     pieces = []
     for k in range(count):
         block = out[rows * k : rows * (k + 1)]
@@ -175,36 +212,73 @@
     return pieces
 
 
-def local_kernel(strips, ahi, alo, bhi, blo, extra, out):
+def pair_facts(where, pair_tiles, owner, pair_offset):
+    plane, core = where[0], where[1]
+    base = ROW * plane
+    count = owner.shape[1]
+    row = lax.broadcasted_iota(jnp.int32, (16, count), 0)
+    place = lax.broadcasted_iota(jnp.int32, (16, count), 1)
+    home = 2 * base + jnp.where(row == 1, 4, jnp.where(row == 2, 2, 0))
+    up = 2 * (base - ROW + row - 3) + 1
+    down = 2 * (base + 2 * core + row - 7) + 1
+    wanted = jnp.where(row < 3, home, jnp.where(row < 7, up, jnp.where(row < 9, down, -100)))
+    first, second = pair_tiles[0:1, :], pair_tiles[1:2, :]
+    key = first * 2 + jnp.where(second - first == 1, 0, 1)
+    match = wanted == key
+    owned = jnp.broadcast_to(owner[...] == 2 * plane + core, match.shape)
+
+    def total(mask, value):
+        return jnp.sum(jnp.where(mask, value, 0), axis=1, keepdims=True)
+
+    offset = [total(match, jnp.broadcast_to(pair_offset[k : k + 1, :], match.shape)) for k in range(3)]
+    at = total(match, place)
+    held = total(match & owned, 1)
+    ordinal = total((place < at) & owned, 1)
+    return offset, jnp.where(held > 0, ordinal, -1)
+
+
+def facts_kernel(where, pair_tiles, owner, pair_offset, ignored, facts, offsets):
+    del ignored
+    offset, slot = pair_facts(where, pair_tiles, owner, pair_offset)
+    lane = lax.broadcasted_iota(jnp.int32, (16, 128), 1)
+    facts[...] = jnp.where(
+        lane == 0, offset[0], jnp.where(lane == 1, offset[1], jnp.where(lane == 2, offset[2], slot))
+    )
+    lane = lane[:8]
+    offsets[...] = jnp.where(
+        lane == 1, offset[0][:8], jnp.where(lane == 2, offset[1][:8], offset[2][:8])
+    ).astype(F32)
+
+
+def local_kernel(strips, tables, out):
     chosen = (1, 4, 2, 6)
     parts = []
     for half in range(2):
-        stack = [across_dft(strips[k], half, ahi, alo) for k in chosen]
-        parts.append(along_dft(jnp.concatenate(stack, axis=0), half, bhi, blo, extra, 4))
+        stack = [across_dft(strips[k], half, tables) for k in chosen]
+        parts.append(along_dft(jnp.concatenate(stack, axis=0), half, tables, 4))
     for k in range(4):
         out[:, 16 * k : 16 * k + 16, :] = jnp.concatenate(
             [parts[0][k], parts[1][k]], axis=1
         ).astype(BF)
 
 
-def remote_kernel(core, below, own, other, ahi, alo, bhi, blo, extra, ignored, out):
-    del ignored
+def remote_kernel(where, here, below, own, other, tables, ignored, out):
+    del here, ignored
     parts = []
     for half in range(2):
-        stack = [across_dft(below[k], half, ahi, alo) for k in range(2)]
-        parts.append(along_dft(jnp.concatenate(stack, axis=0), half, bhi, blo, extra, 2))
+        stack = [across_dft(below[k], half, tables) for k in range(2)]
+        parts.append(along_dft(jnp.concatenate(stack, axis=0), half, tables, 2))
     for k in range(2):
-        out[:, 16 * k : 16 * k + 16, :] = jnp.concatenate(
+        out[:, 64 + 16 * k : 80 + 16 * k, :] = jnp.concatenate(
             [parts[0][k], parts[1][k]], axis=1
         ).astype(BF)
-    me = core[0]
-    is_left = me == 0
+    core = where[1]
     mine, theirs = own[...], other[...]
-    first = jnp.where(is_left, mine, theirs)
-    second = jnp.where(is_left, theirs, mine)
-    stack = [across_dft(strip, me, ahi, alo) for strip in (first, second)]
-    seam = along_dft(jnp.concatenate(stack, axis=0), me, bhi, blo, extra, 2)
-    out[:, 32:48, :] = jnp.concatenate(seam, axis=1).astype(BF)
+    first = jnp.where(core == 0, mine, theirs)
+    second = jnp.where(core == 0, theirs, mine)
+    stack = [across_dft(strip, core, tables) for strip in (first, second)]
+    seam = along_dft(jnp.concatenate(stack, axis=0), core, tables, 2)
+    out[:, 96:112, :] = jnp.concatenate(seam, axis=1).astype(BF)
 
 
 def spectrum_of(block, lanes, mhi, mlo):
@@ -231,8 +305,10 @@
     return real * norm, imag * norm_im
 
 
-def window_kernel(meta, circle, sub, core, got, mhi, mlo, vhi, vlo, ehi, elo, shift, out):
-    d, c = sub[0], core[0]
+def window_kernel(where, meta, circle, got, depth, vhi, vlo, planes, shift, out, table, arrived):
+    c, d = where[1], where[2]
+    fetch = pltpu.make_async_copy(planes.at[d], table, arrived)
+    fetch.start()
     row = lax.broadcasted_iota(jnp.int32, (2 * DEPTH, HALF), 0)
     lane = lax.broadcasted_iota(jnp.int32, (2 * DEPTH, HALF), 1)
     freq = lax.rem(row, DEPTH)
@@ -246,7 +322,7 @@
         return (low, high), edge
 
     lanes, edge = special(row // DEPTH)
-    mh, ml = mhi[...], mlo[...]
+    mh, ml = wide_rows(depth, 0, 512), wide_rows(depth, 512, 512)
 
     def spectrum(slot, masks):
         block = got[:, 16 * slot : 16 * slot + 16, :].reshape(2 * DEPTH, 2 * HALF)
@@ -296,22 +372,39 @@
     )
     terms = jnp.concatenate(pieces, axis=0)
     high, low = split(terms)
-    table_hi, table_lo = ehi[0], elo[0]
-    sums = dot(high, table_hi) + dot(low, table_hi) + dot(high, table_lo)
-    packed = jnp.concatenate(
-        [sums[16 * k : 16 * k + WIN] for k in range(4)] + [jnp.zeros((4, 128), F32)], axis=0
-    )
+    fetch.wait()
+    both = jnp.concatenate([table[0], table[1]], axis=1)
+    sums = dot(high, both) + jnp.concatenate(
+        [dot(low, both[:, :128]), jnp.zeros((64, 128), F32)], axis=1
+    )
+    sums = sums[:, :128] + sums[:, 128:]
+    wide = jnp.zeros((12, 256), F32)
+    for third in range(3):
+        rows = [sums[16 * k + 3 * third : 16 * k + 3 * third + 3] for k in range(4)]
+        rows = jnp.concatenate([jnp.concatenate(rows, axis=0), jnp.zeros((12, 128), F32)], axis=1)
+        wide = wide + (pltpu.roll(rows, 81 * third, 1) if third else rows)
+    packed = jnp.concatenate([wide[:, :128], wide[:, 128:]], axis=0)
     out[...] = jnp.broadcast_to(packed[None], out.shape)
 
 
-def energy_kernel(core, got, offsets, windows, terms):
+def unpack(packed):
+    wide = jnp.concatenate([packed[:12], packed[12:]], axis=1)
+    lane = lax.broadcasted_iota(jnp.int32, (12, 128), 1)
+    thirds = []
+    for third in range(3):
+        rows = pltpu.roll(wide, 256 - 81 * third, 1) if third else wide
+        thirds.append(jnp.where(lane < WIN * WIN, rows[:, :128], 0.0))
+    return [jnp.concatenate([t[3 * k : 3 * k + 3] for t in thirds], axis=0) for k in range(4)]
+
+
+def energy_kernel(where, got, offsets, windows, terms):
     left = got[0]
     right = got[SUBS]
     for k in range(1, SUBS):
         left = left + got[k]
         right = right + got[SUBS + k]
-    blocks = [left[:WIN], right[:WIN], left[27:36] + right[27:36]]
-    blocks += [left[9:18], left[18:27], right[9:18], right[18:27]]
+    left, right = unpack(left), unpack(right)
+    blocks = [left[0], right[0], left[3] + right[3], left[1], left[2], right[1], right[2]]
     step_z = (lax.broadcasted_iota(jnp.int32, (WIN, 128), 0) - REACH).astype(F32)
     sums, sums_z = [], []
     for block in blocks:
@@ -332,7 +425,7 @@
     value = jnp.where(lane == 0, energy, energy * place)
     value = jnp.where(lane < 4, value, 0.0)
     terms[...] = jnp.broadcast_to(value[None], terms.shape)
-    is_left = core[0] == 0
+    is_left = where[1] == 0
     mine = [
         jnp.where(is_left, blocks[0], blocks[1]),
         blocks[2],
@@ -344,15 +437,8 @@
         windows[k, WIN:, :] = jnp.zeros((16 - WIN, 128), F32)
 
 
-def final_kernel(meta, mine, below, terms, graph, windows, matrix, rhs):
-    slot = lax.broadcasted_iota(jnp.int32, (6, 128), 0)
-    blocks = [mine[k] for k in range(4)] + [below[k] for k in range(2)]
-    places = [slot == meta[9 + k, 0] for k in range(6)]
-    for step in range(WIN):
-        rows = jnp.zeros((6, 128), F32)
-        for block, place in zip(blocks, places):
-            rows = jnp.where(place, block[step : step + 1], rows)
-        windows[:, WIN * WIN * step : WIN * WIN * (step + 1)] = rows[:, : WIN * WIN]
+def graph_kernel(terms, graph, ignored, matrix, rhs):
+    del ignored
     table = graph[...]
     value = terms[...].reshape(PLANES * 8, 128)
     weighted = table * value[:, :1]
@@ -361,43 +447,25 @@
         table, weighted, over, precision=lax.Precision.HIGHEST, preferred_element_type=F32
     )
     load = lax.dot_general(
-        table, value, over, precision=lax.Precision.HIGHEST, preferred_element_type=F32
-    )
-    rhs[...] = load[:, 1:4]
-
-
-def pair_facts(pair_tiles, pair_owner, pair_offset, plane, core):
-    count = pair_owner.shape[0]
-    key = pair_tiles[:, 0] * 2 + (pair_tiles[:, 1] - pair_tiles[:, 0] != 1)
-    base = ROW * plane
-    here = [base, base + 2, base + 1]
-    up = [base - ROW + col for col in range(ROW)]
-    down = [base + 2 * core, base + 2 * core + 1]
-    wanted = jnp.stack([2 * t for t in here] + [2 * t + 1 for t in up + down])
-    match = (wanted[:, None] == key[None, :]).astype(jnp.int32)
-    owned = (pair_owner == 2 * plane + core).astype(jnp.int32)
-    place = jnp.arange(count, dtype=jnp.int32)
-    offset = jnp.sum(match[:, :, None] * pair_offset[None], axis=1)
-    at = jnp.sum(match * place[None], axis=1)
-    held = jnp.sum(match * owned[None], axis=1)
-    ordinal = jnp.sum((place[None] < at[:, None]).astype(jnp.int32) * owned[None], axis=1)
-    row = jnp.where(held > 0, ordinal, -1)
-    mine = jnp.stack(
-        [
-            jnp.where(core == 0, row[0], row[1]),
-            row[2],
-            jnp.where(core == 0, row[3], row[5]),
-            jnp.where(core == 0, row[4], row[6]),
-            row[7],
-            row[8],
-        ]
-    )
-    facts = jnp.concatenate([offset, jnp.broadcast_to(mine[:, None], (6, 3))], axis=0)
-    lanes = jnp.zeros((8, 128), F32).at[:7, 1:4].set(offset[:7].astype(F32))
-    return facts, lanes
-
-
-def call(kernel, shapes, operands, spaces, aliases=None, **params):
+        value, table, over, precision=lax.Precision.HIGHEST, preferred_element_type=F32
+    )
+    rhs[...] = load[1:4]
+
+
+def place_kernel(where, meta, mine, below, windows, done):
+    done[...] = mine[0, :8]
+    c = where[1]
+    slot = lax.broadcasted_iota(jnp.int32, (6, 128), 0)
+    blocks = [mine[k] for k in range(4)] + [below[k] for k in range(2)]
+    places = [slot == meta[k, 3] for k in (c, 2, 3 + 2 * c, 4 + 2 * c, 7, 8)]
+    for step in range(WIN):
+        rows = jnp.zeros((6, 128), F32)
+        for block, place in zip(blocks, places):
+            rows = jnp.where(place, block[step : step + 1], rows)
+        windows[:, WIN * WIN * step : WIN * WIN * (step + 1)] = rows[:, : WIN * WIN]
+
+
+def call(kernel, shapes, operands, spaces, **params):
     specs = [pl.BlockSpec(memory_space=space) for space in spaces]
     outs = jax.tree.map(lambda _: pl.BlockSpec(memory_space=pltpu.VMEM), shapes)
     return pl.pallas_call(
@@ -411,68 +479,66 @@
 
 
 def local(strips, pair_tiles, pair_owner, pair_offset):
-    plane, core, sub = (lax.axis_index(name) for name in ("z", "core", "sub"))
-    ahi, alo = split_np(across_table())
-    bhi, blo = split_np(along_table())
-    extra = extra_table().astype(ml_dtypes.bfloat16)
-    mhi, mlo = split_np(depth_table())
+    where = jnp.stack([lax.axis_index(name) for name in ("z", "core", "sub")]).astype(jnp.int32)
+    core = where[1]
+    tables = plane_dft_tables()
+    depth = lane_tiles(np.concatenate(split_np(depth_table()), axis=0))
     vhi, vlo = split_np(window_table())
-    ehi, elo = split_np(plane_table())
+    planes = np.stack(split_np(plane_table()), axis=1)
     vmem, smem = pltpu.VMEM, pltpu.SMEM
-    core_arr = core.reshape(1).astype(jnp.int32)
-    sub_arr = sub.reshape(1).astype(jnp.int32)
 
     tiles = strips.reshape(8, LOCAL * ACROSS, ALONG)
-    from_above = lax.ppermute(
-        jnp.stack([tiles[3], tiles[7]]), "z", [(k, k + 1) for k in range(PLANES - 1)]
-    )
-    own = jnp.where(core == 0, tiles[5], tiles[0])
+    bottoms = jnp.stack([tiles[3], tiles[7]])
+    from_above = lax.ppermute(bottoms, "z", [(k, k + 1) for k in range(PLANES - 1)])
+    core_after, bottoms = lax.optimization_barrier((core, bottoms))
+    own = lax.dynamic_index_in_dim(tiles, 5 - 5 * core_after, 0, keepdims=False)
     other = lax.ppermute(own, "core", [(0, 1), (1, 0)])
-    facts, lanes = pair_facts(pair_tiles, pair_owner, pair_offset, plane, core)
-
-    tables = (ahi, alo, bhi, blo, extra)
-    here = call(
-        local_kernel,
-        jax.ShapeDtypeStruct((SUBS, 64, 2 * HALF), BF),
-        (tiles,) + tables,
-        (vmem,) * 6,
-    )
-    there = call(
+
+    chunks = jax.ShapeDtypeStruct((SUBS, 16 * SLOTS, 2 * HALF), BF)
+    here = call(local_kernel, chunks, (tiles, tables), (vmem, vmem))
+    facts, offsets = call(
+        facts_kernel,
+        (jax.ShapeDtypeStruct((16, 128), jnp.int32), jax.ShapeDtypeStruct((8, 128), F32)),
+        (where, pair_tiles.T, pair_owner.reshape(1, -1), pair_offset.T, here),
+        (smem,) + (vmem,) * 3 + (pl.ANY,),
+    )
+    sent = call(
         remote_kernel,
-        jax.ShapeDtypeStruct((SUBS, 48, 2 * HALF), BF),
-        (core_arr, from_above, own, other) + tables + (core_arr,),
-        (smem,) + (vmem,) * 8 + (smem,),
-    )
-    sent = jnp.concatenate([here, there], axis=1)
+        chunks,
+        (where, here, from_above, own, other, tables, offsets),
+        (smem, vmem, vmem, vmem, vmem, vmem, pl.ANY),
+        input_output_aliases={1: 0},
+    )
     got = lax.all_to_all(sent, "sub", split_axis=0, concat_axis=0, tiled=True)
-
-    ehi_here = lax.dynamic_slice_in_dim(jnp.asarray(ehi), sub, 1, 0)
-    elo_here = lax.dynamic_slice_in_dim(jnp.asarray(elo), sub, 1, 0)
     partial = call(
         window_kernel,
-        jax.ShapeDtypeStruct((2 * SUBS, 40, 128), F32),
-        (facts, circle_table(), sub_arr, core_arr, got, mhi, mlo, vhi, vlo, ehi_here, elo_here, shift_table()),
-        (smem,) * 4 + (vmem,) * 8,
+        jax.ShapeDtypeStruct((2 * SUBS, 24, 128), F32),
+        (where, facts, circle_table(), got, depth, vhi, vlo, planes, shift_table()),
+        (smem,) * 3 + (vmem,) * 4 + (pltpu.HBM, vmem),
+        scratch_shapes=[pltpu.VMEM((2, 4 * HALF, 128), BF), pltpu.SemaphoreType.DMA],
     )
     shares = lax.all_to_all(partial, ("core", "sub"), split_axis=0, concat_axis=0, tiled=True)
     mine, terms = call(
         energy_kernel,
         (jax.ShapeDtypeStruct((4, 16, 128), F32), jax.ShapeDtypeStruct((PLANES, 8, 128), F32)),
-        (core_arr, shares, lanes),
+        (where, shares, offsets),
         (smem, vmem, vmem),
     )
     below = lax.ppermute(mine[2:], "z", [(k + 1, k) for k in range(PLANES - 1)])
     all_terms = lax.all_to_all(terms, "z", split_axis=0, concat_axis=0, tiled=True)
-    return call(
-        final_kernel,
-        (
-            jax.ShapeDtypeStruct((6, WIN * WIN * WIN), F32),
-            jax.ShapeDtypeStruct((64, 64), F32),
-            jax.ShapeDtypeStruct((64, 3), F32),
-        ),
-        (facts, mine, below, all_terms, graph_table()),
-        (smem,) + (vmem,) * 4,
-    )
+    windows, done = call(
+        place_kernel,
+        (jax.ShapeDtypeStruct((6, WIN * WIN * WIN), F32), jax.ShapeDtypeStruct((8, 128), F32)),
+        (where, facts, mine, below),
+        (smem, smem, vmem, vmem),
+    )
+    matrix, rhs = call(
+        graph_kernel,
+        (jax.ShapeDtypeStruct((64, 64), F32), jax.ShapeDtypeStruct((3, 64), F32)),
+        (all_terms, graph_table(), done),
+        (vmem, vmem, pl.ANY),
+    )
+    return windows, matrix, rhs.T
 
 
 def solution(mesh):

time: 94.5 us -> 85.5 us (0.905)
  blocking collectives: 0 us -> 32.9 us
  waiting for transfers between devices: 29.1 us -> 9.01 us
  starting transfers between devices: 34.6 us -> 25.4 us
  local copies, waits for them, and re-layouts: 10.6 us -> 4.66 us
  other arithmetic: 4.44 us -> 0.11 us
  between operations: 4.75 us -> 0.86 us
  Pallas kernels: 9.64 us -> 11.5 us
    all_to_all x0 -> x2, blocking collectives: none -> 32.9 us  [the longest x1 19 us: local(): got = lax.all_to_all(sent, 'sub', split_axis=0, concat_axis=0, tiled=True)]
    all_to_all x2 -> x0, waiting for transfers between devices: 18.7 us -> none  [the longest x1 9.96 us: local(): lax.all_to_all(partial, ('core', 'sub'), split_axis=0, concat_axis=0, til...]
    all_to_all x2 -> x0, starting transfers between devices: 9.07 us -> none  [the longest x1 5.15 us: local(): lax.all_to_all(partial, ('core', 'sub'), split_axis=0, concat_axis=0, til...]
    unnamed x36 -> x26, local copies, waits for them, and re-layouts: 4.96 us -> 2.73 us
    pallas_call x5 -> x7, Pallas kernels: 9.64 us -> 11.5 us  [call(): pl.pallas_call(kernel, out_shape=shapes, in_specs=specs, out_specs=outs,...]
    scatter x1 -> x0, local copies, waits for them, and re-layouts: 1.82 us -> none  [pair_facts(): lanes = jnp.zeros((8, 128), F32).at[:7, 1:4].set(offset[:7].astype(F32))]
    another operation x4 -> x0, local copies, waits for them, and re-layouts: 1.38 us -> none  [the longest x1 0.71 us: pair_facts(): jnp.stack([jnp.where(core == 0, row[0], row[1]), row[2], jnp.where(core =...]
    all_to_all x1, waiting for transfers between devices: 6.76 us -> 5.41 us  [local(): lax.all_to_all(terms, 'z', split_axis=0, concat_axis=0, tiled=True)]
  transfers between devices with their start and end apart: 6 -> 4, of which waited for: 4 -> 2; matrix products, arithmetic and copies ran while one was open for 8% -> 1% of each run, Pallas kernels for 2% -> 4%
where the time goes in v2:
time: 85.5 us; the launch traced here: 84.4 us
  blocking collectives  32.9 us (38%)
  starting transfers between devices  25.4 us (30%)
  Pallas kernels  11.5 us (13%)
  waiting for transfers between devices  9.01 us (11%)
  local copies, waits for them, and re-layouts  4.66 us (5%)
  between operations  0.86 us (1%)
    all_to_all x1, blocking collectives, local(): got = lax.all_to_all(sent, 'sub', split_axis=0, concat_axis=0, tiled=True)  19 us
    all_to_all x1, starting transfers between devices, local(): lax.all_to_all(terms, 'z', split_axis=0, concat_axis=0, tiled=True)  14 us
    all_to_all x1, blocking collectives, local(): lax.all_to_all(partial, ('core', 'sub'), split_axis=0, concat_axis=0, til...  13.9 us
    pallas_call x7, Pallas kernels, call(): pl.pallas_call(kernel, out_shape=shapes, in_specs=specs, out_specs=outs,...  11.5 us
    ppermute x1, starting transfers between devices, local(): other = lax.ppermute(own, 'core', [(0, 1), (1, 0)])  5.71 us
    all_to_all x1, waiting for transfers between devices, local(): lax.all_to_all(terms, 'z', split_axis=0, concat_axis=0, tiled=True)  5.41 us
    ppermute x1, starting transfers between devices, local(): lax.ppermute(bottoms, 'z', [(k, k + 1) for k in range(PLANES - 1)])  4.39 us
    ppermute x1, waiting for transfers between devices, local(): below = lax.ppermute(mine[2:], 'z', [(k + 1, k) for k in range(PLANES - 1)])  3.59 us
  transfers between devices with their start and end apart: 4, of which 2 were waited for; matrix products, arithmetic and copies ran while one was open for 1% of the time, Pallas kernels for 4%

profile of v2, /device:TPU:1, one launch (start us, length us, event | category | flops | bytes accessed | tf_op | source)
XLA Modules:
  0.0 84.4 jit_solution(6141503029274179426)
XLA Ops:
  0.7 1.0 %fusion = (bf16[1,256,256]{2,1,0:T(8,128)(2,1)S(1)}, bf16[1,256,256]{2,1,0:T(8,128)(2,1)S(1)}) fusion(bf16[8,256,256]{2,1,0:T(8,128)(2,1)} %bitcast.10), kind=kLoop, calls=%fused_computation.3 | loop fusion | bytes 524288 | tf_op jit(solution)/shard_map/slice | solution.py:491
  1.7 4.4 %collective-permute-start = (bf16[2,256,256]{2,1,0:T(8,128)(2,1)S(1)}, bf16[2,256,256]{2,1,0:T(8,128)(2,1)S(1)}, u32[]{:S(2)}, u32[]{:S(2)}) collective-permute-start(bf16[2,256,256]{2,1,0:T(8,128)(2,1)S(1)} %pad_maximum_fusion), channel_id=1, source_target_pairs={{0,32},{32,64},{64,96},{96,128},{128,160},{160,192},{192,224},{224... | collective-permute-start | bytes 786440 | tf_op jit(solution)/shard_map/ppermute | solution.py:492
  6.1 0.9 %dynamic-slice_bitcast_fusion.own = bf16[256,256]{1,0:T(8,128)(2,1)S(1)} fusion(bf16[8,256,256]{2,1,0:T(8,128)(2,1)} %bitcast.11, s32[]{:T(128)S(6)} %select_n.4), kind=kLoop, calls=%fused_computation.1 | loop fusion | bytes 262148 | tf_op jit(solution)/shard_map/jit(dynamic_index_in_dim)/squeeze | solution.py:494
  7.0 5.7 %collective-permute-start.1 = (bf16[256,256]{1,0:T(8,128)(2,1)S(1)}, bf16[256,256]{1,0:T(8,128)(2,1)S(1)}, u32[]{:S(2)}, u32[]{:S(2)}) collective-permute-start(bf16[256,256]{1,0:T(8,128)(2,1)S(1)} %dynamic-slice_bitcast_fusion.own), channel_id=1, source_target_pairs={{0,16},{16,0},{1,17},{17,1},{2,18},{18,2},{3,19},{19,3},{4,20},{20... | collective-permute-start | bytes 393224 | tf_op jit(solution)/shard_map/ppermute | solution.py:495
  12.8 1.4 %copy-done = bf16[2,3328,128]{2,1,0:T(8,128)(2,1)S(1)} copy-done((bf16[2,3328,128]{2,1,0:T(8,128)(2,1)S(1)}, bf16[2,3328,128]{2,1,0:T(8,128)(2,1)}, u32[]{:S(2)}) %copy-start) | copy-done | bytes 1703960
  14.2 1.2 %copy-done.3 = bf16[2,4,8,32,256]{4,3,2,1,0:T(8,128)(2,1)S(1)} copy-done((bf16[2,4,8,32,256]{4,3,2,1,0:T(8,128)(2,1)S(1)}, bf16[2,4,8,32,256]{4,3,2,1,0:T(8,128)(2,1)}, u32[]{:S(2)}) %copy-start.3) | copy-done | bytes 1048600
  15.4 1.6 %shard_map.139.ignored.here = bf16[16,112,256]{2,1,0:T(8,128)(2,1)S(1)} custom-call(bf16[8,256,256]{2,1,0:T(8,128)(2,1)S(1)} %bitcast.12, bf16[2,3328,128]{2,1,0:T(8,128)(2,1)S(1)} %copy-done), custom_call_target="tpu_custom_call" | custom-call | tf_op jit(solution)/shard_map/pallas_call | solution.py:471
  17.1 0.0 copy-start.4
  17.1 0.0 copy-start.5
  17.1 0.0 copy-start.6
  17.1 0.0 copy-start.8
  17.1 0.1 pad_add_fusion.where
  17.2 0.7 shard_map.140
  18.0 2.1 %shard_map.141 = bf16[16,112,256]{2,1,0:T(8,128)(2,1)S(1)} custom-call(s32[3]{0:T(128)S(1)} %pad_add_fusion.where, bf16[16,112,256]{2,1,0:T(8,128)(2,1)S(1)} %shard_map.139.ignored.here, bf16[2,256,256]{2,1,0:T(8,128)(2,1)S(1)} %collective-permute-done.below, bf16[256,256]{1,0:T(8,128)(2,1)S(1)} %dynamic-slice_bitcast_fusion.own, ...), custom_call_target="tpu_custom_call", output_to_operand_aliasing={{}: (1, {})} | custom-call | tf_op jit(solution)/shard_map/pallas_call | solution.py:471
  20.1 19.0 %all_to_all.15.got = bf16[16,112,256]{2,1,0:T(8,128)(2,1)S(1)} all-to-all(bf16[16,112,256]{2,1,0:T(8,128)(2,1)S(1)} %shard_map.141), channel_id=1, replica_groups=mesh['z'=16,'core'=2,'sub'=16] {'sub'}, dimensions={0} | all-to-all | bytes 1835008 | tf_op jit(solution)/shard_map/all_to_all | solution.py:512
  39.2 3.3 %shard_map.142 = f32[32,24,128]{2,1,0:T(8,128)S(1)} custom-call(s32[3]{0:T(128)S(1)} %pad_add_fusion.where, s32[16,128]{1,0:T(8,128)S(1)} %get-tuple-element.12.meta, f32[2,32]{1,0:T(2,128)S(1)} %copy-done.11, bf16[16,112,256]{2,1,0:T(8,128)(2,1)S(1)} %all_to_all.15.got, bf16[2,1024,128]{2,1,0:T(8,128)(2,1)S(1)} %copy-done.4, ...), custom_call_target="tpu_custom_call" | custom-call | tf_op jit(solution)/shard_map/pallas_call | solution.py:471
  42.5 13.9 %all_to_all.16.got = f32[32,24,128]{2,1,0:T(8,128)S(1)} all-to-all(f32[32,24,128]{2,1,0:T(8,128)S(1)} %shard_map.142), channel_id=1, replica_groups=mesh['z'=16,'core'=2,'sub'=16] {'core','sub'}, dimensions={0} | all-to-all | bytes 786432 | tf_op jit(solution)/shard_map/all_to_all | solution.py:520
  56.3 1.4 %shard_map.143 = (f32[4,16,128]{2,1,0:T(8,128)S(1)}, f32[16,8,128]{2,1,0:T(8,128)}) custom-call(s32[3]{0:T(128)S(1)} %pad_add_fusion.where, f32[32,24,128]{2,1,0:T(8,128)S(1)} %all_to_all.16.got, f32[8,128]{1,0:T(8,128)S(1)} %get-tuple-element.14.ignored.offsets), custom_call_target="tpu_custom_call" | custom-call | tf_op jit(solution)/shard_map/pallas_call | solution.py:471
  57.7 14.0 %all-to-all-start.2 = ((f32[16,8,128]{2,1,0:T(8,128)}), f32[16,8,128]{2,1,0:T(8,128)S(1)}, u32[]{:S(2)}, u32[]{:S(2)}) async-start(f32[16,8,128]{2,1,0:T(8,128)} %get-tuple-element.17), calls=%async_computation.2 | async-start | bytes 131072 | tf_op jit(solution)/shard_map/all_to_all | solution.py:528
  71.7 1.3 %collective-permute-start.2 = (f32[2,16,128]{2,1,0:T(8,128)S(1)}, f32[2,16,128]{2,1,0:T(8,128)S(1)}, u32[]{:S(2)}, u32[]{:S(2)}) collective-permute-start(f32[2,16,128]{2,1,0:T(8,128)S(1)} %slice.11), channel_id=1, source_target_pairs={{32,0},{64,32},{96,64},{128,96},{160,128},{192,160},{224,192},{256... | collective-permute-start | bytes 49160 | tf_op jit(solution)/shard_map/ppermute | solution.py:527
  73.0 3.6 %collective-permute-done.2.below = f32[2,16,128]{2,1,0:T(8,128)S(1)} collective-permute-done((f32[2,16,128]{2,1,0:T(8,128)S(1)}, f32[2,16,128]{2,1,0:T(8,128)S(1)}, u32[]{:S(2)}, u32[]{:S(2)}) %collective-permute-start.2) | collective-permute-done | bytes 16416 | tf_op jit(solution)/shard_map/ppermute | solution.py:527
  76.6 1.4 %shard_map.144 = (f32[6,729]{1,0:T(8,128)}, f32[8,128]{1,0:T(8,128)S(1)}) custom-call(s32[3]{0:T(128)S(1)} %pad_add_fusion.where, s32[16,128]{1,0:T(8,128)S(1)} %get-tuple-element.12.meta, f32[4,16,128]{2,1,0:T(8,128)S(1)} %get-tuple-element.15.mine, f32[2,16,128]{2,1,0:T(8,128)S(1)} %collective-permute-done.2.below), custom_call_target="tpu_custom_call" | custom-call | tf_op jit(solution)/shard_map/pallas_call | solution.py:471
  78.0 5.4 %all-to-all-done.2.terms = f32[16,8,128]{2,1,0:T(8,128)S(1)} async-done(((f32[16,8,128]{2,1,0:T(8,128)}), f32[16,8,128]{2,1,0:T(8,128)S(1)}, u32[]{:S(2)}, u32[]{:S(2)}) %all-to-all-start.2) | async-done | bytes 65568 | tf_op jit(solution)/shard_map/all_to_all | solution.py:528
  83.4 0.9 %shard_map.145 = (f32[64,64]{1,0:T(8,128)}, f32[3,64]{1,0:T(4,128)}) custom-call(f32[16,8,128]{2,1,0:T(8,128)S(1)} %all-to-all-done.2.terms, f32[128,64]{1,0:T(8,128)S(1)} %copy-done.7, f32[8,128]{1,0:T(8,128)S(1)} %get-tuple-element.18.ignored), custom_call_target="tpu_custom_call" | custom-call | tf_op jit(solution)/shard_map/pallas_call | solution.py:471
  (24 shorter events, 0.1 us)
Async XLA Ops:
  0.6 16.6 %copy-start.10 = (s32[108,2]{0,1:T(2,128)S(1)}, s32[108,2]{0,1:T(2,128)}, u32[]{:S(2)}) copy-start(s32[108,2]{0,1:T(2,128)} %param.13) | copy-start | bytes 2596
  0.6 16.6 %copy-start.12 = (s32[108]{0:T(128)S(1)}, s32[108]{0:T(128)}, u32[]{:S(2)}) copy-start(s32[108]{0:T(128)} %param.14) | copy-start | bytes 1300
  0.7 16.6 %copy-start.9 = (s32[108,3]{0,1:T(4,128)S(1)}, s32[108,3]{0,1:T(4,128)}, u32[]{:S(2)}) copy-start(s32[108,3]{0,1:T(4,128)} %param.15) | copy-start | bytes 3892
  1.7 16.3 %collective-permute-start = (bf16[2,256,256]{2,1,0:T(8,128)(2,1)S(1)}, bf16[2,256,256]{2,1,0:T(8,128)(2,1)S(1)}, u32[]{:S(2)}, u32[]{:S(2)}) collective-permute-start(bf16[2,256,256]{2,1,0:T(8,128)(2,1)S(1)} %pad_maximum_fusion), channel_id=1, source_target_pairs={{0,32},{32,64},{64,96},{96,128},{128,160},{160,192},{192,224},{224... | collective-permute-start | bytes 786440 | tf_op jit(solution)/shard_map/ppermute | solution.py:492
  7.0 10.9 %collective-permute-start.1 = (bf16[256,256]{1,0:T(8,128)(2,1)S(1)}, bf16[256,256]{1,0:T(8,128)(2,1)S(1)}, u32[]{:S(2)}, u32[]{:S(2)}) collective-permute-start(bf16[256,256]{1,0:T(8,128)(2,1)S(1)} %dynamic-slice_bitcast_fusion.own), channel_id=1, source_target_pairs={{0,16},{16,0},{1,17},{17,1},{2,18},{18,2},{3,19},{19,3},{4,20},{20... | collective-permute-start | bytes 393224 | tf_op jit(solution)/shard_map/ppermute | solution.py:495
  12.7 1.5 %copy-start = (bf16[2,3328,128]{2,1,0:T(8,128)(2,1)S(1)}, bf16[2,3328,128]{2,1,0:T(8,128)(2,1)}, u32[]{:S(2)}) copy-start(bf16[2,3328,128]{2,1,0:T(8,128)(2,1)} %constant.38.clone.tables) | copy-start | bytes 5111812
  14.2 1.2 %copy-start.3 = (bf16[2,4,8,32,256]{4,3,2,1,0:T(8,128)(2,1)S(1)}, bf16[2,4,8,32,256]{4,3,2,1,0:T(8,128)(2,1)}, u32[]{:S(2)}) copy-start(bf16[2,4,8,32,256]{4,3,2,1,0:T(8,128)(2,1)} %param.12) | copy-start | bytes 3145732
  15.4 2.5 %copy-start.1 = (bf16[2,3328,128]{2,1,0:T(8,128)(2,1)S(1)}, bf16[2,3328,128]{2,1,0:T(8,128)(2,1)}, u32[]{:S(2)}) copy-start(bf16[2,3328,128]{2,1,0:T(8,128)(2,1)} %constant.38.clone.tables) | copy-start | bytes 5111812
  17.1 22.1 %copy-start.2 = (bf16[16,2,512,128]{3,2,1,0:T(8,128)(2,1)S(1)}, bf16[16,2,512,128]{3,2,1,0:T(8,128)(2,1)}, u32[]{:S(2)}) copy-start(bf16[16,2,512,128]{3,2,1,0:T(8,128)(2,1)} %constant.43.clone.planes) | copy-start | bytes 12582916
  17.1 22.1 %copy-start.4 = (bf16[2,1024,128]{2,1,0:T(8,128)(2,1)S(1)}, bf16[2,1024,128]{2,1,0:T(8,128)(2,1)}, u32[]{:S(2)}) copy-start(bf16[2,1024,128]{2,1,0:T(8,128)(2,1)} %constant.40.clone.depth) | copy-start | bytes 1572868
  17.1 22.1 %copy-start.5 = (bf16[11,96,128]{2,1,0:T(8,128)(2,1)S(1)}, bf16[11,96,128]{2,1,0:T(8,128)(2,1)}, u32[]{:S(2)}) copy-start(bf16[11,96,128]{2,1,0:T(8,128)(2,1)} %constant.41.clone.vhi) | copy-start | bytes 811012
  17.1 22.0 %copy-start.6 = (bf16[11,96,128]{2,1,0:T(8,128)(2,1)S(1)}, bf16[11,96,128]{2,1,0:T(8,128)(2,1)}, u32[]{:S(2)}) copy-start(bf16[11,96,128]{2,1,0:T(8,128)(2,1)} %constant.42.clone.vlo) | copy-start | bytes 811012
  17.1 22.0 %copy-start.8 = (f32[4,16,128]{2,1,0:T(8,128)S(1)}, f32[4,16,128]{2,1,0:T(8,128)}, u32[]{:S(2)}) copy-start(f32[4,16,128]{2,1,0:T(8,128)} %constant.44.clone.shift) | copy-start | bytes 98308
  17.1 22.0 %copy-start.11 = (f32[2,32]{1,0:T(2,128)S(1)}, f32[2,32]{1,0:T(2,128)}, u32[]{:S(2)}) copy-start(f32[2,32]{1,0:T(2,128)} %constant.39.clone.circle) | copy-start | bytes 772
  39.1 44.3 %copy-start.7 = (f32[128,64]{1,0:T(8,128)S(1)}, f32[128,64]{1,0:T(8,128)}, u32[]{:S(2)}) copy-start(f32[128,64]{1,0:T(8,128)} %constant.45.clone.graph) | copy-start | bytes 98308
  57.7 25.7 %all-to-all-start.2 = ((f32[16,8,128]{2,1,0:T(8,128)}), f32[16,8,128]{2,1,0:T(8,128)S(1)}, u32[]{:S(2)}, u32[]{:S(2)}) async-start(f32[16,8,128]{2,1,0:T(8,128)} %get-tuple-element.17), calls=%async_computation.2 | async-start | bytes 131072 | tf_op jit(solution)/shard_map/all_to_all | solution.py:528
  71.7 4.9 %collective-permute-start.2 = (f32[2,16,128]{2,1,0:T(8,128)S(1)}, f32[2,16,128]{2,1,0:T(8,128)S(1)}, u32[]{:S(2)}, u32[]{:S(2)}) collective-permute-start(f32[2,16,128]{2,1,0:T(8,128)S(1)} %slice.11), channel_id=1, source_target_pairs={{32,0},{64,32},{96,64},{128,96},{160,128},{192,160},{224,192},{256... | collective-permute-start | bytes 49160 | tf_op jit(solution)/shard_map/ppermute | solution.py:527

commit v3 on v2

--- a/solution.py
+++ b/solution.py
@@ -20,7 +20,6 @@
 VOXELS = DEPTH * ACROSS * ALONG
 MAX_OFF = 5
 OFFS = 2 * MAX_OFF + 1
-SLOTS = 7
 BF = jnp.bfloat16
 F32 = jnp.float32
 
@@ -132,22 +131,28 @@
     return table.reshape(OFFS, 96, DEPTH)
 
 
-def plane_table():
-    table = np.zeros((SUBS, 2, 2, HALF, 128))
+def step_table():
     step = np.arange(WIN) - REACH
-    ones = np.ones(WIN)
+    table = np.zeros((2, 2, HALF, 128))
+    for half in range(2):
+        theta = angles(np.arange(HALF) + half, step, ALONG)
+        table[half, 0, :, :WIN] = np.cos(theta)
+        table[half, 1, :, :WIN] = -np.sin(theta)
+        table[half, 0, :, 64 : 64 + WIN] = np.sin(theta)
+        table[half, 1, :, 64 : 64 + WIN] = np.cos(theta)
+    high, low = split_np(table.reshape(2, 2 * HALF, 128) * (2.0 / VOXELS))
+    return np.stack([high, low], axis=1)
+
+
+def turn_table():
+    step = np.arange(WIN) - REACH
+    table = np.zeros((SUBS, 16, 128), np.float32)
     for sub in range(SUBS):
-        for half in range(2):
-            freq = np.arange(HALF) + half
-            theta_x = angles(freq, step, ALONG)
-            theta_y = angles([across_freq(half, sub)], step, ACROSS)[0]
-            theta = theta_y[None, :, None] + theta_x[:, None, :]
-            table[sub, half, 0, :, : WIN * WIN] = np.cos(theta).reshape(HALF, -1)
-            table[sub, half, 1, :, : WIN * WIN] = -np.sin(theta).reshape(HALF, -1)
-    sign = np.where(step % 2 == 0, 1.0, -1.0)
-    table[0, 0, 1, 0, : WIN * WIN] = np.outer(ones, sign).reshape(-1)
-    table[0, 1, 1, HALF - 1, : WIN * WIN] = np.outer(sign, ones).reshape(-1)
-    return table.reshape(SUBS, 4 * HALF, 128) * (2.0 / VOXELS)
+        theta = angles(step, [sub], ACROSS)
+        table[sub, :WIN, :64] = np.cos(theta)
+        table[sub, :WIN, 64:] = -np.sin(theta)
+    table[0, :WIN, 64:] = np.where(step % 2 == 0, 1.0, -1.0)[:, None]
+    return table
 
 
 def shift_table():
@@ -157,6 +162,19 @@
         table[half, 0, :OFFS] = np.cos(theta)
         table[half, 1, :OFFS] = np.sin(theta)
     return table.reshape(4, 16, HALF).astype(np.float32)
+
+
+GROUP = 6
+
+
+def place_table():
+    table = np.zeros((3, 4, 8, 128), np.float32)
+    for index in range(4 * WIN):
+        pair, depth = divmod(index, WIN)
+        group, row = divmod(index, GROUP)
+        for along in range(WIN):
+            table[:, pair, row, WIN * group + along] = (1.0, depth - REACH, along - REACH)
+    return table
 
 
 def circle_table():
@@ -250,45 +268,55 @@
     ).astype(F32)
 
 
-def local_kernel(strips, tables, out):
+def chunk(pieces):
+    return jnp.concatenate(pieces, axis=1).astype(BF)
+
+
+def local_kernel(where, strips, own, other, tables, out):
     chosen = (1, 4, 2, 6)
     parts = []
     for half in range(2):
         stack = [across_dft(strips[k], half, tables) for k in chosen]
         parts.append(along_dft(jnp.concatenate(stack, axis=0), half, tables, 4))
     for k in range(4):
-        out[:, 16 * k : 16 * k + 16, :] = jnp.concatenate(
-            [parts[0][k], parts[1][k]], axis=1
-        ).astype(BF)
-
-
-def remote_kernel(where, here, below, own, other, tables, ignored, out):
-    del here, ignored
-    parts = []
-    for half in range(2):
-        stack = [across_dft(below[k], half, tables) for k in range(2)]
-        parts.append(along_dft(jnp.concatenate(stack, axis=0), half, tables, 2))
-    for k in range(2):
-        out[:, 64 + 16 * k : 80 + 16 * k, :] = jnp.concatenate(
-            [parts[0][k], parts[1][k]], axis=1
-        ).astype(BF)
+        out[:, 16 * k : 16 * k + 16, :] = chunk([parts[0][k], parts[1][k]])
     core = where[1]
     mine, theirs = own[...], other[...]
     first = jnp.where(core == 0, mine, theirs)
     second = jnp.where(core == 0, theirs, mine)
     stack = [across_dft(strip, core, tables) for strip in (first, second)]
-    seam = along_dft(jnp.concatenate(stack, axis=0), core, tables, 2)
-    out[:, 96:112, :] = jnp.concatenate(seam, axis=1).astype(BF)
-
-
-def spectrum_of(block, lanes, mhi, mlo):
-    both = dot(mhi, block) + dot(mlo, block)
+    out[:, 96:112, :] = chunk(along_dft(jnp.concatenate(stack, axis=0), core, tables, 2))
+
+
+def remote_kernel(here, below, tables, ignored, out, moved):
+    del ignored
+    kept = ((pl.ds(0, 16), pl.ds(0, 64)), (pl.ds(0, 16), pl.ds(96, 16)))
+    copies = [
+        pltpu.make_async_copy(here.at[at + (slice(None),)], out.at[at + (slice(None),)], moved.at[k])
+        for k, at in enumerate(kept)
+    ]
+    for copy in copies:
+        copy.start()
+    parts = []
+    for half in range(2):
+        stack = [across_dft(below[k], half, tables) for k in range(2)]
+        parts.append(along_dft(jnp.concatenate(stack, axis=0), half, tables, 2))
+    for k in range(2):
+        out[:, 64 + 16 * k : 80 + 16 * k, :] = chunk([parts[0][k], parts[1][k]])
+    for copy in copies:
+        copy.wait()
+
+
+def spectrum_of(block, lanes, depth_hi, depth_lo):
+    both = dot(depth_hi, block) + dot(depth_lo, block)
     cos, sin = both[: 2 * DEPTH], both[2 * DEPTH :]
     cos_re, cos_im = cos[:, :HALF], cos[:, HALF:]
     sin_re, sin_im = sin[:, :HALF], sin[:, HALF:]
-    low, high = lanes
-    real = jnp.where(low, cos_re, jnp.where(high, cos_im, cos_re + sin_im))
-    imag = jnp.where(low, -sin_re, jnp.where(high, -sin_im, cos_im - sin_re))
+    real, imag = cos_re + sin_im, cos_im - sin_re
+    if lanes is not None:
+        low, high = lanes
+        real = jnp.where(low, cos_re, jnp.where(high, cos_im, real))
+        imag = jnp.where(low, -sin_re, jnp.where(high, -sin_im, imag))
     return real, imag
 
 
@@ -297,18 +325,21 @@
     first_re, first_im = first
     second_re, second_im = second
     straight, crossed = first_re * second_re, first_im * second_im
+    imag = first_im * second_re - first_re * second_im
+    if edge is None:
+        real = straight + crossed
+        norm = lax.rsqrt(real * real + imag * imag + floor)
+        return real * norm, imag * norm
     real = straight + jnp.where(edge, 0.0, crossed)
-    imag = jnp.where(edge, crossed, first_im * second_re - first_re * second_im)
+    imag = jnp.where(edge, crossed, imag)
     real_sq, imag_sq = real * real, imag * imag
     norm = lax.rsqrt(real_sq + jnp.where(edge, 0.0, imag_sq) + floor)
     norm_im = jnp.where(edge, lax.rsqrt(imag_sq + floor), norm)
     return real * norm, imag * norm_im
 
 
-def window_kernel(where, meta, circle, got, depth, vhi, vlo, planes, shift, out, table, arrived):
+def window_kernel(where, meta, circle, got, depth, vhi, vlo, steps, shift, out):
     c, d = where[1], where[2]
-    fetch = pltpu.make_async_copy(planes.at[d], table, arrived)
-    fetch.start()
     row = lax.broadcasted_iota(jnp.int32, (2 * DEPTH, HALF), 0)
     lane = lax.broadcasted_iota(jnp.int32, (2 * DEPTH, HALF), 1)
     freq = lax.rem(row, DEPTH)
@@ -322,27 +353,23 @@
         return (low, high), edge
 
     lanes, edge = special(row // DEPTH)
-    mh, ml = wide_rows(depth, 0, 512), wide_rows(depth, 512, 512)
+    depth_hi, depth_lo = wide_rows(depth, 0, 512), wide_rows(depth, 512, 512)
 
     def spectrum(slot, masks):
         block = got[:, 16 * slot : 16 * slot + 16, :].reshape(2 * DEPTH, 2 * HALF)
-        return spectrum_of(block, masks, mh, ml)
+        return spectrum_of(block, masks, depth_hi, depth_lo)
 
     small_lane = lax.broadcasted_iota(jnp.int32, (16, HALF), 1)
 
     def window_rows(phase, half, slot):
         off_z, off_y, off_x = meta[slot, 0], meta[slot, 1], meta[slot, 2]
-        both = jnp.concatenate(phase, axis=1)
-        high, low = split(both)
+        high, low = split(jnp.concatenate(phase, axis=1))
         table_hi, table_lo = vhi[off_z + MAX_OFF], vlo[off_z + MAX_OFF]
         rows = dot(table_hi, high) + dot(table_lo, high) + dot(table_hi, low)
         part = [(rows[16 * k : 16 * k + 16, :HALF], rows[16 * k : 16 * k + 16, HALF:]) for k in range(6)]
-        real = part[0][0] - part[1][1]
-        imag = part[1][0] + part[0][1]
         held = small_lane == half * (HALF - 1) + nowhere
-        sign = jnp.where(lax.rem(off_x + 6, 2) == 0, 1.0, -1.0).astype(F32)
-        real = jnp.where(held, part[2][0] - part[3][1], real)
-        imag = jnp.where(held, (part[4][0] + part[5][1]) * sign, imag)
+        real = jnp.where(held, part[2][0] - part[3][1], part[0][0] - part[1][1])
+        imag = jnp.where(held, 0.0, part[1][0] + part[0][1])
         freq_y = jnp.where(half == 0, d, jnp.where(d == 0, ACROSS // 2, ACROSS - d))
         turn = lax.rem(freq_y * (off_y + ACROSS), ACROSS)
         cos_y, sin_y = circle[0, turn], circle[1, turn]
@@ -350,91 +377,107 @@
         sin_x = shift[2 * half + 1, pl.ds(off_x + MAX_OFF, 1), :]
         cos = cos_x * cos_y - sin_x * sin_y
         sin = sin_x * cos_y + cos_x * sin_y
-        return jnp.concatenate([real * cos - imag * sin, real * sin + imag * cos], axis=1)
-
-    pieces = []
+        turned = jnp.concatenate([real * cos - imag * sin, real * sin + imag * cos], axis=1)
+        other = jnp.sum(jnp.where(held, part[4][0] + part[5][1], 0.0), axis=1, keepdims=True)
+        even = (lax.rem(small_lane + off_x + 6, 2) == 0) | (half == 1)
+        sign = jnp.where(even, 1.0, -1.0) * (cos_y * (2.0 / VOXELS))
+        return turned, other * jnp.where(small_lane < WIN, sign, 0.0)
+
+    terms, extra = ([], []), ([], [])
     for first, second, slot in ((0, 1, c), (4, 2, 3 + 2 * c), (5, 3, 4 + 2 * c)):
         real, imag = phase_of(spectrum(first, lanes), spectrum(second, lanes), edge)
-        halves = [
-            window_rows((real[DEPTH * h : DEPTH * (h + 1)], imag[DEPTH * h : DEPTH * (h + 1)]), h, slot)
-            for h in range(2)
-        ]
-        pieces.append(jnp.concatenate(halves, axis=1))
+        for half in range(2):
+            rows = slice(DEPTH * half, DEPTH * (half + 1))
+            turned, more = window_rows((real[rows], imag[rows]), half, slot)
+            terms[half].append(turned)
+            extra[half].append(more)
     seam_lanes, seam_edge = special(c)
     real, imag = spectrum(6, seam_lanes)
     phase = phase_of(
         (real[:DEPTH], imag[:DEPTH]), (real[DEPTH:], imag[DEPTH:]), seam_edge[:DEPTH]
     )
-    seam = window_rows(phase, c, 2)
-    empty = jnp.zeros_like(seam)
-    pieces.append(
-        jnp.concatenate([jnp.where(c == 0, seam, empty), jnp.where(c == 0, empty, seam)], axis=1)
-    )
-    terms = jnp.concatenate(pieces, axis=0)
-    high, low = split(terms)
-    fetch.wait()
-    both = jnp.concatenate([table[0], table[1]], axis=1)
-    sums = dot(high, both) + jnp.concatenate(
-        [dot(low, both[:, :128]), jnp.zeros((64, 128), F32)], axis=1
-    )
-    sums = sums[:, :128] + sums[:, 128:]
-    wide = jnp.zeros((12, 256), F32)
-    for third in range(3):
-        rows = [sums[16 * k + 3 * third : 16 * k + 3 * third + 3] for k in range(4)]
-        rows = jnp.concatenate([jnp.concatenate(rows, axis=0), jnp.zeros((12, 128), F32)], axis=1)
-        wide = wide + (pltpu.roll(rows, 81 * third, 1) if third else rows)
-    packed = jnp.concatenate([wide[:, :128], wide[:, 128:]], axis=0)
+    turned, more = window_rows(phase, c, 2)
+    for half in range(2):
+        terms[half].append(jnp.where(c == half, turned, 0.0))
+        extra[half].append(jnp.where(c == half, more, 0.0))
+    sums = []
+    for half in range(2):
+        high, low = split(jnp.concatenate(terms[half], axis=0))
+        table_hi, table_lo = steps[half, 0], steps[half, 1]
+        total = dot(high, table_hi) + dot(low, table_hi) + dot(high, table_lo)
+        sums.append(total + jnp.concatenate(extra[half], axis=0))
+    lane = lax.broadcasted_iota(jnp.int32, sums[0].shape, 1)
+    both = sums[0] + jnp.where(lane < 64, sums[1], -sums[1])
+    apart = jnp.where(lane < 64, sums[0], pltpu.roll(sums[1], 64, 1))
+    both = jnp.where(d == 0, apart, both)
+    rows = jnp.concatenate([both[16 * k : 16 * k + WIN] for k in range(4)], axis=0)
+    packed = rows[:GROUP]
+    for group in range(1, GROUP):
+        packed = packed + pltpu.roll(rows[GROUP * group : GROUP * (group + 1)], WIN * group, 1)
+    packed = jnp.concatenate([packed, jnp.zeros((2, 128), F32)], axis=0)
     out[...] = jnp.broadcast_to(packed[None], out.shape)
 
 
-def unpack(packed):
-    wide = jnp.concatenate([packed[:12], packed[12:]], axis=1)
-    lane = lax.broadcasted_iota(jnp.int32, (12, 128), 1)
-    thirds = []
-    for third in range(3):
-        rows = pltpu.roll(wide, 256 - 81 * third, 1) if third else wide
-        thirds.append(jnp.where(lane < WIN * WIN, rows[:, :128], 0.0))
-    return [jnp.concatenate([t[3 * k : 3 * k + 3] for t in thirds], axis=0) for k in range(4)]
-
-
-def energy_kernel(where, got, offsets, windows, terms):
-    left = got[0]
-    right = got[SUBS]
-    for k in range(1, SUBS):
-        left = left + got[k]
-        right = right + got[SUBS + k]
-    left, right = unpack(left), unpack(right)
-    blocks = [left[0], right[0], left[3] + right[3], left[1], left[2], right[1], right[2]]
-    step_z = (lax.broadcasted_iota(jnp.int32, (WIN, 128), 0) - REACH).astype(F32)
-    sums, sums_z = [], []
-    for block in blocks:
-        square = block * block
-        sums.append(jnp.sum(square, axis=0, keepdims=True))
-        sums_z.append(jnp.sum(square * step_z, axis=0, keepdims=True))
-    zero = jnp.zeros((1, 128), F32)
-    sums = jnp.concatenate(sums + [zero], axis=0)
-    sums_z = jnp.concatenate(sums_z + [zero], axis=0)
+def energy_kernel(where, got, offsets, turns, places, windows, terms):
+    sums = [[None] * WIN, [None] * WIN]
+    for sub in range(SUBS):
+        turn = turns[sub]
+        for core in range(2):
+            value = got[SUBS * core + sub]
+            for step in range(WIN):
+                term = value * turn[step : step + 1]
+                sums[core][step] = term if sub == 0 else sums[core][step] + term
+    sums = [[value + pltpu.roll(value, 64, 1) for value in side] for side in sums]
+    seam = [left + right for left, right in zip(*sums)]
+    totals = []
+    for side in (sums[0], sums[1], seam):
+        squares = [value * value for value in side]
+        total = squares[0]
+        for value in squares[1:]:
+            total = total + value
+        across = squares[0] * float(-REACH)
+        for step in range(1, WIN):
+            across = across + squares[step] * float(step - REACH)
+        totals.append((total, across))
+    slots = ((0, 0), (1, 0), (2, 3), (0, 1), (0, 2), (1, 1), (1, 2))
+
+    def stacked(kind, which):
+        rows = [
+            jnp.sum(totals[side][which] * places[kind, pair], axis=0, keepdims=True)
+            for side, pair in slots
+        ]
+        rows = jnp.concatenate(rows + [jnp.zeros((1, 128), F32)], axis=0)
+        return jnp.sum(rows, axis=1, keepdims=True)
+
+    energy = stacked(0, 0)
+    moments = [stacked(1, 0), stacked(0, 1), stacked(2, 0)]
     lane = lax.broadcasted_iota(jnp.int32, (8, 128), 1)
-    step_y = (lane // WIN - REACH).astype(F32)
-    step_x = (lane % WIN - REACH).astype(F32)
-    energy = jnp.sum(sums, axis=1, keepdims=True)
-    moments = [sums_z, sums * step_y, sums * step_x]
-    moments = [jnp.sum(m, axis=1, keepdims=True) for m in moments]
     mixed = jnp.where(lane == 1, moments[0], jnp.where(lane == 2, moments[1], moments[2]))
     place = offsets[...] + mixed / (energy + EPSILON)
     value = jnp.where(lane == 0, energy, energy * place)
     value = jnp.where(lane < 4, value, 0.0)
     terms[...] = jnp.broadcast_to(value[None], terms.shape)
     is_left = where[1] == 0
-    mine = [
-        jnp.where(is_left, blocks[0], blocks[1]),
-        blocks[2],
-        jnp.where(is_left, blocks[3], blocks[5]),
-        jnp.where(is_left, blocks[4], blocks[6]),
-    ]
-    for k in range(4):
-        windows[k, :WIN, :] = mine[k]
-        windows[k, WIN:, :] = jnp.zeros((16 - WIN, 128), F32)
+    at_seam = places[0, 3] > 0.0
+    for step in range(WIN):
+        mine = jnp.where(is_left, sums[0][step], sums[1][step])
+        windows[step] = jnp.where(at_seam, seam[step], mine)
+
+
+def unpack(packed):
+    lane = lax.broadcasted_iota(jnp.int32, (8, 128), 1)
+    values = [packed[step] for step in range(WIN)]
+    groups = []
+    for group in range(GROUP):
+        inside = (lane >= WIN * group) & (lane < WIN * (group + 1))
+        rows = jnp.zeros((8, 128), F32)
+        for step in range(WIN):
+            moved = WIN * (step - group) % 128
+            value = jnp.where(inside, values[step], 0.0)
+            rows = rows + (pltpu.roll(value, moved, 1) if moved else value)
+        groups.append(rows[:GROUP])
+    rows = jnp.concatenate(groups, axis=0)
+    return [rows[WIN * pair : WIN * (pair + 1)] for pair in range(4)]
 
 
 def graph_kernel(terms, graph, ignored, matrix, rhs):
@@ -453,11 +496,11 @@
 
 
 def place_kernel(where, meta, mine, below, windows, done):
-    done[...] = mine[0, :8]
+    done[...] = mine[0]
     c = where[1]
     slot = lax.broadcasted_iota(jnp.int32, (6, 128), 0)
-    blocks = [mine[k] for k in range(4)] + [below[k] for k in range(2)]
-    places = [slot == meta[k, 3] for k in (c, 2, 3 + 2 * c, 4 + 2 * c, 7, 8)]
+    blocks = unpack(mine) + unpack(below)[1:3]
+    places = [slot == meta[k, 3] for k in (c, 3 + 2 * c, 4 + 2 * c, 2, 7, 8)]
     for step in range(WIN):
         rows = jnp.zeros((6, 128), F32)
         for block, place in zip(blocks, places):
@@ -473,29 +516,32 @@
         out_shape=shapes,
         in_specs=specs,
         out_specs=outs,
-        compiler_params=pltpu.CompilerParams(vmem_limit_bytes=40 * 1024 * 1024),
+        compiler_params=pltpu.CompilerParams(vmem_limit_bytes=16 * 1024 * 1024),
         **params,
     )(*operands)
 
 
 def local(strips, pair_tiles, pair_owner, pair_offset):
     where = jnp.stack([lax.axis_index(name) for name in ("z", "core", "sub")]).astype(jnp.int32)
-    core = where[1]
     tables = plane_dft_tables()
     depth = lane_tiles(np.concatenate(split_np(depth_table()), axis=0))
     vhi, vlo = split_np(window_table())
-    planes = np.stack(split_np(plane_table()), axis=1)
     vmem, smem = pltpu.VMEM, pltpu.SMEM
 
     tiles = strips.reshape(8, LOCAL * ACROSS, ALONG)
     bottoms = jnp.stack([tiles[3], tiles[7]])
     from_above = lax.ppermute(bottoms, "z", [(k, k + 1) for k in range(PLANES - 1)])
-    core_after, bottoms = lax.optimization_barrier((core, bottoms))
-    own = lax.dynamic_index_in_dim(tiles, 5 - 5 * core_after, 0, keepdims=False)
+    core, bottoms = lax.optimization_barrier((where[1], bottoms))
+    own = lax.dynamic_index_in_dim(tiles, 5 - 5 * core, 0, keepdims=False)
     other = lax.ppermute(own, "core", [(0, 1), (1, 0)])
 
-    chunks = jax.ShapeDtypeStruct((SUBS, 16 * SLOTS, 2 * HALF), BF)
-    here = call(local_kernel, chunks, (tiles, tables), (vmem, vmem))
+    chunks = jax.ShapeDtypeStruct((SUBS, 112, 2 * HALF), BF)
+    here = call(
+        local_kernel,
+        chunks,
+        (where, tiles, own, other, tables),
+        (smem,) + (vmem,) * 4,
+    )
     facts, offsets = call(
         facts_kernel,
         (jax.ShapeDtypeStruct((16, 128), jnp.int32), jax.ShapeDtypeStruct((8, 128), F32)),
@@ -505,26 +551,25 @@
     sent = call(
         remote_kernel,
         chunks,
-        (where, here, from_above, own, other, tables, offsets),
-        (smem, vmem, vmem, vmem, vmem, vmem, pl.ANY),
-        input_output_aliases={1: 0},
+        (here, from_above, tables, offsets),
+        (vmem,) * 3 + (pl.ANY,),
+        scratch_shapes=[pltpu.SemaphoreType.DMA((2,))],
     )
     got = lax.all_to_all(sent, "sub", split_axis=0, concat_axis=0, tiled=True)
     partial = call(
         window_kernel,
-        jax.ShapeDtypeStruct((2 * SUBS, 24, 128), F32),
-        (where, facts, circle_table(), got, depth, vhi, vlo, planes, shift_table()),
-        (smem,) * 3 + (vmem,) * 4 + (pltpu.HBM, vmem),
-        scratch_shapes=[pltpu.VMEM((2, 4 * HALF, 128), BF), pltpu.SemaphoreType.DMA],
+        jax.ShapeDtypeStruct((2 * SUBS, 8, 128), F32),
+        (where, facts, circle_table(), got, depth, vhi, vlo, step_table(), shift_table()),
+        (smem,) * 3 + (vmem,) * 6,
     )
     shares = lax.all_to_all(partial, ("core", "sub"), split_axis=0, concat_axis=0, tiled=True)
     mine, terms = call(
         energy_kernel,
-        (jax.ShapeDtypeStruct((4, 16, 128), F32), jax.ShapeDtypeStruct((PLANES, 8, 128), F32)),
-        (where, shares, offsets),
-        (smem, vmem, vmem),
-    )
-    below = lax.ppermute(mine[2:], "z", [(k + 1, k) for k in range(PLANES - 1)])
+        (jax.ShapeDtypeStruct((WIN, 8, 128), F32), jax.ShapeDtypeStruct((PLANES, 8, 128), F32)),
+        (where, shares, offsets, turn_table(), place_table()),
+        (smem, vmem, vmem, vmem, vmem),
+    )
+    below = lax.ppermute(mine, "z", [(k + 1, k) for k in range(PLANES - 1)])
     all_terms = lax.all_to_all(terms, "z", split_axis=0, concat_axis=0, tiled=True)
     windows, done = call(
         place_kernel,

time: 85.5 us -> 82.8 us (0.968)
  blocking collectives: 32.9 us -> 31 us
  local copies, waits for them, and re-layouts: 4.66 us -> 3.52 us
    all_to_all x1, blocking collectives: 13.9 us -> 12 us  [local(): lax.all_to_all(partial, ('core', 'sub'), split_axis=0, concat_axis=0, til...]
    unnamed x26 -> x30, local copies, waits for them, and re-layouts: 2.73 us -> 1.53 us
    all_to_all x1, waiting for transfers between devices: 5.41 us -> 4.53 us  [local(): lax.all_to_all(terms, 'z', split_axis=0, concat_axis=0, tiled=True)]
    ppermute x1, waiting for transfers between devices: 0.01 us -> 0.88 us  [local(): other = lax.ppermute(own, 'core', [(0, 1), (1, 0)])]
  transfers between devices with their start and end apart: 4 -> 4, of which waited for: 2 -> 3; matrix products, arithmetic and copies ran while one was open for 1% -> 1% of each run, Pallas kernels for 4% -> 6%
where the time goes in v3:
time: 82.8 us; the launch traced here: 82.3 us
  blocking collectives  31 us (37%)
  starting transfers between devices  25.4 us (31%)
  Pallas kernels  11.8 us (14%)
  waiting for transfers between devices  9.64 us (12%)
  local copies, waits for them, and re-layouts  3.52 us (4%)
  between operations  0.85 us (1%)
    all_to_all x1, blocking collectives, local(): got = lax.all_to_all(sent, 'sub', split_axis=0, concat_axis=0, tiled=True)  19 us
    all_to_all x1, starting transfers between devices, local(): lax.all_to_all(terms, 'z', split_axis=0, concat_axis=0, tiled=True)  14 us
    all_to_all x1, blocking collectives, local(): lax.all_to_all(partial, ('core', 'sub'), split_axis=0, concat_axis=0, til...  12 us
    pallas_call x7, Pallas kernels, call(): pl.pallas_call(kernel, out_shape=shapes, in_specs=specs, out_specs=outs,...  11.8 us
    ppermute x1, starting transfers between devices, local(): other = lax.ppermute(own, 'core', [(0, 1), (1, 0)])  5.71 us
    all_to_all x1, waiting for transfers between devices, local(): lax.all_to_all(terms, 'z', split_axis=0, concat_axis=0, tiled=True)  4.53 us
    ppermute x1, starting transfers between devices, local(): lax.ppermute(bottoms, 'z', [(k, k + 1) for k in range(PLANES - 1)])  4.39 us
    ppermute x1, waiting for transfers between devices, local(): below = lax.ppermute(mine, 'z', [(k + 1, k) for k in range(PLANES - 1)])  4.22 us
  transfers between devices with their start and end apart: 4, of which 3 were waited for; matrix products, arithmetic and copies ran while one was open for 1% of the time, Pallas kernels for 6%

profile of v3, /device:TPU:1, one launch (start us, length us, event | category | flops | bytes accessed | tf_op | source)
XLA Modules:
  0.0 82.3 jit_solution(6505522853051806376)
XLA Ops:
  0.6 0.0 copy-start.2
  0.6 1.1 %fusion = (bf16[1,256,256]{2,1,0:T(8,128)(2,1)S(1)}, bf16[1,256,256]{2,1,0:T(8,128)(2,1)S(1)}) fusion(bf16[8,256,256]{2,1,0:T(8,128)(2,1)} %bitcast.10), kind=kLoop, calls=%fused_computation.3 | loop fusion | bytes 524288 | tf_op jit(solution)/shard_map/slice | solution.py:532
  1.8 4.4 %collective-permute-start.1 = (bf16[2,256,256]{2,1,0:T(8,128)(2,1)S(1)}, bf16[2,256,256]{2,1,0:T(8,128)(2,1)S(1)}, u32[]{:S(2)}, u32[]{:S(2)}) collective-permute-start(bf16[2,256,256]{2,1,0:T(8,128)(2,1)S(1)} %pad_maximum_fusion), channel_id=1, source_target_pairs={{0,32},{32,64},{64,96},{96,128},{128,160},{160,192},{192,224},{224... | collective-permute-start | bytes 786440 | tf_op jit(solution)/shard_map/ppermute | solution.py:533
  6.2 0.9 %dynamic-slice_bitcast_fusion.own = bf16[256,256]{1,0:T(8,128)(2,1)S(1)} fusion(bf16[8,256,256]{2,1,0:T(8,128)(2,1)} %bitcast.11, s32[]{:T(128)S(6)} %select_n.4), kind=kLoop, calls=%fused_computation.1 | loop fusion | bytes 262148 | tf_op jit(solution)/shard_map/jit(dynamic_index_in_dim)/squeeze | solution.py:535
  7.1 5.7 %collective-permute-start = (bf16[256,256]{1,0:T(8,128)(2,1)S(1)}, bf16[256,256]{1,0:T(8,128)(2,1)S(1)}, u32[]{:S(2)}, u32[]{:S(2)}) collective-permute-start(bf16[256,256]{1,0:T(8,128)(2,1)S(1)} %dynamic-slice_bitcast_fusion.own), channel_id=1, source_target_pairs={{0,16},{16,0},{1,17},{17,1},{2,18},{18,2},{3,19},{19,3},{4,20},{20... | collective-permute-start | bytes 393224 | tf_op jit(solution)/shard_map/ppermute | solution.py:536
  12.8 0.1 pad_add_fusion.where
  12.9 0.9 %collective-permute-done.other = bf16[256,256]{1,0:T(8,128)(2,1)S(1)} collective-permute-done((bf16[256,256]{1,0:T(8,128)(2,1)S(1)}, bf16[256,256]{1,0:T(8,128)(2,1)S(1)}, u32[]{:S(2)}, u32[]{:S(2)}) %collective-permute-start) | collective-permute-done | bytes 131104 | tf_op jit(solution)/shard_map/ppermute | solution.py:536
  13.8 1.5 %copy-done = bf16[2,3328,128]{2,1,0:T(8,128)(2,1)S(1)} copy-done((bf16[2,3328,128]{2,1,0:T(8,128)(2,1)S(1)}, bf16[2,3328,128]{2,1,0:T(8,128)(2,1)}, u32[]{:S(2)}) %copy-start) | copy-done | bytes 1703960
  15.2 2.6 %shard_map.157.ignored.here = bf16[16,112,256]{2,1,0:T(8,128)(2,1)S(1)} custom-call(s32[3]{0:T(128)S(1)} %pad_add_fusion.where, bf16[8,256,256]{2,1,0:T(8,128)(2,1)S(1)} %bitcast.12, bf16[256,256]{1,0:T(8,128)(2,1)S(1)} %dynamic-slice_bitcast_fusion.own, bf16[256,256]{1,0:T(8,128)(2,1)S(1)} %collective-permute-done.other, bf16[2,3328,128]{2,1,0:T(8,128)(2,1)S(1)} %copy-done), custom_call_target="tpu_custom_call" | custom-call | tf_op jit(solution)/shard_map/pallas_call | solution.py:514
  17.8 0.7 shard_map.158
  18.6 1.3 %shard_map.159 = bf16[16,112,256]{2,1,0:T(8,128)(2,1)S(1)} custom-call(bf16[16,112,256]{2,1,0:T(8,128)(2,1)S(1)} %shard_map.157.ignored.here, bf16[2,256,256]{2,1,0:T(8,128)(2,1)S(1)} %collective-permute-done.1.below, bf16[2,3328,128]{2,1,0:T(8,128)(2,1)S(1)} %copy-done.1, f32[8,128]{1,0:T(8,128)S(1)} %get-tuple-element.14.ignored.offsets), custom_call_target="tpu_custom_call" | custom-call | tf_op jit(solution)/shard_map/pallas_call | solution.py:514
  19.9 0.0 copy-start.3
  19.9 0.0 copy-start.4
  19.9 0.0 copy-start.6
  20.0 19.0 %all_to_all.15.got = bf16[16,112,256]{2,1,0:T(8,128)(2,1)S(1)} all-to-all(bf16[16,112,256]{2,1,0:T(8,128)(2,1)S(1)} %shard_map.159), channel_id=1, replica_groups=mesh['z'=16,'core'=2,'sub'=16] {'sub'}, dimensions={0} | all-to-all | bytes 1835008 | tf_op jit(solution)/shard_map/all_to_all | solution.py:558
  39.0 3.3 %shard_map.160 = f32[32,8,128]{2,1,0:T(8,128)S(1)} custom-call(s32[3]{0:T(128)S(1)} %pad_add_fusion.where, s32[16,128]{1,0:T(8,128)S(1)} %get-tuple-element.13.meta, f32[2,32]{1,0:T(2,128)S(1)} %copy-done.12, bf16[16,112,256]{2,1,0:T(8,128)(2,1)S(1)} %all_to_all.15.got, bf16[2,1024,128]{2,1,0:T(8,128)(2,1)S(1)} %copy-done.3, ...), custom_call_target="tpu_custom_call" | custom-call | tf_op jit(solution)/shard_map/pallas_call | solution.py:514
  42.3 12.0 %all_to_all.16.got = f32[32,8,128]{2,1,0:T(8,128)S(1)} all-to-all(f32[32,8,128]{2,1,0:T(8,128)S(1)} %shard_map.160), channel_id=1, replica_groups=mesh['z'=16,'core'=2,'sub'=16] {'core','sub'}, dimensions={0} | all-to-all | bytes 262144 | tf_op jit(solution)/shard_map/all_to_all | solution.py:565
  54.3 1.4 %shard_map.161 = (f32[9,8,128]{2,1,0:T(8,128)S(1)}, f32[16,8,128]{2,1,0:T(8,128)}) custom-call(s32[3]{0:T(128)S(1)} %pad_add_fusion.where, f32[32,8,128]{2,1,0:T(8,128)S(1)} %all_to_all.16.got, f32[8,128]{1,0:T(8,128)S(1)} %get-tuple-element.14.ignored.offsets, f32[16,16,128]{2,1,0:T(8,128)S(1)} %copy-done.7, f32[3,4,8,128]{3,2,1,0:T(8,128)S(1)} %copy-done.9), custom_call_target="tpu_custom_call" | custom-call | tf_op jit(solution)/shard_map/pallas_call | solution.py:514
  55.8 14.0 %all-to-all-start.2 = ((f32[16,8,128]{2,1,0:T(8,128)}), f32[16,8,128]{2,1,0:T(8,128)S(1)}, u32[]{:S(2)}, u32[]{:S(2)}) async-start(f32[16,8,128]{2,1,0:T(8,128)} %get-tuple-element.17), calls=%async_computation.2 | async-start | bytes 131072 | tf_op jit(solution)/shard_map/all_to_all | solution.py:573
  69.8 1.3 %collective-permute-start.2 = (f32[9,8,128]{2,1,0:T(8,128)S(1)}, f32[9,8,128]{2,1,0:T(8,128)S(1)}, u32[]{:S(2)}, u32[]{:S(2)}) collective-permute-start(f32[9,8,128]{2,1,0:T(8,128)S(1)} %get-tuple-element.15.mine), channel_id=1, source_target_pairs={{32,0},{64,32},{96,64},{128,96},{160,128},{192,160},{224,192},{256... | collective-permute-start | bytes 110600 | tf_op jit(solution)/shard_map/ppermute | solution.py:572
  71.1 4.2 %collective-permute-done.2.below = f32[9,8,128]{2,1,0:T(8,128)S(1)} collective-permute-done((f32[9,8,128]{2,1,0:T(8,128)S(1)}, f32[9,8,128]{2,1,0:T(8,128)S(1)}, u32[]{:S(2)}, u32[]{:S(2)}) %collective-permute-start.2) | collective-permute-done | bytes 36896 | tf_op jit(solution)/shard_map/ppermute | solution.py:572
  75.3 1.5 %shard_map.162 = (f32[6,729]{1,0:T(8,128)}, f32[8,128]{1,0:T(8,128)S(1)}) custom-call(s32[3]{0:T(128)S(1)} %pad_add_fusion.where, s32[16,128]{1,0:T(8,128)S(1)} %get-tuple-element.13.meta, f32[9,8,128]{2,1,0:T(8,128)S(1)} %get-tuple-element.15.mine, f32[9,8,128]{2,1,0:T(8,128)S(1)} %collective-permute-done.2.below), custom_call_target="tpu_custom_call" | custom-call | tf_op jit(solution)/shard_map/pallas_call | solution.py:514
  76.8 4.5 %all-to-all-done.2.terms = f32[16,8,128]{2,1,0:T(8,128)S(1)} async-done(((f32[16,8,128]{2,1,0:T(8,128)}), f32[16,8,128]{2,1,0:T(8,128)S(1)}, u32[]{:S(2)}, u32[]{:S(2)}) %all-to-all-start.2) | async-done | bytes 65568 | tf_op jit(solution)/shard_map/all_to_all | solution.py:573
  81.4 0.9 %shard_map.163 = (f32[64,64]{1,0:T(8,128)}, f32[3,64]{1,0:T(4,128)}) custom-call(f32[16,8,128]{2,1,0:T(8,128)S(1)} %all-to-all-done.2.terms, f32[128,64]{1,0:T(8,128)S(1)} %copy-done.8, f32[8,128]{1,0:T(8,128)S(1)} %get-tuple-element.18.ignored), custom_call_target="tpu_custom_call" | custom-call | tf_op jit(solution)/shard_map/pallas_call | solution.py:514
  (27 shorter events, 0.1 us)
Async XLA Ops:
  0.6 13.1 %copy-start.2 = (bf16[2,4,8,32,256]{4,3,2,1,0:T(8,128)(2,1)S(1)}, bf16[2,4,8,32,256]{4,3,2,1,0:T(8,128)(2,1)}, u32[]{:S(2)}) copy-start(bf16[2,4,8,32,256]{4,3,2,1,0:T(8,128)(2,1)} %param.14) | copy-start | bytes 3145732
  1.8 16.8 %collective-permute-start.1 = (bf16[2,256,256]{2,1,0:T(8,128)(2,1)S(1)}, bf16[2,256,256]{2,1,0:T(8,128)(2,1)S(1)}, u32[]{:S(2)}, u32[]{:S(2)}) collective-permute-start(bf16[2,256,256]{2,1,0:T(8,128)(2,1)S(1)} %pad_maximum_fusion), channel_id=1, source_target_pairs={{0,32},{32,64},{64,96},{96,128},{128,160},{160,192},{192,224},{224... | collective-permute-start | bytes 786440 | tf_op jit(solution)/shard_map/ppermute | solution.py:533
  7.1 6.7 %collective-permute-start = (bf16[256,256]{1,0:T(8,128)(2,1)S(1)}, bf16[256,256]{1,0:T(8,128)(2,1)S(1)}, u32[]{:S(2)}, u32[]{:S(2)}) collective-permute-start(bf16[256,256]{1,0:T(8,128)(2,1)S(1)} %dynamic-slice_bitcast_fusion.own), channel_id=1, source_target_pairs={{0,16},{16,0},{1,17},{17,1},{2,18},{18,2},{3,19},{19,3},{4,20},{20... | collective-permute-start | bytes 393224 | tf_op jit(solution)/shard_map/ppermute | solution.py:536
  13.8 1.5 %copy-start = (bf16[2,3328,128]{2,1,0:T(8,128)(2,1)S(1)}, bf16[2,3328,128]{2,1,0:T(8,128)(2,1)}, u32[]{:S(2)}) copy-start(bf16[2,3328,128]{2,1,0:T(8,128)(2,1)} %constant.42.clone.tables) | copy-start | bytes 5111812
  15.2 2.6 %copy-start.11 = (s32[108,3]{0,1:T(4,128)S(1)}, s32[108,3]{0,1:T(4,128)}, u32[]{:S(2)}) copy-start(s32[108,3]{0,1:T(4,128)} %param.17) | copy-start | bytes 3892
  15.2 2.6 %copy-start.13 = (s32[108,2]{0,1:T(2,128)S(1)}, s32[108,2]{0,1:T(2,128)}, u32[]{:S(2)}) copy-start(s32[108,2]{0,1:T(2,128)} %param.15) | copy-start | bytes 2596
  15.2 2.6 %copy-start.14 = (s32[108]{0:T(128)S(1)}, s32[108]{0:T(128)}, u32[]{:S(2)}) copy-start(s32[108]{0:T(128)} %param.16) | copy-start | bytes 1300
  15.2 3.4 %copy-start.1 = (bf16[2,3328,128]{2,1,0:T(8,128)(2,1)S(1)}, bf16[2,3328,128]{2,1,0:T(8,128)(2,1)}, u32[]{:S(2)}) copy-start(bf16[2,3328,128]{2,1,0:T(8,128)(2,1)} %constant.42.clone.tables) | copy-start | bytes 5111812
  19.9 19.1 %copy-start.3 = (bf16[2,1024,128]{2,1,0:T(8,128)(2,1)S(1)}, bf16[2,1024,128]{2,1,0:T(8,128)(2,1)}, u32[]{:S(2)}) copy-start(bf16[2,1024,128]{2,1,0:T(8,128)(2,1)} %constant.44.clone.depth) | copy-start | bytes 1572868
  19.9 19.1 %copy-start.4 = (bf16[11,96,128]{2,1,0:T(8,128)(2,1)S(1)}, bf16[11,96,128]{2,1,0:T(8,128)(2,1)}, u32[]{:S(2)}) copy-start(bf16[11,96,128]{2,1,0:T(8,128)(2,1)} %constant.45.clone.vhi) | copy-start | bytes 811012
  19.9 19.1 %copy-start.5 = (bf16[11,96,128]{2,1,0:T(8,128)(2,1)S(1)}, bf16[11,96,128]{2,1,0:T(8,128)(2,1)}, u32[]{:S(2)}) copy-start(bf16[11,96,128]{2,1,0:T(8,128)(2,1)} %constant.46.clone.vlo) | copy-start | bytes 811012
  19.9 19.1 %copy-start.6 = (bf16[2,2,256,128]{3,2,1,0:T(8,128)(2,1)S(1)}, bf16[2,2,256,128]{3,2,1,0:T(8,128)(2,1)}, u32[]{:S(2)}) copy-start(bf16[2,2,256,128]{3,2,1,0:T(8,128)(2,1)} %constant.47.clone.steps) | copy-start | bytes 786436
  19.9 19.1 %copy-start.10 = (f32[4,16,128]{2,1,0:T(8,128)S(1)}, f32[4,16,128]{2,1,0:T(8,128)}, u32[]{:S(2)}) copy-start(f32[4,16,128]{2,1,0:T(8,128)} %constant.48.clone.shift) | copy-start | bytes 98308
  20.0 19.1 %copy-start.12 = (f32[2,32]{1,0:T(2,128)S(1)}, f32[2,32]{1,0:T(2,128)}, u32[]{:S(2)}) copy-start(f32[2,32]{1,0:T(2,128)} %constant.43.clone.circle) | copy-start | bytes 772
  39.0 15.4 %copy-start.7 = (f32[16,16,128]{2,1,0:T(8,128)S(1)}, f32[16,16,128]{2,1,0:T(8,128)}, u32[]{:S(2)}) copy-start(f32[16,16,128]{2,1,0:T(8,128)} %constant.49.clone.turns) | copy-start | bytes 393220
  39.0 15.4 %copy-start.9 = (f32[3,4,8,128]{3,2,1,0:T(8,128)S(1)}, f32[3,4,8,128]{3,2,1,0:T(8,128)}, u32[]{:S(2)}) copy-start(f32[3,4,8,128]{3,2,1,0:T(8,128)} %constant.50.clone.places) | copy-start | bytes 147460
  39.0 42.4 %copy-start.8 = (f32[128,64]{1,0:T(8,128)S(1)}, f32[128,64]{1,0:T(8,128)}, u32[]{:S(2)}) copy-start(f32[128,64]{1,0:T(8,128)} %constant.51.clone.graph) | copy-start | bytes 98308
  55.8 25.6 %all-to-all-start.2 = ((f32[16,8,128]{2,1,0:T(8,128)}), f32[16,8,128]{2,1,0:T(8,128)S(1)}, u32[]{:S(2)}, u32[]{:S(2)}) async-start(f32[16,8,128]{2,1,0:T(8,128)} %get-tuple-element.17), calls=%async_computation.2 | async-start | bytes 131072 | tf_op jit(solution)/shard_map/all_to_all | solution.py:573
  69.8 5.5 %collective-permute-start.2 = (f32[9,8,128]{2,1,0:T(8,128)S(1)}, f32[9,8,128]{2,1,0:T(8,128)S(1)}, u32[]{:S(2)}, u32[]{:S(2)}) collective-permute-start(f32[9,8,128]{2,1,0:T(8,128)S(1)} %get-tuple-element.15.mine), channel_id=1, source_target_pairs={{32,0},{64,32},{96,64},{128,96},{160,128},{192,160},{224,192},{256... | collective-permute-start | bytes 110600 | tf_op jit(solution)/shard_map/ppermute | solution.py:572

commit v4 on v3

--- a/solution.py
+++ b/solution.py
@@ -105,12 +105,17 @@
 
 
 def depth_table():
-    theta = angles(np.arange(DEPTH), np.arange(DEPTH), DEPTH).reshape(DEPTH, SUBS, LOCAL)
-    table = np.zeros((2, 2, DEPTH, SUBS, 2, LOCAL))
-    for half in range(2):
-        table[0, half, :, :, half, :] = np.cos(theta)
-        table[1, half, :, :, half, :] = np.sin(theta)
-    return table.reshape(4 * DEPTH, 2 * DEPTH)
+    theta = angles(np.arange(64), np.arange(DEPTH), DEPTH)
+    cos, sin = np.cos(theta), np.sin(theta)
+    sin[0] = np.where(np.arange(DEPTH) % 2 == 0, 1.0, -1.0)
+    table = np.zeros((2, 2, 64, SUBS, 2, LOCAL))
+    for half in range(2):
+        table[0, half, :, :, half, :] = cos.reshape(64, SUBS, LOCAL)
+        table[1, half, :, :, half, :] = sin.reshape(64, SUBS, LOCAL)
+    return table.reshape(4 * 64, 2 * DEPTH)
+
+
+ORDER = np.concatenate([np.arange(65), np.arange(127, 64, -1)])
 
 
 def window_table():
@@ -128,7 +133,7 @@
         table[index, 3, :WIN] = sin * low
         table[index, 4, :WIN] = cos * high
         table[index, 5, :WIN] = edge - sin * high
-    return table.reshape(OFFS, 96, DEPTH)
+    return table.reshape(OFFS, 96, DEPTH)[:, :, ORDER]
 
 
 def step_table():
@@ -255,8 +260,26 @@
     return offset, jnp.where(held > 0, ordinal, -1)
 
 
-def facts_kernel(where, pair_tiles, owner, pair_offset, ignored, facts, offsets):
-    del ignored
+def chunk(pieces):
+    return jnp.concatenate(pieces, axis=1).astype(BF)
+
+
+def local_kernel(strips, tables, out):
+    chosen = (1, 4, 2, 6)
+    parts = []
+    for half in range(2):
+        stack = [across_dft(strips[k], half, tables) for k in chosen]
+        parts.append(along_dft(jnp.concatenate(stack, axis=0), half, tables, 4))
+    for k in range(4):
+        out[:, 16 * k : 16 * k + 16, :] = chunk([parts[0][k], parts[1][k]])
+
+
+def remote_kernel(
+    where, here, below, own, other, tables, pair_tiles, owner, pair_offset,
+    out, facts, offsets, moved,
+):
+    kept = pltpu.make_async_copy(here, out.at[:, pl.ds(0, 64), :], moved)
+    kept.start()
     offset, slot = pair_facts(where, pair_tiles, owner, pair_offset)
     lane = lax.broadcasted_iota(jnp.int32, (16, 128), 1)
     facts[...] = jnp.where(
@@ -266,58 +289,35 @@
     offsets[...] = jnp.where(
         lane == 1, offset[0][:8], jnp.where(lane == 2, offset[1][:8], offset[2][:8])
     ).astype(F32)
-
-
-def chunk(pieces):
-    return jnp.concatenate(pieces, axis=1).astype(BF)
-
-
-def local_kernel(where, strips, own, other, tables, out):
-    chosen = (1, 4, 2, 6)
     parts = []
     for half in range(2):
-        stack = [across_dft(strips[k], half, tables) for k in chosen]
-        parts.append(along_dft(jnp.concatenate(stack, axis=0), half, tables, 4))
-    for k in range(4):
-        out[:, 16 * k : 16 * k + 16, :] = chunk([parts[0][k], parts[1][k]])
+        stack = [across_dft(below[k], half, tables) for k in range(2)]
+        parts.append(along_dft(jnp.concatenate(stack, axis=0), half, tables, 2))
+    for k in range(2):
+        out[:, 64 + 16 * k : 80 + 16 * k, :] = chunk([parts[0][k], parts[1][k]])
     core = where[1]
     mine, theirs = own[...], other[...]
     first = jnp.where(core == 0, mine, theirs)
     second = jnp.where(core == 0, theirs, mine)
     stack = [across_dft(strip, core, tables) for strip in (first, second)]
     out[:, 96:112, :] = chunk(along_dft(jnp.concatenate(stack, axis=0), core, tables, 2))
-
-
-def remote_kernel(here, below, tables, ignored, out, moved):
-    del ignored
-    kept = ((pl.ds(0, 16), pl.ds(0, 64)), (pl.ds(0, 16), pl.ds(96, 16)))
-    copies = [
-        pltpu.make_async_copy(here.at[at + (slice(None),)], out.at[at + (slice(None),)], moved.at[k])
-        for k, at in enumerate(kept)
-    ]
-    for copy in copies:
-        copy.start()
-    parts = []
-    for half in range(2):
-        stack = [across_dft(below[k], half, tables) for k in range(2)]
-        parts.append(along_dft(jnp.concatenate(stack, axis=0), half, tables, 2))
-    for k in range(2):
-        out[:, 64 + 16 * k : 80 + 16 * k, :] = chunk([parts[0][k], parts[1][k]])
-    for copy in copies:
-        copy.wait()
-
-
-def spectrum_of(block, lanes, depth_hi, depth_lo):
+    kept.wait()
+
+
+def spectrum_of(block, zeroth, held, depth_hi, depth_lo):
     both = dot(depth_hi, block) + dot(depth_lo, block)
-    cos, sin = both[: 2 * DEPTH], both[2 * DEPTH :]
+    cos, sin = both[:DEPTH], both[DEPTH:]
     cos_re, cos_im = cos[:, :HALF], cos[:, HALF:]
     sin_re, sin_im = sin[:, :HALF], sin[:, HALF:]
-    real, imag = cos_re + sin_im, cos_im - sin_re
-    if lanes is not None:
-        low, high = lanes
-        real = jnp.where(low, cos_re, jnp.where(high, cos_im, real))
-        imag = jnp.where(low, -sin_re, jnp.where(high, -sin_im, imag))
-    return real, imag
+    low_re = jnp.where(zeroth | held, cos_re, cos_re + sin_im)
+    low_im = jnp.where(zeroth, cos_im, jnp.where(held, 0.0, cos_im) - sin_re)
+    high_re = jnp.where(zeroth, sin_re, jnp.where(held, cos_im, cos_re - sin_im))
+    high_im = jnp.where(zeroth, sin_im, jnp.where(held, sin_im, cos_im + sin_re))
+
+    def rows(low, high):
+        return jnp.concatenate([low[:64], high[:64], low[64:], high[64:]], axis=0)
+
+    return rows(low_re, high_re), rows(low_im, high_im)
 
 
 def phase_of(first, second, edge):
@@ -340,24 +340,26 @@
 
 def window_kernel(where, meta, circle, got, depth, vhi, vlo, steps, shift, out):
     c, d = where[1], where[2]
-    row = lax.broadcasted_iota(jnp.int32, (2 * DEPTH, HALF), 0)
-    lane = lax.broadcasted_iota(jnp.int32, (2 * DEPTH, HALF), 1)
-    freq = lax.rem(row, DEPTH)
+    row = lax.broadcasted_iota(jnp.int32, (DEPTH, HALF), 0)
+    lane = lax.broadcasted_iota(jnp.int32, (DEPTH, HALF), 1)
+    zeroth = lax.rem(row, 64) == 0
     nowhere = jnp.where(d == 0, 0, 2 * HALF)
 
     def special(half_of_row):
-        held = lane == half_of_row * (HALF - 1) + nowhere
-        low = held & (freq > 0) & (freq < 64)
-        high = held & (freq > 64)
-        edge = held & ((freq == 0) | (freq == 64))
-        return (low, high), edge
-
-    lanes, edge = special(row // DEPTH)
-    depth_hi, depth_lo = wide_rows(depth, 0, 512), wide_rows(depth, 512, 512)
-
-    def spectrum(slot, masks):
+        return (lane == half_of_row * (HALF - 1) + nowhere) & (lax.rem(row, 64) != 0)
+
+    def edges(count, half_of_row):
+        row = lax.broadcasted_iota(jnp.int32, (count, HALF), 0)
+        lane = lax.broadcasted_iota(jnp.int32, (count, HALF), 1)
+        return (lane == half_of_row(row) * (HALF - 1) + nowhere) & (lax.rem(row, 64) == 0)
+
+    held = special(row // 64)
+    edge = edges(2 * DEPTH, lambda row: row // DEPTH)
+    depth_hi, depth_lo = wide_rows(depth, 0, 256), wide_rows(depth, 256, 256)
+
+    def spectrum(slot, held):
         block = got[:, 16 * slot : 16 * slot + 16, :].reshape(2 * DEPTH, 2 * HALF)
-        return spectrum_of(block, masks, depth_hi, depth_lo)
+        return spectrum_of(block, zeroth, held, depth_hi, depth_lo)
 
     small_lane = lax.broadcasted_iota(jnp.int32, (16, HALF), 1)
 
@@ -385,17 +387,15 @@
 
     terms, extra = ([], []), ([], [])
     for first, second, slot in ((0, 1, c), (4, 2, 3 + 2 * c), (5, 3, 4 + 2 * c)):
-        real, imag = phase_of(spectrum(first, lanes), spectrum(second, lanes), edge)
+        real, imag = phase_of(spectrum(first, held), spectrum(second, held), edge)
         for half in range(2):
             rows = slice(DEPTH * half, DEPTH * (half + 1))
             turned, more = window_rows((real[rows], imag[rows]), half, slot)
             terms[half].append(turned)
             extra[half].append(more)
-    seam_lanes, seam_edge = special(c)
-    real, imag = spectrum(6, seam_lanes)
-    phase = phase_of(
-        (real[:DEPTH], imag[:DEPTH]), (real[DEPTH:], imag[DEPTH:]), seam_edge[:DEPTH]
-    )
+    real, imag = spectrum(6, special(c))
+    seam_edge = edges(DEPTH, lambda row: c)
+    phase = phase_of((real[:DEPTH], imag[:DEPTH]), (real[DEPTH:], imag[DEPTH:]), seam_edge)
     turned, more = window_rows(phase, c, 2)
     for half in range(2):
         terms[half].append(jnp.where(c == half, turned, 0.0))
@@ -535,25 +535,22 @@
     own = lax.dynamic_index_in_dim(tiles, 5 - 5 * core, 0, keepdims=False)
     other = lax.ppermute(own, "core", [(0, 1), (1, 0)])
 
-    chunks = jax.ShapeDtypeStruct((SUBS, 112, 2 * HALF), BF)
     here = call(
-        local_kernel,
-        chunks,
-        (where, tiles, own, other, tables),
-        (smem,) + (vmem,) * 4,
-    )
-    facts, offsets = call(
-        facts_kernel,
-        (jax.ShapeDtypeStruct((16, 128), jnp.int32), jax.ShapeDtypeStruct((8, 128), F32)),
-        (where, pair_tiles.T, pair_owner.reshape(1, -1), pair_offset.T, here),
-        (smem,) + (vmem,) * 3 + (pl.ANY,),
-    )
-    sent = call(
+        local_kernel, jax.ShapeDtypeStruct((SUBS, 64, 2 * HALF), BF), (tiles, tables), (vmem, vmem)
+    )
+    sent, facts, offsets = call(
         remote_kernel,
-        chunks,
-        (here, from_above, tables, offsets),
-        (vmem,) * 3 + (pl.ANY,),
-        scratch_shapes=[pltpu.SemaphoreType.DMA((2,))],
+        (
+            jax.ShapeDtypeStruct((SUBS, 112, 2 * HALF), BF),
+            jax.ShapeDtypeStruct((16, 128), jnp.int32),
+            jax.ShapeDtypeStruct((8, 128), F32),
+        ),
+        (
+            where, here, from_above, own, other, tables,
+            pair_tiles.T, pair_owner.reshape(1, -1), pair_offset.T,
+        ),
+        (smem,) + (vmem,) * 8,
+        scratch_shapes=[pltpu.SemaphoreType.DMA],
     )
     got = lax.all_to_all(sent, "sub", split_axis=0, concat_axis=0, tiled=True)
     partial = call(

time: 82.8 us -> 81.4 us (0.983)
  Pallas kernels: 11.8 us -> 10.5 us
  waiting for transfers between devices: 9.64 us -> 8.76 us
    pallas_call x7 -> x6, Pallas kernels: 11.8 us -> 10.5 us  [call(): pl.pallas_call(kernel, out_shape=shapes, in_specs=specs, out_specs=outs,...]
    ppermute x1, waiting for transfers between devices: 0.88 us -> 0.01 us  [local(): other = lax.ppermute(own, 'core', [(0, 1), (1, 0)])]
  transfers between devices with their start and end apart: 4 -> 4, of which waited for: 3 -> 2; matrix products, arithmetic and copies ran while one was open for 1% -> 1% of each run, Pallas kernels for 6% -> 4%
where the time goes in v4:
time: 81.4 us; the launch traced here: 80.8 us
  blocking collectives  31 us (38%)
  starting transfers between devices  26 us (32%)
  Pallas kernels  10.5 us (13%)
  waiting for transfers between devices  8.76 us (11%)
  local copies, waits for them, and re-layouts  3.53 us (4%)
  between operations  0.88 us (1%)
    all_to_all x1, blocking collectives, local(): got = lax.all_to_all(sent, 'sub', split_axis=0, concat_axis=0, tiled=True)  19.1 us
    all_to_all x1, starting transfers between devices, local(): lax.all_to_all(terms, 'z', split_axis=0, concat_axis=0, tiled=True)  14.5 us
    all_to_all x1, blocking collectives, local(): lax.all_to_all(partial, ('core', 'sub'), split_axis=0, concat_axis=0, til...  11.8 us
    pallas_call x6, Pallas kernels, call(): pl.pallas_call(kernel, out_shape=shapes, in_specs=specs, out_specs=outs,...  10.5 us
    ppermute x1, starting transfers between devices, local(): other = lax.ppermute(own, 'core', [(0, 1), (1, 0)])  5.84 us
    all_to_all x1, waiting for transfers between devices, local(): lax.all_to_all(terms, 'z', split_axis=0, concat_axis=0, tiled=True)  4.53 us
    ppermute x1, starting transfers between devices, local(): lax.ppermute(bottoms, 'z', [(k, k + 1) for k in range(PLANES - 1)])  4.39 us
    ppermute x1, waiting for transfers between devices, local(): below = lax.ppermute(mine, 'z', [(k + 1, k) for k in range(PLANES - 1)])  4.22 us
  transfers between devices with their start and end apart: 4, of which 2 were waited for; matrix products, arithmetic and copies ran while one was open for 1% of the time, Pallas kernels for 4%

profile of v4, /device:TPU:1, one launch (start us, length us, event | category | flops | bytes accessed | tf_op | source)
XLA Modules:
  0.0 80.8 jit_solution(10351198269951590352)
XLA Ops:
  0.6 0.0 copy-start.2
  0.6 1.1 %fusion = (bf16[1,256,256]{2,1,0:T(8,128)(2,1)S(1)}, bf16[1,256,256]{2,1,0:T(8,128)(2,1)S(1)}) fusion(bf16[8,256,256]{2,1,0:T(8,128)(2,1)} %bitcast.10), kind=kLoop, calls=%fused_computation.3 | loop fusion | bytes 524288 | tf_op jit(solution)/shard_map/slice | solution.py:532
  1.8 4.4 %collective-permute-start = (bf16[2,256,256]{2,1,0:T(8,128)(2,1)S(1)}, bf16[2,256,256]{2,1,0:T(8,128)(2,1)S(1)}, u32[]{:S(2)}, u32[]{:S(2)}) collective-permute-start(bf16[2,256,256]{2,1,0:T(8,128)(2,1)S(1)} %pad_maximum_fusion), channel_id=1, source_target_pairs={{0,32},{32,64},{64,96},{96,128},{128,160},{160,192},{192,224},{224... | collective-permute-start | bytes 786440 | tf_op jit(solution)/shard_map/ppermute | solution.py:533
  6.2 0.9 %dynamic-slice_bitcast_fusion.own = bf16[256,256]{1,0:T(8,128)(2,1)S(1)} fusion(bf16[8,256,256]{2,1,0:T(8,128)(2,1)} %bitcast.11, s32[]{:T(128)S(6)} %select_n.4), kind=kLoop, calls=%fused_computation.1 | loop fusion | bytes 262148 | tf_op jit(solution)/shard_map/jit(dynamic_index_in_dim)/squeeze | solution.py:535
  7.1 5.8 %collective-permute-start.1 = (bf16[256,256]{1,0:T(8,128)(2,1)S(1)}, bf16[256,256]{1,0:T(8,128)(2,1)S(1)}, u32[]{:S(2)}, u32[]{:S(2)}) collective-permute-start(bf16[256,256]{1,0:T(8,128)(2,1)S(1)} %dynamic-slice_bitcast_fusion.own), channel_id=1, source_target_pairs={{0,16},{16,0},{1,17},{17,1},{2,18},{18,2},{3,19},{19,3},{4,20},{20... | collective-permute-start | bytes 393224 | tf_op jit(solution)/shard_map/ppermute | solution.py:536
  13.0 0.0 copy-start
  13.0 1.4 %copy-done = bf16[2,3328,128]{2,1,0:T(8,128)(2,1)S(1)} copy-done((bf16[2,3328,128]{2,1,0:T(8,128)(2,1)S(1)}, bf16[2,3328,128]{2,1,0:T(8,128)(2,1)}, u32[]{:S(2)}) %copy-start) | copy-done | bytes 1703960
  14.4 1.6 %shard_map.157.here = bf16[16,64,256]{2,1,0:T(8,128)(2,1)S(1)} custom-call(bf16[8,256,256]{2,1,0:T(8,128)(2,1)S(1)} %bitcast.12, bf16[2,3328,128]{2,1,0:T(8,128)(2,1)S(1)} %copy-done), custom_call_target="tpu_custom_call" | custom-call | tf_op jit(solution)/shard_map/pallas_call | solution.py:514
  16.1 0.1 pad_add_fusion.where
  16.2 0.0 copy-start.4
  16.2 0.0 copy-start.5
  16.2 0.0 copy-start.6
  16.2 0.0 copy-start.10
  16.3 2.2 %shard_map.158 = (bf16[16,112,256]{2,1,0:T(8,128)(2,1)S(1)}, s32[16,128]{1,0:T(8,128)S(1)}, f32[8,128]{1,0:T(8,128)S(1)}) custom-call(s32[3]{0:T(128)S(1)} %pad_add_fusion.where, bf16[16,64,256]{2,1,0:T(8,128)(2,1)S(1)} %shard_map.157.here, bf16[2,256,256]{2,1,0:T(8,128)(2,1)S(1)} %collective-permute-done.below, ...), custom_call_target="tpu_custom_call" | custom-call | tf_op jit(solution)/shard_map/pallas_call | solution.py:514
  18.5 19.1 %all_to_all.15.got = bf16[16,112,256]{2,1,0:T(8,128)(2,1)S(1)} all-to-all(bf16[16,112,256]{2,1,0:T(8,128)(2,1)S(1)} %get-tuple-element.15), channel_id=1, replica_groups=mesh['z'=16,'core'=2,'sub'=16] {'sub'}, dimensions={0} | all-to-all | bytes 1835008 | tf_op jit(solution)/shard_map/all_to_all | solution.py:555
  37.7 2.8 %shard_map.159 = f32[32,8,128]{2,1,0:T(8,128)S(1)} custom-call(s32[3]{0:T(128)S(1)} %pad_add_fusion.where, s32[16,128]{1,0:T(8,128)S(1)} %get-tuple-element.14.meta, f32[2,32]{1,0:T(2,128)S(1)} %copy-done.13, bf16[16,112,256]{2,1,0:T(8,128)(2,1)S(1)} %all_to_all.15.got, bf16[2,512,128]{2,1,0:T(8,128)(2,1)S(1)} %copy-done.6, ...), custom_call_target="tpu_custom_call" | custom-call | tf_op jit(solution)/shard_map/pallas_call | solution.py:514
  40.5 11.8 %all_to_all.16.got = f32[32,8,128]{2,1,0:T(8,128)S(1)} all-to-all(f32[32,8,128]{2,1,0:T(8,128)S(1)} %shard_map.159), channel_id=1, replica_groups=mesh['z'=16,'core'=2,'sub'=16] {'core','sub'}, dimensions={0} | all-to-all | bytes 262144 | tf_op jit(solution)/shard_map/all_to_all | solution.py:562
  52.4 1.4 %shard_map.160 = (f32[9,8,128]{2,1,0:T(8,128)S(1)}, f32[16,8,128]{2,1,0:T(8,128)}) custom-call(s32[3]{0:T(128)S(1)} %pad_add_fusion.where, f32[32,8,128]{2,1,0:T(8,128)S(1)} %all_to_all.16.got, f32[8,128]{1,0:T(8,128)S(1)} %get-tuple-element.16.offsets, f32[16,16,128]{2,1,0:T(8,128)S(1)} %copy-done.7, f32[3,4,8,128]{3,2,1,0:T(8,128)S(1)} %copy-done.9), custom_call_target="tpu_custom_call" | custom-call | tf_op jit(solution)/shard_map/pallas_call | solution.py:514
  53.8 14.5 %all-to-all-start.2 = ((f32[16,8,128]{2,1,0:T(8,128)}), f32[16,8,128]{2,1,0:T(8,128)S(1)}, u32[]{:S(2)}, u32[]{:S(2)}) async-start(f32[16,8,128]{2,1,0:T(8,128)} %get-tuple-element.19), calls=%async_computation.2 | async-start | bytes 131072 | tf_op jit(solution)/shard_map/all_to_all | solution.py:570
  68.3 1.3 %collective-permute-start.2 = (f32[9,8,128]{2,1,0:T(8,128)S(1)}, f32[9,8,128]{2,1,0:T(8,128)S(1)}, u32[]{:S(2)}, u32[]{:S(2)}) collective-permute-start(f32[9,8,128]{2,1,0:T(8,128)S(1)} %get-tuple-element.17.mine), channel_id=1, source_target_pairs={{32,0},{64,32},{96,64},{128,96},{160,128},{192,160},{224,192},{256... | collective-permute-start | bytes 110600 | tf_op jit(solution)/shard_map/ppermute | solution.py:569
  69.6 4.2 %collective-permute-done.2.below = f32[9,8,128]{2,1,0:T(8,128)S(1)} collective-permute-done((f32[9,8,128]{2,1,0:T(8,128)S(1)}, f32[9,8,128]{2,1,0:T(8,128)S(1)}, u32[]{:S(2)}, u32[]{:S(2)}) %collective-permute-start.2) | collective-permute-done | bytes 36896 | tf_op jit(solution)/shard_map/ppermute | solution.py:569
  73.9 1.5 %shard_map.161 = (f32[6,729]{1,0:T(8,128)}, f32[8,128]{1,0:T(8,128)S(1)}) custom-call(s32[3]{0:T(128)S(1)} %pad_add_fusion.where, s32[16,128]{1,0:T(8,128)S(1)} %get-tuple-element.14.meta, f32[9,8,128]{2,1,0:T(8,128)S(1)} %get-tuple-element.17.mine, f32[9,8,128]{2,1,0:T(8,128)S(1)} %collective-permute-done.2.below), custom_call_target="tpu_custom_call" | custom-call | tf_op jit(solution)/shard_map/pallas_call | solution.py:514
  75.4 4.5 %all-to-all-done.2.terms = f32[16,8,128]{2,1,0:T(8,128)S(1)} async-done(((f32[16,8,128]{2,1,0:T(8,128)}), f32[16,8,128]{2,1,0:T(8,128)S(1)}, u32[]{:S(2)}, u32[]{:S(2)}) %all-to-all-start.2) | async-done | bytes 65568 | tf_op jit(solution)/shard_map/all_to_all | solution.py:570
  79.9 0.9 %shard_map.162 = (f32[64,64]{1,0:T(8,128)}, f32[3,64]{1,0:T(4,128)}) custom-call(f32[16,8,128]{2,1,0:T(8,128)S(1)} %all-to-all-done.2.terms, f32[128,64]{1,0:T(8,128)S(1)} %copy-done.8, f32[8,128]{1,0:T(8,128)S(1)} %get-tuple-element.20.ignored), custom_call_target="tpu_custom_call" | custom-call | tf_op jit(solution)/shard_map/pallas_call | solution.py:514
  (26 shorter events, 0.1 us)
Async XLA Ops:
  0.6 12.3 %copy-start.2 = (bf16[2,4,8,32,256]{4,3,2,1,0:T(8,128)(2,1)S(1)}, bf16[2,4,8,32,256]{4,3,2,1,0:T(8,128)(2,1)}, u32[]{:S(2)}) copy-start(bf16[2,4,8,32,256]{4,3,2,1,0:T(8,128)(2,1)} %param.14) | copy-start | bytes 3145732
  1.8 14.4 %collective-permute-start = (bf16[2,256,256]{2,1,0:T(8,128)(2,1)S(1)}, bf16[2,256,256]{2,1,0:T(8,128)(2,1)S(1)}, u32[]{:S(2)}, u32[]{:S(2)}) collective-permute-start(bf16[2,256,256]{2,1,0:T(8,128)(2,1)S(1)} %pad_maximum_fusion), channel_id=1, source_target_pairs={{0,32},{32,64},{64,96},{96,128},{128,160},{160,192},{192,224},{224... | collective-permute-start | bytes 786440 | tf_op jit(solution)/shard_map/ppermute | solution.py:533
  7.1 9.1 %copy-start.11 = (s32[108,3]{0,1:T(4,128)S(1)}, s32[108,3]{0,1:T(4,128)}, u32[]{:S(2)}) copy-start(s32[108,3]{0,1:T(4,128)} %param.17) | copy-start | bytes 3892
  7.1 9.1 %copy-start.12 = (s32[108,2]{0,1:T(2,128)S(1)}, s32[108,2]{0,1:T(2,128)}, u32[]{:S(2)}) copy-start(s32[108,2]{0,1:T(2,128)} %param.15) | copy-start | bytes 2596
  7.1 9.1 %copy-start.14 = (s32[108]{0:T(128)S(1)}, s32[108]{0:T(128)}, u32[]{:S(2)}) copy-start(s32[108]{0:T(128)} %param.16) | copy-start | bytes 1300
  7.1 9.0 %collective-permute-start.1 = (bf16[256,256]{1,0:T(8,128)(2,1)S(1)}, bf16[256,256]{1,0:T(8,128)(2,1)S(1)}, u32[]{:S(2)}, u32[]{:S(2)}) collective-permute-start(bf16[256,256]{1,0:T(8,128)(2,1)S(1)} %dynamic-slice_bitcast_fusion.own), channel_id=1, source_target_pairs={{0,16},{16,0},{1,17},{17,1},{2,18},{18,2},{3,19},{19,3},{4,20},{20... | collective-permute-start | bytes 393224 | tf_op jit(solution)/shard_map/ppermute | solution.py:536
  13.0 1.5 %copy-start = (bf16[2,3328,128]{2,1,0:T(8,128)(2,1)S(1)}, bf16[2,3328,128]{2,1,0:T(8,128)(2,1)}, u32[]{:S(2)}) copy-start(bf16[2,3328,128]{2,1,0:T(8,128)(2,1)} %constant.42.clone.tables) | copy-start | bytes 5111812
  14.4 1.8 %copy-start.1 = (bf16[2,3328,128]{2,1,0:T(8,128)(2,1)S(1)}, bf16[2,3328,128]{2,1,0:T(8,128)(2,1)}, u32[]{:S(2)}) copy-start(bf16[2,3328,128]{2,1,0:T(8,128)(2,1)} %constant.42.clone.tables) | copy-start | bytes 5111812
  16.2 21.5 %copy-start.3 = (bf16[11,96,128]{2,1,0:T(8,128)(2,1)S(1)}, bf16[11,96,128]{2,1,0:T(8,128)(2,1)}, u32[]{:S(2)}) copy-start(bf16[11,96,128]{2,1,0:T(8,128)(2,1)} %constant.46.clone.vlo) | copy-start | bytes 811012
  16.2 21.5 %copy-start.4 = (bf16[11,96,128]{2,1,0:T(8,128)(2,1)S(1)}, bf16[11,96,128]{2,1,0:T(8,128)(2,1)}, u32[]{:S(2)}) copy-start(bf16[11,96,128]{2,1,0:T(8,128)(2,1)} %constant.45.clone.vhi) | copy-start | bytes 811012
  16.2 21.4 %copy-start.5 = (bf16[2,2,256,128]{3,2,1,0:T(8,128)(2,1)S(1)}, bf16[2,2,256,128]{3,2,1,0:T(8,128)(2,1)}, u32[]{:S(2)}) copy-start(bf16[2,2,256,128]{3,2,1,0:T(8,128)(2,1)} %constant.47.clone.steps) | copy-start | bytes 786436
  16.2 21.4 %copy-start.6 = (bf16[2,512,128]{2,1,0:T(8,128)(2,1)S(1)}, bf16[2,512,128]{2,1,0:T(8,128)(2,1)}, u32[]{:S(2)}) copy-start(bf16[2,512,128]{2,1,0:T(8,128)(2,1)} %constant.44.clone.depth) | copy-start | bytes 786436
  16.2 21.4 %copy-start.10 = (f32[4,16,128]{2,1,0:T(8,128)S(1)}, f32[4,16,128]{2,1,0:T(8,128)}, u32[]{:S(2)}) copy-start(f32[4,16,128]{2,1,0:T(8,128)} %constant.48.clone.shift) | copy-start | bytes 98308
  16.3 21.4 %copy-start.13 = (f32[2,32]{1,0:T(2,128)S(1)}, f32[2,32]{1,0:T(2,128)}, u32[]{:S(2)}) copy-start(f32[2,32]{1,0:T(2,128)} %constant.43.clone.circle) | copy-start | bytes 772
  18.5 33.9 %copy-start.7 = (f32[16,16,128]{2,1,0:T(8,128)S(1)}, f32[16,16,128]{2,1,0:T(8,128)}, u32[]{:S(2)}) copy-start(f32[16,16,128]{2,1,0:T(8,128)} %constant.49.clone.turns) | copy-start | bytes 393220
  18.5 33.9 %copy-start.9 = (f32[3,4,8,128]{3,2,1,0:T(8,128)S(1)}, f32[3,4,8,128]{3,2,1,0:T(8,128)}, u32[]{:S(2)}) copy-start(f32[3,4,8,128]{3,2,1,0:T(8,128)} %constant.50.clone.places) | copy-start | bytes 147460
  37.6 42.3 %copy-start.8 = (f32[128,64]{1,0:T(8,128)S(1)}, f32[128,64]{1,0:T(8,128)}, u32[]{:S(2)}) copy-start(f32[128,64]{1,0:T(8,128)} %constant.51.clone.graph) | copy-start | bytes 98308
  53.8 26.1 %all-to-all-start.2 = ((f32[16,8,128]{2,1,0:T(8,128)}), f32[16,8,128]{2,1,0:T(8,128)S(1)}, u32[]{:S(2)}, u32[]{:S(2)}) async-start(f32[16,8,128]{2,1,0:T(8,128)} %get-tuple-element.19), calls=%async_computation.2 | async-start | bytes 131072 | tf_op jit(solution)/shard_map/all_to_all | solution.py:570
  68.3 5.5 %collective-permute-start.2 = (f32[9,8,128]{2,1,0:T(8,128)S(1)}, f32[9,8,128]{2,1,0:T(8,128)S(1)}, u32[]{:S(2)}, u32[]{:S(2)}) collective-permute-start(f32[9,8,128]{2,1,0:T(8,128)S(1)} %get-tuple-element.17.mine), channel_id=1, source_target_pairs={{32,0},{64,32},{96,64},{128,96},{160,128},{192,160},{224,192},{256... | collective-permute-start | bytes 110600 | tf_op jit(solution)/shard_map/ppermute | solution.py:569

commit v5 on v4

--- a/solution.py
+++ b/solution.py
@@ -188,15 +188,15 @@
 
 
 def graph_table():
-    table = np.zeros((PLANES, 8, ROW * PLANES), np.float32)
+    table = np.zeros((8, PLANES, ROW * PLANES), np.float32)
     for plane in range(PLANES):
         base = ROW * plane
         pairs = [(base, base + 1), (base + 2, base + 3), (base + 1, base + 2)]
         pairs += [(base - ROW + col, base + col) for col in range(ROW)]
         for slot, (first, second) in enumerate(pairs):
             if first >= 0:
-                table[plane, slot, first] = 1.0
-                table[plane, slot, second] = -1.0
+                table[slot, plane, first] = 1.0
+                table[slot, plane, second] = -1.0
     return table.reshape(PLANES * 8, ROW * PLANES)
 
 
@@ -418,7 +418,7 @@
     out[...] = jnp.broadcast_to(packed[None], out.shape)
 
 
-def energy_kernel(where, got, offsets, turns, places, windows, terms):
+def across_sums(got, turns):
     sums = [[None] * WIN, [None] * WIN]
     for sub in range(SUBS):
         turn = turns[sub]
@@ -428,7 +428,11 @@
                 term = value * turn[step : step + 1]
                 sums[core][step] = term if sub == 0 else sums[core][step] + term
     sums = [[value + pltpu.roll(value, 64, 1) for value in side] for side in sums]
-    seam = [left + right for left, right in zip(*sums)]
+    return sums, [left + right for left, right in zip(*sums)]
+
+
+def energy_kernel(got, offsets, turns, places, terms):
+    sums, seam = across_sums(got, turns)
     totals = []
     for side in (sums[0], sums[1], seam):
         squares = [value * value for value in side]
@@ -456,7 +460,15 @@
     place = offsets[...] + mixed / (energy + EPSILON)
     value = jnp.where(lane == 0, energy, energy * place)
     value = jnp.where(lane < 4, value, 0.0)
-    terms[...] = jnp.broadcast_to(value[None], terms.shape)
+    line = value[0:1]
+    for slot in range(1, 7):
+        line = line + pltpu.roll(value[slot : slot + 1], 4 * slot, 1)
+    terms[...] = jnp.broadcast_to(line[None], terms.shape)
+
+
+def values_kernel(where, got, turns, places, ignored, windows):
+    del ignored
+    sums, seam = across_sums(got, turns)
     is_left = where[1] == 0
     at_seam = places[0, 3] > 0.0
     for step in range(WIN):
@@ -480,19 +492,18 @@
     return [rows[WIN * pair : WIN * (pair + 1)] for pair in range(4)]
 
 
-def graph_kernel(terms, graph, ignored, matrix, rhs):
+def graph_kernel(terms, graph, turned, ignored, matrix, rhs):
     del ignored
-    table = graph[...]
-    value = terms[...].reshape(PLANES * 8, 128)
-    weighted = table * value[:, :1]
-    over = (((0,), (0,)), ((), ()))
-    matrix[...] = lax.dot_general(
-        table, weighted, over, precision=lax.Precision.HIGHEST, preferred_element_type=F32
-    )
-    load = lax.dot_general(
-        value, table, over, precision=lax.Precision.HIGHEST, preferred_element_type=F32
-    )
-    rhs[...] = load[1:4]
+    lines = jnp.concatenate([terms[plane, 0:1] for plane in range(PLANES)], axis=0)
+    slots = [lines] + [pltpu.roll(lines, 128 - 4 * slot, 1) for slot in range(1, 8)]
+    value = jnp.concatenate(slots, axis=0)
+    wide = jnp.concatenate([graph[...] * value[:, :1], value[:, :64]], axis=1)
+    high, rest = wide.astype(BF), wide - wide.astype(BF).astype(F32)
+    middle, low = split(rest)
+    table = turned[...]
+    both = dot(table, high) + dot(table, middle) + dot(table, low)
+    matrix[...] = both[:, :64]
+    rhs[...] = both.T[65:68]
 
 
 def place_kernel(where, meta, mine, below, windows, done):
@@ -560,11 +571,17 @@
         (smem,) * 3 + (vmem,) * 6,
     )
     shares = lax.all_to_all(partial, ("core", "sub"), split_axis=0, concat_axis=0, tiled=True)
-    mine, terms = call(
+    terms = call(
         energy_kernel,
-        (jax.ShapeDtypeStruct((WIN, 8, 128), F32), jax.ShapeDtypeStruct((PLANES, 8, 128), F32)),
-        (where, shares, offsets, turn_table(), place_table()),
-        (smem, vmem, vmem, vmem, vmem),
+        jax.ShapeDtypeStruct((PLANES, 8, 128), F32),
+        (shares, offsets, turn_table(), place_table()),
+        (vmem,) * 4,
+    )
+    mine = call(
+        values_kernel,
+        jax.ShapeDtypeStruct((WIN, 8, 128), F32),
+        (where, shares, turn_table(), place_table(), terms),
+        (smem, vmem, vmem, vmem, pl.ANY),
     )
     below = lax.ppermute(mine, "z", [(k + 1, k) for k in range(PLANES - 1)])
     all_terms = lax.all_to_all(terms, "z", split_axis=0, concat_axis=0, tiled=True)
@@ -577,8 +594,8 @@
     matrix, rhs = call(
         graph_kernel,
         (jax.ShapeDtypeStruct((64, 64), F32), jax.ShapeDtypeStruct((3, 64), F32)),
-        (all_terms, graph_table(), done),
-        (vmem, vmem, pl.ANY),
+        (all_terms, graph_table(), graph_table().T.astype(ml_dtypes.bfloat16), done),
+        (vmem, vmem, vmem, pl.ANY),
     )
     return windows, matrix, rhs.T
 

time: 81.4 us -> 80.8 us (level)
    pallas_call x6 -> x7, Pallas kernels: 10.5 us -> 10.8 us  [call(): pl.pallas_call(kernel, out_shape=shapes, in_specs=specs, out_specs=outs,...]
  transfers between devices with their start and end apart: 4 -> 4, of which waited for: 2 -> 2; matrix products, arithmetic and copies ran while one was open for 1% -> 1% of each run, Pallas kernels for 4% -> 5%
where the time goes in v5:
time: 80.8 us; the launch traced here: 80.4 us
  blocking collectives  31 us (38%)
  starting transfers between devices  26.1 us (32%)
  Pallas kernels  10.8 us (13%)
  waiting for transfers between devices  8.05 us (10%)
  local copies, waits for them, and re-layouts  3.54 us (4%)
  between operations  0.9 us (1%)
    all_to_all x1, blocking collectives, local(): got = lax.all_to_all(sent, 'sub', split_axis=0, concat_axis=0, tiled=True)  19.1 us
    all_to_all x1, starting transfers between devices, local(): lax.all_to_all(terms, 'z', split_axis=0, concat_axis=0, tiled=True)  14.5 us
    all_to_all x1, blocking collectives, local(): lax.all_to_all(partial, ('core', 'sub'), split_axis=0, concat_axis=0, til...  11.8 us
    pallas_call x7, Pallas kernels, call(): pl.pallas_call(kernel, out_shape=shapes, in_specs=specs, out_specs=outs,...  10.8 us
    ppermute x1, starting transfers between devices, local(): other = lax.ppermute(own, 'core', [(0, 1), (1, 0)])  5.84 us
    ppermute x1, starting transfers between devices, local(): lax.ppermute(bottoms, 'z', [(k, k + 1) for k in range(PLANES - 1)])  4.39 us
    all_to_all x1, waiting for transfers between devices, local(): lax.all_to_all(terms, 'z', split_axis=0, concat_axis=0, tiled=True)  4.35 us
    ppermute x1, waiting for transfers between devices, local(): below = lax.ppermute(mine, 'z', [(k + 1, k) for k in range(PLANES - 1)])  3.7 us
  transfers between devices with their start and end apart: 4, of which 2 were waited for; matrix products, arithmetic and copies ran while one was open for 1% of the time, Pallas kernels for 5%

profile of v5, /device:TPU:1, one launch (start us, length us, event | category | flops | bytes accessed | tf_op | source)
XLA Modules:
  0.0 80.4 jit_solution(16743485541815382476)
XLA Ops:
  0.6 0.0 copy-start.2
  0.6 1.1 %fusion = (bf16[1,256,256]{2,1,0:T(8,128)(2,1)S(1)}, bf16[1,256,256]{2,1,0:T(8,128)(2,1)S(1)}) fusion(bf16[8,256,256]{2,1,0:T(8,128)(2,1)} %bitcast.10), kind=kLoop, calls=%fused_computation.3 | loop fusion | bytes 524288 | tf_op jit(solution)/shard_map/slice | solution.py:543
  1.8 4.4 %collective-permute-start = (bf16[2,256,256]{2,1,0:T(8,128)(2,1)S(1)}, bf16[2,256,256]{2,1,0:T(8,128)(2,1)S(1)}, u32[]{:S(2)}, u32[]{:S(2)}) collective-permute-start(bf16[2,256,256]{2,1,0:T(8,128)(2,1)S(1)} %pad_maximum_fusion), channel_id=1, source_target_pairs={{0,32},{32,64},{64,96},{96,128},{128,160},{160,192},{192,224},{224... | collective-permute-start | bytes 786440 | tf_op jit(solution)/shard_map/ppermute | solution.py:544
  6.2 0.9 %dynamic-slice_bitcast_fusion.own = bf16[256,256]{1,0:T(8,128)(2,1)S(1)} fusion(bf16[8,256,256]{2,1,0:T(8,128)(2,1)} %bitcast.11, s32[]{:T(128)S(6)} %select_n.4), kind=kLoop, calls=%fused_computation.1 | loop fusion | bytes 262148 | tf_op jit(solution)/shard_map/jit(dynamic_index_in_dim)/squeeze | solution.py:546
  7.1 5.8 %collective-permute-start.1 = (bf16[256,256]{1,0:T(8,128)(2,1)S(1)}, bf16[256,256]{1,0:T(8,128)(2,1)S(1)}, u32[]{:S(2)}, u32[]{:S(2)}) collective-permute-start(bf16[256,256]{1,0:T(8,128)(2,1)S(1)} %dynamic-slice_bitcast_fusion.own), channel_id=1, source_target_pairs={{0,16},{16,0},{1,17},{17,1},{2,18},{18,2},{3,19},{19,3},{4,20},{20... | collective-permute-start | bytes 393224 | tf_op jit(solution)/shard_map/ppermute | solution.py:547
  13.0 0.0 copy-start
  13.0 1.4 %copy-done = bf16[2,3328,128]{2,1,0:T(8,128)(2,1)S(1)} copy-done((bf16[2,3328,128]{2,1,0:T(8,128)(2,1)S(1)}, bf16[2,3328,128]{2,1,0:T(8,128)(2,1)}, u32[]{:S(2)}) %copy-start) | copy-done | bytes 1703960
  14.4 1.6 %shard_map.184.here = bf16[16,64,256]{2,1,0:T(8,128)(2,1)S(1)} custom-call(bf16[8,256,256]{2,1,0:T(8,128)(2,1)S(1)} %bitcast.12, bf16[2,3328,128]{2,1,0:T(8,128)(2,1)S(1)} %copy-done), custom_call_target="tpu_custom_call" | custom-call | tf_op jit(solution)/shard_map/pallas_call | solution.py:525
  16.1 0.1 pad_add_fusion.where
  16.2 0.0 copy-start.5
  16.2 0.0 copy-start.6
  16.2 0.0 copy-start.7
  16.3 2.2 %shard_map.185 = (bf16[16,112,256]{2,1,0:T(8,128)(2,1)S(1)}, s32[16,128]{1,0:T(8,128)S(1)}, f32[8,128]{1,0:T(8,128)S(1)}) custom-call(s32[3]{0:T(128)S(1)} %pad_add_fusion.where, bf16[16,64,256]{2,1,0:T(8,128)(2,1)S(1)} %shard_map.184.here, bf16[2,256,256]{2,1,0:T(8,128)(2,1)S(1)} %collective-permute-done.below, ...), custom_call_target="tpu_custom_call" | custom-call | tf_op jit(solution)/shard_map/pallas_call | solution.py:525
  18.5 19.1 %all_to_all.15.got = bf16[16,112,256]{2,1,0:T(8,128)(2,1)S(1)} all-to-all(bf16[16,112,256]{2,1,0:T(8,128)(2,1)S(1)} %get-tuple-element.13), channel_id=1, replica_groups=mesh['z'=16,'core'=2,'sub'=16] {'sub'}, dimensions={0} | all-to-all | bytes 1835008 | tf_op jit(solution)/shard_map/all_to_all | solution.py:566
  37.7 2.8 %shard_map.186 = f32[32,8,128]{2,1,0:T(8,128)S(1)} custom-call(s32[3]{0:T(128)S(1)} %pad_add_fusion.where, s32[16,128]{1,0:T(8,128)S(1)} %get-tuple-element.12.meta, f32[2,32]{1,0:T(2,128)S(1)} %copy-done.14, bf16[16,112,256]{2,1,0:T(8,128)(2,1)S(1)} %all_to_all.15.got, bf16[2,512,128]{2,1,0:T(8,128)(2,1)S(1)} %copy-done.7, ...), custom_call_target="tpu_custom_call" | custom-call | tf_op jit(solution)/shard_map/pallas_call | solution.py:525
  40.5 11.8 %all_to_all.16.got = f32[32,8,128]{2,1,0:T(8,128)S(1)} all-to-all(f32[32,8,128]{2,1,0:T(8,128)S(1)} %shard_map.186), channel_id=1, replica_groups=mesh['z'=16,'core'=2,'sub'=16] {'core','sub'}, dimensions={0} | all-to-all | bytes 262144 | tf_op jit(solution)/shard_map/all_to_all | solution.py:573
  52.4 1.0 %shard_map.187.ignored = f32[16,8,128]{2,1,0:T(8,128)} custom-call(f32[32,8,128]{2,1,0:T(8,128)S(1)} %all_to_all.16.got, f32[8,128]{1,0:T(8,128)S(1)} %get-tuple-element.14.offsets, f32[16,16,128]{2,1,0:T(8,128)S(1)} %copy-done.3, f32[3,4,8,128]{3,2,1,0:T(8,128)S(1)} %copy-done.8), custom_call_target="tpu_custom_call" | custom-call | tf_op jit(solution)/shard_map/pallas_call | solution.py:525
  53.3 14.5 %all-to-all-start.2 = ((f32[16,8,128]{2,1,0:T(8,128)}), f32[16,8,128]{2,1,0:T(8,128)S(1)}, u32[]{:S(2)}, u32[]{:S(2)}) async-start(f32[16,8,128]{2,1,0:T(8,128)} %shard_map.187.ignored), calls=%async_computation.2 | async-start | bytes 131072 | tf_op jit(solution)/shard_map/all_to_all | solution.py:587
  67.9 0.7 shard_map.188.mine
  68.6 1.3 %collective-permute-start.2 = (f32[9,8,128]{2,1,0:T(8,128)S(1)}, f32[9,8,128]{2,1,0:T(8,128)S(1)}, u32[]{:S(2)}, u32[]{:S(2)}) collective-permute-start(f32[9,8,128]{2,1,0:T(8,128)S(1)} %shard_map.188.mine), channel_id=1, source_target_pairs={{32,0},{64,32},{96,64},{128,96},{160,128},{192,160},{224,192},{256... | collective-permute-start | bytes 110600 | tf_op jit(solution)/shard_map/ppermute | solution.py:586
  69.9 3.7 %collective-permute-done.2.below = f32[9,8,128]{2,1,0:T(8,128)S(1)} collective-permute-done((f32[9,8,128]{2,1,0:T(8,128)S(1)}, f32[9,8,128]{2,1,0:T(8,128)S(1)}, u32[]{:S(2)}, u32[]{:S(2)}) %collective-permute-start.2) | collective-permute-done | bytes 36896 | tf_op jit(solution)/shard_map/ppermute | solution.py:586
  73.6 1.5 %shard_map.189 = (f32[6,729]{1,0:T(8,128)}, f32[8,128]{1,0:T(8,128)S(1)}) custom-call(s32[3]{0:T(128)S(1)} %pad_add_fusion.where, s32[16,128]{1,0:T(8,128)S(1)} %get-tuple-element.12.meta, f32[9,8,128]{2,1,0:T(8,128)S(1)} %shard_map.188.mine, f32[9,8,128]{2,1,0:T(8,128)S(1)} %collective-permute-done.2.below), custom_call_target="tpu_custom_call" | custom-call | tf_op jit(solution)/shard_map/pallas_call | solution.py:525
  75.1 4.4 %all-to-all-done.2.terms = f32[16,8,128]{2,1,0:T(8,128)S(1)} async-done(((f32[16,8,128]{2,1,0:T(8,128)}), f32[16,8,128]{2,1,0:T(8,128)S(1)}, u32[]{:S(2)}, u32[]{:S(2)}) %all-to-all-start.2) | async-done | bytes 65568 | tf_op jit(solution)/shard_map/all_to_all | solution.py:587
  79.5 1.0 %shard_map.190 = (f32[64,64]{1,0:T(8,128)}, f32[3,64]{1,0:T(4,128)}) custom-call(f32[16,8,128]{2,1,0:T(8,128)S(1)} %all-to-all-done.2.terms, f32[128,64]{1,0:T(8,128)S(1)} %copy-done.9, bf16[64,128]{1,0:T(8,128)(2,1)S(1)} %copy-done.11, f32[8,128]{1,0:T(8,128)S(1)} %get-tuple-element.16.ignored), custom_call_target="tpu_custom_call" | custom-call | tf_op jit(solution)/shard_map/pallas_call | solution.py:525
  (29 shorter events, 0.1 us)
Async XLA Ops:
  0.6 12.3 %copy-start.2 = (bf16[2,4,8,32,256]{4,3,2,1,0:T(8,128)(2,1)S(1)}, bf16[2,4,8,32,256]{4,3,2,1,0:T(8,128)(2,1)}, u32[]{:S(2)}) copy-start(bf16[2,4,8,32,256]{4,3,2,1,0:T(8,128)(2,1)} %param.17) | copy-start | bytes 3145732
  1.8 14.4 %collective-permute-start = (bf16[2,256,256]{2,1,0:T(8,128)(2,1)S(1)}, bf16[2,256,256]{2,1,0:T(8,128)(2,1)S(1)}, u32[]{:S(2)}, u32[]{:S(2)}) collective-permute-start(bf16[2,256,256]{2,1,0:T(8,128)(2,1)S(1)} %pad_maximum_fusion), channel_id=1, source_target_pairs={{0,32},{32,64},{64,96},{96,128},{128,160},{160,192},{192,224},{224... | collective-permute-start | bytes 786440 | tf_op jit(solution)/shard_map/ppermute | solution.py:544
  7.1 9.1 %copy-start.12 = (s32[108,3]{0,1:T(4,128)S(1)}, s32[108,3]{0,1:T(4,128)}, u32[]{:S(2)}) copy-start(s32[108,3]{0,1:T(4,128)} %param.20) | copy-start | bytes 3892
  7.1 9.1 %copy-start.13 = (s32[108,2]{0,1:T(2,128)S(1)}, s32[108,2]{0,1:T(2,128)}, u32[]{:S(2)}) copy-start(s32[108,2]{0,1:T(2,128)} %param.18) | copy-start | bytes 2596
  7.1 9.1 %copy-start.15 = (s32[108]{0:T(128)S(1)}, s32[108]{0:T(128)}, u32[]{:S(2)}) copy-start(s32[108]{0:T(128)} %param.19) | copy-start | bytes 1300
  7.1 9.0 %collective-permute-start.1 = (bf16[256,256]{1,0:T(8,128)(2,1)S(1)}, bf16[256,256]{1,0:T(8,128)(2,1)S(1)}, u32[]{:S(2)}, u32[]{:S(2)}) collective-permute-start(bf16[256,256]{1,0:T(8,128)(2,1)S(1)} %dynamic-slice_bitcast_fusion.own), channel_id=1, source_target_pairs={{0,16},{16,0},{1,17},{17,1},{2,18},{18,2},{3,19},{19,3},{4,20},{20... | collective-permute-start | bytes 393224 | tf_op jit(solution)/shard_map/ppermute | solution.py:547
  13.0 1.5 %copy-start = (bf16[2,3328,128]{2,1,0:T(8,128)(2,1)S(1)}, bf16[2,3328,128]{2,1,0:T(8,128)(2,1)}, u32[]{:S(2)}) copy-start(bf16[2,3328,128]{2,1,0:T(8,128)(2,1)} %constant.44.clone.tables) | copy-start | bytes 5111812
  14.4 1.8 %copy-start.1 = (bf16[2,3328,128]{2,1,0:T(8,128)(2,1)S(1)}, bf16[2,3328,128]{2,1,0:T(8,128)(2,1)}, u32[]{:S(2)}) copy-start(bf16[2,3328,128]{2,1,0:T(8,128)(2,1)} %constant.44.clone.tables) | copy-start | bytes 5111812
  16.2 21.5 %copy-start.4 = (bf16[11,96,128]{2,1,0:T(8,128)(2,1)S(1)}, bf16[11,96,128]{2,1,0:T(8,128)(2,1)}, u32[]{:S(2)}) copy-start(bf16[11,96,128]{2,1,0:T(8,128)(2,1)} %constant.48.clone.vlo) | copy-start | bytes 811012
  16.2 21.4 %copy-start.5 = (bf16[11,96,128]{2,1,0:T(8,128)(2,1)S(1)}, bf16[11,96,128]{2,1,0:T(8,128)(2,1)}, u32[]{:S(2)}) copy-start(bf16[11,96,128]{2,1,0:T(8,128)(2,1)} %constant.47.clone.vhi) | copy-start | bytes 811012
  16.2 21.4 %copy-start.6 = (bf16[2,2,256,128]{3,2,1,0:T(8,128)(2,1)S(1)}, bf16[2,2,256,128]{3,2,1,0:T(8,128)(2,1)}, u32[]{:S(2)}) copy-start(bf16[2,2,256,128]{3,2,1,0:T(8,128)(2,1)} %constant.49.clone.steps) | copy-start | bytes 786436
  16.2 21.4 %copy-start.7 = (bf16[2,512,128]{2,1,0:T(8,128)(2,1)S(1)}, bf16[2,512,128]{2,1,0:T(8,128)(2,1)}, u32[]{:S(2)}) copy-start(bf16[2,512,128]{2,1,0:T(8,128)(2,1)} %constant.46.clone.depth) | copy-start | bytes 786436
  16.2 21.4 %copy-start.10 = (f32[4,16,128]{2,1,0:T(8,128)S(1)}, f32[4,16,128]{2,1,0:T(8,128)}, u32[]{:S(2)}) copy-start(f32[4,16,128]{2,1,0:T(8,128)} %constant.50.clone.shift) | copy-start | bytes 98308
  16.3 21.4 %copy-start.14 = (f32[2,32]{1,0:T(2,128)S(1)}, f32[2,32]{1,0:T(2,128)}, u32[]{:S(2)}) copy-start(f32[2,32]{1,0:T(2,128)} %constant.45.clone.circle) | copy-start | bytes 772
  18.5 33.9 %copy-start.3 = (f32[16,16,128]{2,1,0:T(8,128)S(1)}, f32[16,16,128]{2,1,0:T(8,128)}, u32[]{:S(2)}) copy-start(f32[16,16,128]{2,1,0:T(8,128)} %constant.51.clone.turns) | copy-start | bytes 393220
  18.5 33.9 %copy-start.8 = (f32[3,4,8,128]{3,2,1,0:T(8,128)S(1)}, f32[3,4,8,128]{3,2,1,0:T(8,128)}, u32[]{:S(2)}) copy-start(f32[3,4,8,128]{3,2,1,0:T(8,128)} %constant.52.clone.places) | copy-start | bytes 147460
  37.7 41.8 %copy-start.9 = (f32[128,64]{1,0:T(8,128)S(1)}, f32[128,64]{1,0:T(8,128)}, u32[]{:S(2)}) copy-start(f32[128,64]{1,0:T(8,128)} %constant.53.clone.graph) | copy-start | bytes 98308
  37.7 41.8 %copy-start.11 = (bf16[64,128]{1,0:T(8,128)(2,1)S(1)}, bf16[64,128]{1,0:T(8,128)(2,1)}, u32[]{:S(2)}) copy-start(bf16[64,128]{1,0:T(8,128)(2,1)} %constant.54.clone.turned) | copy-start | bytes 49156
  53.3 26.1 %all-to-all-start.2 = ((f32[16,8,128]{2,1,0:T(8,128)}), f32[16,8,128]{2,1,0:T(8,128)S(1)}, u32[]{:S(2)}, u32[]{:S(2)}) async-start(f32[16,8,128]{2,1,0:T(8,128)} %shard_map.187.ignored), calls=%async_computation.2 | async-start | bytes 131072 | tf_op jit(solution)/shard_map/all_to_all | solution.py:587
  68.6 5.0 %collective-permute-start.2 = (f32[9,8,128]{2,1,0:T(8,128)S(1)}, f32[9,8,128]{2,1,0:T(8,128)S(1)}, u32[]{:S(2)}, u32[]{:S(2)}) collective-permute-start(f32[9,8,128]{2,1,0:T(8,128)S(1)} %shard_map.188.mine), channel_id=1, source_target_pairs={{32,0},{64,32},{96,64},{128,96},{160,128},{192,160},{224,192},{256... | collective-permute-start | bytes 110600 | tf_op jit(solution)/shard_map/ppermute | solution.py:586

commit v6 on v5

--- a/solution.py
+++ b/solution.py
@@ -274,12 +274,10 @@
         out[:, 16 * k : 16 * k + 16, :] = chunk([parts[0][k], parts[1][k]])
 
 
-def remote_kernel(
-    where, here, below, own, other, tables, pair_tiles, owner, pair_offset,
-    out, facts, offsets, moved,
+def seam_kernel(
+    where, own, other, tables, pair_tiles, owner, pair_offset, ignored, out, facts, offsets
 ):
-    kept = pltpu.make_async_copy(here, out.at[:, pl.ds(0, 64), :], moved)
-    kept.start()
+    del ignored
     offset, slot = pair_facts(where, pair_tiles, owner, pair_offset)
     lane = lax.broadcasted_iota(jnp.int32, (16, 128), 1)
     facts[...] = jnp.where(
@@ -289,19 +287,29 @@
     offsets[...] = jnp.where(
         lane == 1, offset[0][:8], jnp.where(lane == 2, offset[1][:8], offset[2][:8])
     ).astype(F32)
-    parts = []
-    for half in range(2):
-        stack = [across_dft(below[k], half, tables) for k in range(2)]
-        parts.append(along_dft(jnp.concatenate(stack, axis=0), half, tables, 2))
-    for k in range(2):
-        out[:, 64 + 16 * k : 80 + 16 * k, :] = chunk([parts[0][k], parts[1][k]])
     core = where[1]
     mine, theirs = own[...], other[...]
     first = jnp.where(core == 0, mine, theirs)
     second = jnp.where(core == 0, theirs, mine)
     stack = [across_dft(strip, core, tables) for strip in (first, second)]
-    out[:, 96:112, :] = chunk(along_dft(jnp.concatenate(stack, axis=0), core, tables, 2))
-    kept.wait()
+    out[...] = chunk(along_dft(jnp.concatenate(stack, axis=0), core, tables, 2))
+
+
+def remote_kernel(here, seam, below, tables, out, moved):
+    kept = [
+        pltpu.make_async_copy(here, out.at[:, pl.ds(0, 64), :], moved.at[0]),
+        pltpu.make_async_copy(seam, out.at[:, pl.ds(96, 16), :], moved.at[1]),
+    ]
+    for copy in kept:
+        copy.start()
+    parts = []
+    for half in range(2):
+        stack = [across_dft(below[k], half, tables) for k in range(2)]
+        parts.append(along_dft(jnp.concatenate(stack, axis=0), half, tables, 2))
+    for k in range(2):
+        out[:, 64 + 16 * k : 80 + 16 * k, :] = chunk([parts[0][k], parts[1][k]])
+    for copy in kept:
+        copy.wait()
 
 
 def spectrum_of(block, zeroth, held, depth_hi, depth_lo):
@@ -549,19 +557,25 @@
     here = call(
         local_kernel, jax.ShapeDtypeStruct((SUBS, 64, 2 * HALF), BF), (tiles, tables), (vmem, vmem)
     )
-    sent, facts, offsets = call(
-        remote_kernel,
+    seam, facts, offsets = call(
+        seam_kernel,
         (
-            jax.ShapeDtypeStruct((SUBS, 112, 2 * HALF), BF),
+            jax.ShapeDtypeStruct((SUBS, 16, 2 * HALF), BF),
             jax.ShapeDtypeStruct((16, 128), jnp.int32),
             jax.ShapeDtypeStruct((8, 128), F32),
         ),
         (
-            where, here, from_above, own, other, tables,
-            pair_tiles.T, pair_owner.reshape(1, -1), pair_offset.T,
+            where, own, other, tables,
+            pair_tiles.T, pair_owner.reshape(1, -1), pair_offset.T, here,
         ),
-        (smem,) + (vmem,) * 8,
-        scratch_shapes=[pltpu.SemaphoreType.DMA],
+        (smem,) + (vmem,) * 6 + (pl.ANY,),
+    )
+    sent = call(
+        remote_kernel,
+        jax.ShapeDtypeStruct((SUBS, 112, 2 * HALF), BF),
+        (here, seam, from_above, tables),
+        (vmem,) * 4,
+        scratch_shapes=[pltpu.SemaphoreType.DMA((2,))],
     )
     got = lax.all_to_all(sent, "sub", split_axis=0, concat_axis=0, tiled=True)
     partial = call(

time: 80.8 us -> 80.8 us (level)
    pallas_call x7 -> x8, Pallas kernels: 10.8 us -> 11.3 us  [call(): pl.pallas_call(kernel, out_shape=shapes, in_specs=specs, out_specs=outs,...]
  transfers between devices with their start and end apart: 4 -> 4, of which waited for: 2 -> 2; matrix products, arithmetic and copies ran while one was open for 1% -> 1% of each run, Pallas kernels for 5% -> 6%
where the time goes in v6:
time: 80.8 us; the launch traced here: 80.4 us
  blocking collectives  31 us (38%)
  starting transfers between devices  25.5 us (32%)
  Pallas kernels  11.3 us (14%)
  waiting for transfers between devices  8.05 us (10%)
  local copies, waits for them, and re-layouts  3.54 us (4%)
  between operations  0.91 us (1%)
    all_to_all x1, blocking collectives, local(): got = lax.all_to_all(sent, 'sub', split_axis=0, concat_axis=0, tiled=True)  19.1 us
    all_to_all x1, starting transfers between devices, local(): lax.all_to_all(terms, 'z', split_axis=0, concat_axis=0, tiled=True)  14 us
    all_to_all x1, blocking collectives, local(): lax.all_to_all(partial, ('core', 'sub'), split_axis=0, concat_axis=0, til...  11.8 us
    pallas_call x8, Pallas kernels, call(): pl.pallas_call(kernel, out_shape=shapes, in_specs=specs, out_specs=outs,...  11.3 us
    ppermute x1, starting transfers between devices, local(): other = lax.ppermute(own, 'core', [(0, 1), (1, 0)])  5.84 us
    ppermute x1, starting transfers between devices, local(): lax.ppermute(bottoms, 'z', [(k, k + 1) for k in range(PLANES - 1)])  4.39 us
    all_to_all x1, waiting for transfers between devices, local(): lax.all_to_all(terms, 'z', split_axis=0, concat_axis=0, tiled=True)  4.35 us
    ppermute x1, waiting for transfers between devices, local(): below = lax.ppermute(mine, 'z', [(k + 1, k) for k in range(PLANES - 1)])  3.7 us
  transfers between devices with their start and end apart: 4, of which 2 were waited for; matrix products, arithmetic and copies ran while one was open for 1% of the time, Pallas kernels for 6%

profile of v6, /device:TPU:1, one launch (start us, length us, event | category | flops | bytes accessed | tf_op | source)
XLA Modules:
  0.0 80.4 jit_solution(9588541723712215921)
XLA Ops:
  0.6 0.0 copy-start.2
  0.6 1.1 %fusion = (bf16[1,256,256]{2,1,0:T(8,128)(2,1)S(1)}, bf16[1,256,256]{2,1,0:T(8,128)(2,1)S(1)}) fusion(bf16[8,256,256]{2,1,0:T(8,128)(2,1)} %bitcast.10), kind=kLoop, calls=%fused_computation.3 | loop fusion | bytes 524288 | tf_op jit(solution)/shard_map/slice | solution.py:551
  1.8 4.4 %collective-permute-start.1 = (bf16[2,256,256]{2,1,0:T(8,128)(2,1)S(1)}, bf16[2,256,256]{2,1,0:T(8,128)(2,1)S(1)}, u32[]{:S(2)}, u32[]{:S(2)}) collective-permute-start(bf16[2,256,256]{2,1,0:T(8,128)(2,1)S(1)} %pad_maximum_fusion), channel_id=1, source_target_pairs={{0,32},{32,64},{64,96},{96,128},{128,160},{160,192},{192,224},{224... | collective-permute-start | bytes 786440 | tf_op jit(solution)/shard_map/ppermute | solution.py:552
  6.2 0.9 %dynamic-slice_bitcast_fusion.own = bf16[256,256]{1,0:T(8,128)(2,1)S(1)} fusion(bf16[8,256,256]{2,1,0:T(8,128)(2,1)} %bitcast.11, s32[]{:T(128)S(6)} %select_n.4), kind=kLoop, calls=%fused_computation.1 | loop fusion | bytes 262148 | tf_op jit(solution)/shard_map/jit(dynamic_index_in_dim)/squeeze | solution.py:554
  7.1 5.8 %collective-permute-start = (bf16[256,256]{1,0:T(8,128)(2,1)S(1)}, bf16[256,256]{1,0:T(8,128)(2,1)S(1)}, u32[]{:S(2)}, u32[]{:S(2)}) collective-permute-start(bf16[256,256]{1,0:T(8,128)(2,1)S(1)} %dynamic-slice_bitcast_fusion.own), channel_id=1, source_target_pairs={{0,16},{16,0},{1,17},{17,1},{2,18},{18,2},{3,19},{19,3},{4,20},{20... | collective-permute-start | bytes 393224 | tf_op jit(solution)/shard_map/ppermute | solution.py:555
  13.0 0.0 copy-start
  13.0 1.4 %copy-done = bf16[2,3328,128]{2,1,0:T(8,128)(2,1)S(1)} copy-done((bf16[2,3328,128]{2,1,0:T(8,128)(2,1)S(1)}, bf16[2,3328,128]{2,1,0:T(8,128)(2,1)}, u32[]{:S(2)}) %copy-start) | copy-done | bytes 1703960
  14.4 1.6 %shard_map.184.ignored.here = bf16[16,64,256]{2,1,0:T(8,128)(2,1)S(1)} custom-call(bf16[8,256,256]{2,1,0:T(8,128)(2,1)S(1)} %bitcast.12, bf16[2,3328,128]{2,1,0:T(8,128)(2,1)S(1)} %copy-done), custom_call_target="tpu_custom_call" | custom-call | tf_op jit(solution)/shard_map/pallas_call | solution.py:533
  16.1 0.1 pad_add_fusion.where
  16.2 1.4 %shard_map.185 = (bf16[16,16,256]{2,1,0:T(8,128)(2,1)S(1)}, s32[16,128]{1,0:T(8,128)S(1)}, f32[8,128]{1,0:T(8,128)S(1)}) custom-call(s32[3]{0:T(128)S(1)} %pad_add_fusion.where, bf16[256,256]{1,0:T(8,128)(2,1)S(1)} %dynamic-slice_bitcast_fusion.own, bf16[256,256]{1,0:T(8,128)(2,1)S(1)} %collective-permute-done.other, bf16[2,3328,128]{2,1,0:T(8,128)(2,1)S(1)} %copy-done.1, ...), custom_call_target="tpu_custom_call" | custom-call | tf_op jit(solution)/shard_map/pallas_call | solution.py:533
  17.6 1.3 %shard_map.186 = bf16[16,112,256]{2,1,0:T(8,128)(2,1)S(1)} custom-call(bf16[16,64,256]{2,1,0:T(8,128)(2,1)S(1)} %shard_map.184.ignored.here, bf16[16,16,256]{2,1,0:T(8,128)(2,1)S(1)} %get-tuple-element.13.seam, bf16[2,256,256]{2,1,0:T(8,128)(2,1)S(1)} %collective-permute-done.1.below, bf16[2,3328,128]{2,1,0:T(8,128)(2,1)S(1)} %copy-done.1), custom_call_target="tpu_custom_call" | custom-call | tf_op jit(solution)/shard_map/pallas_call | solution.py:533
  18.9 0.0 copy-start.4
  18.9 0.0 copy-start.6
  19.0 19.1 %all_to_all.15.got = bf16[16,112,256]{2,1,0:T(8,128)(2,1)S(1)} all-to-all(bf16[16,112,256]{2,1,0:T(8,128)(2,1)S(1)} %shard_map.186), channel_id=1, replica_groups=mesh['z'=16,'core'=2,'sub'=16] {'sub'}, dimensions={0} | all-to-all | bytes 1835008 | tf_op jit(solution)/shard_map/all_to_all | solution.py:580
  38.2 2.8 %shard_map.187 = f32[32,8,128]{2,1,0:T(8,128)S(1)} custom-call(s32[3]{0:T(128)S(1)} %pad_add_fusion.where, s32[16,128]{1,0:T(8,128)S(1)} %get-tuple-element.12.meta, f32[2,32]{1,0:T(2,128)S(1)} %copy-done.14, bf16[16,112,256]{2,1,0:T(8,128)(2,1)S(1)} %all_to_all.15.got, bf16[2,512,128]{2,1,0:T(8,128)(2,1)S(1)} %copy-done.7, ...), custom_call_target="tpu_custom_call" | custom-call | tf_op jit(solution)/shard_map/pallas_call | solution.py:533
  41.0 11.8 %all_to_all.16.got = f32[32,8,128]{2,1,0:T(8,128)S(1)} all-to-all(f32[32,8,128]{2,1,0:T(8,128)S(1)} %shard_map.187), channel_id=1, replica_groups=mesh['z'=16,'core'=2,'sub'=16] {'core','sub'}, dimensions={0} | all-to-all | bytes 262144 | tf_op jit(solution)/shard_map/all_to_all | solution.py:587
  52.8 1.0 %shard_map.188.ignored = f32[16,8,128]{2,1,0:T(8,128)} custom-call(f32[32,8,128]{2,1,0:T(8,128)S(1)} %all_to_all.16.got, f32[8,128]{1,0:T(8,128)S(1)} %get-tuple-element.14.offsets, f32[16,16,128]{2,1,0:T(8,128)S(1)} %copy-done.3, f32[3,4,8,128]{3,2,1,0:T(8,128)S(1)} %copy-done.8), custom_call_target="tpu_custom_call" | custom-call | tf_op jit(solution)/shard_map/pallas_call | solution.py:533
  53.8 14.0 %all-to-all-start.2 = ((f32[16,8,128]{2,1,0:T(8,128)}), f32[16,8,128]{2,1,0:T(8,128)S(1)}, u32[]{:S(2)}, u32[]{:S(2)}) async-start(f32[16,8,128]{2,1,0:T(8,128)} %shard_map.188.ignored), calls=%async_computation.2 | async-start | bytes 131072 | tf_op jit(solution)/shard_map/all_to_all | solution.py:601
  67.8 0.7 shard_map.189.mine
  68.5 1.3 %collective-permute-start.2 = (f32[9,8,128]{2,1,0:T(8,128)S(1)}, f32[9,8,128]{2,1,0:T(8,128)S(1)}, u32[]{:S(2)}, u32[]{:S(2)}) collective-permute-start(f32[9,8,128]{2,1,0:T(8,128)S(1)} %shard_map.189.mine), channel_id=1, source_target_pairs={{32,0},{64,32},{96,64},{128,96},{160,128},{192,160},{224,192},{256... | collective-permute-start | bytes 110600 | tf_op jit(solution)/shard_map/ppermute | solution.py:600
  69.8 3.7 %collective-permute-done.2.below = f32[9,8,128]{2,1,0:T(8,128)S(1)} collective-permute-done((f32[9,8,128]{2,1,0:T(8,128)S(1)}, f32[9,8,128]{2,1,0:T(8,128)S(1)}, u32[]{:S(2)}, u32[]{:S(2)}) %collective-permute-start.2) | collective-permute-done | bytes 36896 | tf_op jit(solution)/shard_map/ppermute | solution.py:600
  73.5 1.5 %shard_map.190 = (f32[6,729]{1,0:T(8,128)}, f32[8,128]{1,0:T(8,128)S(1)}) custom-call(s32[3]{0:T(128)S(1)} %pad_add_fusion.where, s32[16,128]{1,0:T(8,128)S(1)} %get-tuple-element.12.meta, f32[9,8,128]{2,1,0:T(8,128)S(1)} %shard_map.189.mine, f32[9,8,128]{2,1,0:T(8,128)S(1)} %collective-permute-done.2.below), custom_call_target="tpu_custom_call" | custom-call | tf_op jit(solution)/shard_map/pallas_call | solution.py:533
  75.0 4.4 %all-to-all-done.2.terms = f32[16,8,128]{2,1,0:T(8,128)S(1)} async-done(((f32[16,8,128]{2,1,0:T(8,128)}), f32[16,8,128]{2,1,0:T(8,128)S(1)}, u32[]{:S(2)}, u32[]{:S(2)}) %all-to-all-start.2) | async-done | bytes 65568 | tf_op jit(solution)/shard_map/all_to_all | solution.py:601
  79.4 1.0 %shard_map.191 = (f32[64,64]{1,0:T(8,128)}, f32[3,64]{1,0:T(4,128)}) custom-call(f32[16,8,128]{2,1,0:T(8,128)S(1)} %all-to-all-done.2.terms, f32[128,64]{1,0:T(8,128)S(1)} %copy-done.9, bf16[64,128]{1,0:T(8,128)(2,1)S(1)} %copy-done.11, f32[8,128]{1,0:T(8,128)S(1)} %get-tuple-element.16.ignored), custom_call_target="tpu_custom_call" | custom-call | tf_op jit(solution)/shard_map/pallas_call | solution.py:533
  (30 shorter events, 0.1 us)
Async XLA Ops:
  0.6 12.3 %copy-start.2 = (bf16[2,4,8,32,256]{4,3,2,1,0:T(8,128)(2,1)S(1)}, bf16[2,4,8,32,256]{4,3,2,1,0:T(8,128)(2,1)}, u32[]{:S(2)}) copy-start(bf16[2,4,8,32,256]{4,3,2,1,0:T(8,128)(2,1)} %param.17) | copy-start | bytes 3145732
  1.8 15.8 %collective-permute-start.1 = (bf16[2,256,256]{2,1,0:T(8,128)(2,1)S(1)}, bf16[2,256,256]{2,1,0:T(8,128)(2,1)S(1)}, u32[]{:S(2)}, u32[]{:S(2)}) collective-permute-start(bf16[2,256,256]{2,1,0:T(8,128)(2,1)S(1)} %pad_maximum_fusion), channel_id=1, source_target_pairs={{0,32},{32,64},{64,96},{96,128},{128,160},{160,192},{192,224},{224... | collective-permute-start | bytes 786440 | tf_op jit(solution)/shard_map/ppermute | solution.py:552
  7.1 9.1 %copy-start.12 = (s32[108,3]{0,1:T(4,128)S(1)}, s32[108,3]{0,1:T(4,128)}, u32[]{:S(2)}) copy-start(s32[108,3]{0,1:T(4,128)} %param.20) | copy-start | bytes 3892
  7.1 9.1 %copy-start.13 = (s32[108,2]{0,1:T(2,128)S(1)}, s32[108,2]{0,1:T(2,128)}, u32[]{:S(2)}) copy-start(s32[108,2]{0,1:T(2,128)} %param.18) | copy-start | bytes 2596
  7.1 9.1 %copy-start.15 = (s32[108]{0:T(128)S(1)}, s32[108]{0:T(128)}, u32[]{:S(2)}) copy-start(s32[108]{0:T(128)} %param.19) | copy-start | bytes 1300
  7.1 9.0 %collective-permute-start = (bf16[256,256]{1,0:T(8,128)(2,1)S(1)}, bf16[256,256]{1,0:T(8,128)(2,1)S(1)}, u32[]{:S(2)}, u32[]{:S(2)}) collective-permute-start(bf16[256,256]{1,0:T(8,128)(2,1)S(1)} %dynamic-slice_bitcast_fusion.own), channel_id=1, source_target_pairs={{0,16},{16,0},{1,17},{17,1},{2,18},{18,2},{3,19},{19,3},{4,20},{20... | collective-permute-start | bytes 393224 | tf_op jit(solution)/shard_map/ppermute | solution.py:555
  13.0 1.5 %copy-start = (bf16[2,3328,128]{2,1,0:T(8,128)(2,1)S(1)}, bf16[2,3328,128]{2,1,0:T(8,128)(2,1)}, u32[]{:S(2)}) copy-start(bf16[2,3328,128]{2,1,0:T(8,128)(2,1)} %constant.44.clone.tables) | copy-start | bytes 5111812
  14.4 1.7 %copy-start.1 = (bf16[2,3328,128]{2,1,0:T(8,128)(2,1)S(1)}, bf16[2,3328,128]{2,1,0:T(8,128)(2,1)}, u32[]{:S(2)}) copy-start(bf16[2,3328,128]{2,1,0:T(8,128)(2,1)} %constant.44.clone.tables) | copy-start | bytes 5111812
  18.9 19.2 %copy-start.4 = (bf16[11,96,128]{2,1,0:T(8,128)(2,1)S(1)}, bf16[11,96,128]{2,1,0:T(8,128)(2,1)}, u32[]{:S(2)}) copy-start(bf16[11,96,128]{2,1,0:T(8,128)(2,1)} %constant.48.clone.vlo) | copy-start | bytes 811012
  18.9 19.2 %copy-start.5 = (bf16[11,96,128]{2,1,0:T(8,128)(2,1)S(1)}, bf16[11,96,128]{2,1,0:T(8,128)(2,1)}, u32[]{:S(2)}) copy-start(bf16[11,96,128]{2,1,0:T(8,128)(2,1)} %constant.47.clone.vhi) | copy-start | bytes 811012
  18.9 19.2 %copy-start.6 = (bf16[2,2,256,128]{3,2,1,0:T(8,128)(2,1)S(1)}, bf16[2,2,256,128]{3,2,1,0:T(8,128)(2,1)}, u32[]{:S(2)}) copy-start(bf16[2,2,256,128]{3,2,1,0:T(8,128)(2,1)} %constant.49.clone.steps) | copy-start | bytes 786436
  18.9 19.2 %copy-start.7 = (bf16[2,512,128]{2,1,0:T(8,128)(2,1)S(1)}, bf16[2,512,128]{2,1,0:T(8,128)(2,1)}, u32[]{:S(2)}) copy-start(bf16[2,512,128]{2,1,0:T(8,128)(2,1)} %constant.46.clone.depth) | copy-start | bytes 786436
  18.9 19.2 %copy-start.10 = (f32[4,16,128]{2,1,0:T(8,128)S(1)}, f32[4,16,128]{2,1,0:T(8,128)}, u32[]{:S(2)}) copy-start(f32[4,16,128]{2,1,0:T(8,128)} %constant.50.clone.shift) | copy-start | bytes 98308
  18.9 19.2 %copy-start.14 = (f32[2,32]{1,0:T(2,128)S(1)}, f32[2,32]{1,0:T(2,128)}, u32[]{:S(2)}) copy-start(f32[2,32]{1,0:T(2,128)} %constant.45.clone.circle) | copy-start | bytes 772
  18.9 33.9 %copy-start.3 = (f32[16,16,128]{2,1,0:T(8,128)S(1)}, f32[16,16,128]{2,1,0:T(8,128)}, u32[]{:S(2)}) copy-start(f32[16,16,128]{2,1,0:T(8,128)} %constant.51.clone.turns) | copy-start | bytes 393220
  18.9 33.9 %copy-start.8 = (f32[3,4,8,128]{3,2,1,0:T(8,128)S(1)}, f32[3,4,8,128]{3,2,1,0:T(8,128)}, u32[]{:S(2)}) copy-start(f32[3,4,8,128]{3,2,1,0:T(8,128)} %constant.52.clone.places) | copy-start | bytes 147460
  38.1 41.3 %copy-start.9 = (f32[128,64]{1,0:T(8,128)S(1)}, f32[128,64]{1,0:T(8,128)}, u32[]{:S(2)}) copy-start(f32[128,64]{1,0:T(8,128)} %constant.53.clone.graph) | copy-start | bytes 98308
  38.2 41.2 %copy-start.11 = (bf16[64,128]{1,0:T(8,128)(2,1)S(1)}, bf16[64,128]{1,0:T(8,128)(2,1)}, u32[]{:S(2)}) copy-start(bf16[64,128]{1,0:T(8,128)(2,1)} %constant.54.clone.turned) | copy-start | bytes 49156
  53.8 25.6 %all-to-all-start.2 = ((f32[16,8,128]{2,1,0:T(8,128)}), f32[16,8,128]{2,1,0:T(8,128)S(1)}, u32[]{:S(2)}, u32[]{:S(2)}) async-start(f32[16,8,128]{2,1,0:T(8,128)} %shard_map.188.ignored), calls=%async_computation.2 | async-start | bytes 131072 | tf_op jit(solution)/shard_map/all_to_all | solution.py:601
  68.5 5.0 %collective-permute-start.2 = (f32[9,8,128]{2,1,0:T(8,128)S(1)}, f32[9,8,128]{2,1,0:T(8,128)S(1)}, u32[]{:S(2)}, u32[]{:S(2)}) collective-permute-start(f32[9,8,128]{2,1,0:T(8,128)S(1)} %shard_map.189.mine), channel_id=1, source_target_pairs={{32,0},{64,32},{96,64},{128,96},{160,128},{192,160},{224,192},{256... | collective-permute-start | bytes 110600 | tf_op jit(solution)/shard_map/ppermute | solution.py:600

commit v7 on v6

--- a/solution.py
+++ b/solution.py
@@ -210,7 +210,8 @@
 
 
 def across_dft(strip, half, tables):
-    both = dot(across_rows(tables, half, 0), strip) + dot(across_rows(tables, half, 1), strip)
+    both = dot(wide_rows(tables, 2 * half * HALF_ROWS, 2 * HALF_ROWS), strip)
+    both = both[:HALF_ROWS] + both[HALF_ROWS:]
     rows = SUBS * LOCAL
     return jnp.concatenate([both[:rows], both[rows:]], axis=1)
 
@@ -312,8 +313,9 @@
         copy.wait()
 
 
-def spectrum_of(block, zeroth, held, depth_hi, depth_lo):
-    both = dot(depth_hi, block) + dot(depth_lo, block)
+def spectrum_of(block, zeroth, held, depth_both):
+    both = dot(depth_both, block)
+    both = both[:256] + both[256:]
     cos, sin = both[:DEPTH], both[DEPTH:]
     cos_re, cos_im = cos[:, :HALF], cos[:, HALF:]
     sin_re, sin_im = sin[:, :HALF], sin[:, HALF:]
@@ -363,11 +365,11 @@
 
     held = special(row // 64)
     edge = edges(2 * DEPTH, lambda row: row // DEPTH)
-    depth_hi, depth_lo = wide_rows(depth, 0, 256), wide_rows(depth, 256, 256)
+    depth_both = wide_rows(depth, 0, 512)
 
     def spectrum(slot, held):
         block = got[:, 16 * slot : 16 * slot + 16, :].reshape(2 * DEPTH, 2 * HALF)
-        return spectrum_of(block, zeroth, held, depth_hi, depth_lo)
+        return spectrum_of(block, zeroth, held, depth_both)
 
     small_lane = lax.broadcasted_iota(jnp.int32, (16, HALF), 1)
 
@@ -375,7 +377,8 @@
         off_z, off_y, off_x = meta[slot, 0], meta[slot, 1], meta[slot, 2]
         high, low = split(jnp.concatenate(phase, axis=1))
         table_hi, table_lo = vhi[off_z + MAX_OFF], vlo[off_z + MAX_OFF]
-        rows = dot(table_hi, high) + dot(table_lo, high) + dot(table_hi, low)
+        rows = dot(jnp.concatenate([table_hi, table_lo], axis=0), high)
+        rows = rows[:96] + rows[96:] + dot(table_hi, low)
         part = [(rows[16 * k : 16 * k + 16, :HALF], rows[16 * k : 16 * k + 16, HALF:]) for k in range(6)]
         held = small_lane == half * (HALF - 1) + nowhere
         real = jnp.where(held, part[2][0] - part[3][1], part[0][0] - part[1][1])

time: 80.8 us -> 81.3 us (level)
  transfers between devices with their start and end apart: 4 -> 4, of which waited for: 2 -> 2; matrix products, arithmetic and copies ran while one was open for 1% -> 1% of each run, Pallas kernels for 6% -> 7%
where the time goes in v7:
time: 81.3 us; the launch traced here: 80.9 us
  blocking collectives  31 us (38%)
  starting transfers between devices  25.5 us (31%)
  Pallas kernels  11.8 us (15%)
  waiting for transfers between devices  8.05 us (10%)
  local copies, waits for them, and re-layouts  3.54 us (4%)
  between operations  0.91 us (1%)
    all_to_all x1, blocking collectives, local(): got = lax.all_to_all(sent, 'sub', split_axis=0, concat_axis=0, tiled=True)  19.1 us
    all_to_all x1, starting transfers between devices, local(): lax.all_to_all(terms, 'z', split_axis=0, concat_axis=0, tiled=True)  14 us
    all_to_all x1, blocking collectives, local(): lax.all_to_all(partial, ('core', 'sub'), split_axis=0, concat_axis=0, til...  11.9 us
    pallas_call x8, Pallas kernels, call(): pl.pallas_call(kernel, out_shape=shapes, in_specs=specs, out_specs=outs,...  11.8 us
    ppermute x1, starting transfers between devices, local(): other = lax.ppermute(own, 'core', [(0, 1), (1, 0)])  5.84 us
    ppermute x1, starting transfers between devices, local(): lax.ppermute(bottoms, 'z', [(k, k + 1) for k in range(PLANES - 1)])  4.39 us
    all_to_all x1, waiting for transfers between devices, local(): lax.all_to_all(terms, 'z', split_axis=0, concat_axis=0, tiled=True)  4.35 us
    ppermute x1, waiting for transfers between devices, local(): below = lax.ppermute(mine, 'z', [(k + 1, k) for k in range(PLANES - 1)])  3.7 us
  transfers between devices with their start and end apart: 4, of which 2 were waited for; matrix products, arithmetic and copies ran while one was open for 1% of the time, Pallas kernels for 7%

profile of v7, /device:TPU:1, one launch (start us, length us, event | category | flops | bytes accessed | tf_op | source)
XLA Modules:
  0.0 80.9 jit_solution(14671291306246803700)
XLA Ops:
  0.6 0.0 copy-start.2
  0.6 1.1 %fusion = (bf16[1,256,256]{2,1,0:T(8,128)(2,1)S(1)}, bf16[1,256,256]{2,1,0:T(8,128)(2,1)S(1)}) fusion(bf16[8,256,256]{2,1,0:T(8,128)(2,1)} %bitcast.10), kind=kLoop, calls=%fused_computation.3 | loop fusion | bytes 524288 | tf_op jit(solution)/shard_map/slice | solution.py:554
  1.8 4.4 %collective-permute-start.1 = (bf16[2,256,256]{2,1,0:T(8,128)(2,1)S(1)}, bf16[2,256,256]{2,1,0:T(8,128)(2,1)S(1)}, u32[]{:S(2)}, u32[]{:S(2)}) collective-permute-start(bf16[2,256,256]{2,1,0:T(8,128)(2,1)S(1)} %pad_maximum_fusion), channel_id=1, source_target_pairs={{0,32},{32,64},{64,96},{96,128},{128,160},{160,192},{192,224},{224... | collective-permute-start | bytes 786440 | tf_op jit(solution)/shard_map/ppermute | solution.py:555
  6.2 0.9 %dynamic-slice_bitcast_fusion.own = bf16[256,256]{1,0:T(8,128)(2,1)S(1)} fusion(bf16[8,256,256]{2,1,0:T(8,128)(2,1)} %bitcast.11, s32[]{:T(128)S(6)} %select_n.4), kind=kLoop, calls=%fused_computation.1 | loop fusion | bytes 262148 | tf_op jit(solution)/shard_map/jit(dynamic_index_in_dim)/squeeze | solution.py:557
  7.1 5.8 %collective-permute-start = (bf16[256,256]{1,0:T(8,128)(2,1)S(1)}, bf16[256,256]{1,0:T(8,128)(2,1)S(1)}, u32[]{:S(2)}, u32[]{:S(2)}) collective-permute-start(bf16[256,256]{1,0:T(8,128)(2,1)S(1)} %dynamic-slice_bitcast_fusion.own), channel_id=1, source_target_pairs={{0,16},{16,0},{1,17},{17,1},{2,18},{18,2},{3,19},{19,3},{4,20},{20... | collective-permute-start | bytes 393224 | tf_op jit(solution)/shard_map/ppermute | solution.py:558
  13.0 0.0 copy-start
  13.0 1.4 %copy-done = bf16[2,3328,128]{2,1,0:T(8,128)(2,1)S(1)} copy-done((bf16[2,3328,128]{2,1,0:T(8,128)(2,1)S(1)}, bf16[2,3328,128]{2,1,0:T(8,128)(2,1)}, u32[]{:S(2)}) %copy-start) | copy-done | bytes 1703960
  14.4 2.2 %shard_map.184.ignored.here = bf16[16,64,256]{2,1,0:T(8,128)(2,1)S(1)} custom-call(bf16[8,256,256]{2,1,0:T(8,128)(2,1)S(1)} %bitcast.12, bf16[2,3328,128]{2,1,0:T(8,128)(2,1)S(1)} %copy-done), custom_call_target="tpu_custom_call" | custom-call | tf_op jit(solution)/shard_map/pallas_call | solution.py:536
  16.6 0.1 pad_add_fusion.where
  16.7 1.4 %shard_map.185 = (bf16[16,16,256]{2,1,0:T(8,128)(2,1)S(1)}, s32[16,128]{1,0:T(8,128)S(1)}, f32[8,128]{1,0:T(8,128)S(1)}) custom-call(s32[3]{0:T(128)S(1)} %pad_add_fusion.where, bf16[256,256]{1,0:T(8,128)(2,1)S(1)} %dynamic-slice_bitcast_fusion.own, bf16[256,256]{1,0:T(8,128)(2,1)S(1)} %collective-permute-done.other, bf16[2,3328,128]{2,1,0:T(8,128)(2,1)S(1)} %copy-done.1, ...), custom_call_target="tpu_custom_call" | custom-call | tf_op jit(solution)/shard_map/pallas_call | solution.py:536
  18.1 1.3 %shard_map.186 = bf16[16,112,256]{2,1,0:T(8,128)(2,1)S(1)} custom-call(bf16[16,64,256]{2,1,0:T(8,128)(2,1)S(1)} %shard_map.184.ignored.here, bf16[16,16,256]{2,1,0:T(8,128)(2,1)S(1)} %get-tuple-element.13.seam, bf16[2,256,256]{2,1,0:T(8,128)(2,1)S(1)} %collective-permute-done.1.below, bf16[2,3328,128]{2,1,0:T(8,128)(2,1)S(1)} %copy-done.1), custom_call_target="tpu_custom_call" | custom-call | tf_op jit(solution)/shard_map/pallas_call | solution.py:536
  19.4 0.0 copy-start.4
  19.4 0.0 copy-start.5
  19.5 19.1 %all_to_all.15.got = bf16[16,112,256]{2,1,0:T(8,128)(2,1)S(1)} all-to-all(bf16[16,112,256]{2,1,0:T(8,128)(2,1)S(1)} %shard_map.186), channel_id=1, replica_groups=mesh['z'=16,'core'=2,'sub'=16] {'sub'}, dimensions={0} | all-to-all | bytes 1835008 | tf_op jit(solution)/shard_map/all_to_all | solution.py:583
  38.7 2.8 %shard_map.187 = f32[32,8,128]{2,1,0:T(8,128)S(1)} custom-call(s32[3]{0:T(128)S(1)} %pad_add_fusion.where, s32[16,128]{1,0:T(8,128)S(1)} %get-tuple-element.12.meta, f32[2,32]{1,0:T(2,128)S(1)} %copy-done.14, bf16[16,112,256]{2,1,0:T(8,128)(2,1)S(1)} %all_to_all.15.got, bf16[2,512,128]{2,1,0:T(8,128)(2,1)S(1)} %copy-done.7, ...), custom_call_target="tpu_custom_call" | custom-call | tf_op jit(solution)/shard_map/pallas_call | solution.py:536
  41.5 11.9 %all_to_all.16.got = f32[32,8,128]{2,1,0:T(8,128)S(1)} all-to-all(f32[32,8,128]{2,1,0:T(8,128)S(1)} %shard_map.187), channel_id=1, replica_groups=mesh['z'=16,'core'=2,'sub'=16] {'core','sub'}, dimensions={0} | all-to-all | bytes 262144 | tf_op jit(solution)/shard_map/all_to_all | solution.py:590
  53.4 1.0 %shard_map.188.ignored = f32[16,8,128]{2,1,0:T(8,128)} custom-call(f32[32,8,128]{2,1,0:T(8,128)S(1)} %all_to_all.16.got, f32[8,128]{1,0:T(8,128)S(1)} %get-tuple-element.14.offsets, f32[16,16,128]{2,1,0:T(8,128)S(1)} %copy-done.3, f32[3,4,8,128]{3,2,1,0:T(8,128)S(1)} %copy-done.8), custom_call_target="tpu_custom_call" | custom-call | tf_op jit(solution)/shard_map/pallas_call | solution.py:536
  54.3 14.0 %all-to-all-start.2 = ((f32[16,8,128]{2,1,0:T(8,128)}), f32[16,8,128]{2,1,0:T(8,128)S(1)}, u32[]{:S(2)}, u32[]{:S(2)}) async-start(f32[16,8,128]{2,1,0:T(8,128)} %shard_map.188.ignored), calls=%async_computation.2 | async-start | bytes 131072 | tf_op jit(solution)/shard_map/all_to_all | solution.py:604
  68.4 0.7 shard_map.189.mine
  69.1 1.3 %collective-permute-start.2 = (f32[9,8,128]{2,1,0:T(8,128)S(1)}, f32[9,8,128]{2,1,0:T(8,128)S(1)}, u32[]{:S(2)}, u32[]{:S(2)}) collective-permute-start(f32[9,8,128]{2,1,0:T(8,128)S(1)} %shard_map.189.mine), channel_id=1, source_target_pairs={{32,0},{64,32},{96,64},{128,96},{160,128},{192,160},{224,192},{256... | collective-permute-start | bytes 110600 | tf_op jit(solution)/shard_map/ppermute | solution.py:603
  70.4 3.7 %collective-permute-done.2.below = f32[9,8,128]{2,1,0:T(8,128)S(1)} collective-permute-done((f32[9,8,128]{2,1,0:T(8,128)S(1)}, f32[9,8,128]{2,1,0:T(8,128)S(1)}, u32[]{:S(2)}, u32[]{:S(2)}) %collective-permute-start.2) | collective-permute-done | bytes 36896 | tf_op jit(solution)/shard_map/ppermute | solution.py:603
  74.1 1.5 %shard_map.190 = (f32[6,729]{1,0:T(8,128)}, f32[8,128]{1,0:T(8,128)S(1)}) custom-call(s32[3]{0:T(128)S(1)} %pad_add_fusion.where, s32[16,128]{1,0:T(8,128)S(1)} %get-tuple-element.12.meta, f32[9,8,128]{2,1,0:T(8,128)S(1)} %shard_map.189.mine, f32[9,8,128]{2,1,0:T(8,128)S(1)} %collective-permute-done.2.below), custom_call_target="tpu_custom_call" | custom-call | tf_op jit(solution)/shard_map/pallas_call | solution.py:536
  75.6 4.4 %all-to-all-done.2.terms = f32[16,8,128]{2,1,0:T(8,128)S(1)} async-done(((f32[16,8,128]{2,1,0:T(8,128)}), f32[16,8,128]{2,1,0:T(8,128)S(1)}, u32[]{:S(2)}, u32[]{:S(2)}) %all-to-all-start.2) | async-done | bytes 65568 | tf_op jit(solution)/shard_map/all_to_all | solution.py:604
  79.9 1.0 %shard_map.191 = (f32[64,64]{1,0:T(8,128)}, f32[3,64]{1,0:T(4,128)}) custom-call(f32[16,8,128]{2,1,0:T(8,128)S(1)} %all-to-all-done.2.terms, f32[128,64]{1,0:T(8,128)S(1)} %copy-done.9, bf16[64,128]{1,0:T(8,128)(2,1)S(1)} %copy-done.11, f32[8,128]{1,0:T(8,128)S(1)} %get-tuple-element.16.ignored), custom_call_target="tpu_custom_call" | custom-call | tf_op jit(solution)/shard_map/pallas_call | solution.py:536
  (30 shorter events, 0.1 us)
Async XLA Ops:
  0.6 12.3 %copy-start.2 = (bf16[2,4,8,32,256]{4,3,2,1,0:T(8,128)(2,1)S(1)}, bf16[2,4,8,32,256]{4,3,2,1,0:T(8,128)(2,1)}, u32[]{:S(2)}) copy-start(bf16[2,4,8,32,256]{4,3,2,1,0:T(8,128)(2,1)} %param.17) | copy-start | bytes 3145732
  1.8 16.3 %collective-permute-start.1 = (bf16[2,256,256]{2,1,0:T(8,128)(2,1)S(1)}, bf16[2,256,256]{2,1,0:T(8,128)(2,1)S(1)}, u32[]{:S(2)}, u32[]{:S(2)}) collective-permute-start(bf16[2,256,256]{2,1,0:T(8,128)(2,1)S(1)} %pad_maximum_fusion), channel_id=1, source_target_pairs={{0,32},{32,64},{64,96},{96,128},{128,160},{160,192},{192,224},{224... | collective-permute-start | bytes 786440 | tf_op jit(solution)/shard_map/ppermute | solution.py:555
  7.1 9.6 %copy-start.12 = (s32[108,3]{0,1:T(4,128)S(1)}, s32[108,3]{0,1:T(4,128)}, u32[]{:S(2)}) copy-start(s32[108,3]{0,1:T(4,128)} %param.20) | copy-start | bytes 3892
  7.1 9.6 %copy-start.13 = (s32[108,2]{0,1:T(2,128)S(1)}, s32[108,2]{0,1:T(2,128)}, u32[]{:S(2)}) copy-start(s32[108,2]{0,1:T(2,128)} %param.18) | copy-start | bytes 2596
  7.1 9.6 %copy-start.15 = (s32[108]{0:T(128)S(1)}, s32[108]{0:T(128)}, u32[]{:S(2)}) copy-start(s32[108]{0:T(128)} %param.19) | copy-start | bytes 1300
  7.1 9.6 %collective-permute-start = (bf16[256,256]{1,0:T(8,128)(2,1)S(1)}, bf16[256,256]{1,0:T(8,128)(2,1)S(1)}, u32[]{:S(2)}, u32[]{:S(2)}) collective-permute-start(bf16[256,256]{1,0:T(8,128)(2,1)S(1)} %dynamic-slice_bitcast_fusion.own), channel_id=1, source_target_pairs={{0,16},{16,0},{1,17},{17,1},{2,18},{18,2},{3,19},{19,3},{4,20},{20... | collective-permute-start | bytes 393224 | tf_op jit(solution)/shard_map/ppermute | solution.py:558
  13.0 1.5 %copy-start = (bf16[2,3328,128]{2,1,0:T(8,128)(2,1)S(1)}, bf16[2,3328,128]{2,1,0:T(8,128)(2,1)}, u32[]{:S(2)}) copy-start(bf16[2,3328,128]{2,1,0:T(8,128)(2,1)} %constant.44.clone.tables) | copy-start | bytes 5111812
  14.4 2.3 %copy-start.1 = (bf16[2,3328,128]{2,1,0:T(8,128)(2,1)S(1)}, bf16[2,3328,128]{2,1,0:T(8,128)(2,1)}, u32[]{:S(2)}) copy-start(bf16[2,3328,128]{2,1,0:T(8,128)(2,1)} %constant.44.clone.tables) | copy-start | bytes 5111812
  19.4 19.2 %copy-start.4 = (bf16[11,96,128]{2,1,0:T(8,128)(2,1)S(1)}, bf16[11,96,128]{2,1,0:T(8,128)(2,1)}, u32[]{:S(2)}) copy-start(bf16[11,96,128]{2,1,0:T(8,128)(2,1)} %constant.48.clone.vlo) | copy-start | bytes 811012
  19.4 19.2 %copy-start.5 = (bf16[11,96,128]{2,1,0:T(8,128)(2,1)S(1)}, bf16[11,96,128]{2,1,0:T(8,128)(2,1)}, u32[]{:S(2)}) copy-start(bf16[11,96,128]{2,1,0:T(8,128)(2,1)} %constant.47.clone.vhi) | copy-start | bytes 811012
  19.4 19.2 %copy-start.6 = (bf16[2,2,256,128]{3,2,1,0:T(8,128)(2,1)S(1)}, bf16[2,2,256,128]{3,2,1,0:T(8,128)(2,1)}, u32[]{:S(2)}) copy-start(bf16[2,2,256,128]{3,2,1,0:T(8,128)(2,1)} %constant.49.clone.steps) | copy-start | bytes 786436
  19.4 19.2 %copy-start.7 = (bf16[2,512,128]{2,1,0:T(8,128)(2,1)S(1)}, bf16[2,512,128]{2,1,0:T(8,128)(2,1)}, u32[]{:S(2)}) copy-start(bf16[2,512,128]{2,1,0:T(8,128)(2,1)} %constant.46.clone.depth) | copy-start | bytes 786436
  19.4 19.2 %copy-start.10 = (f32[4,16,128]{2,1,0:T(8,128)S(1)}, f32[4,16,128]{2,1,0:T(8,128)}, u32[]{:S(2)}) copy-start(f32[4,16,128]{2,1,0:T(8,128)} %constant.50.clone.shift) | copy-start | bytes 98308
  19.4 19.2 %copy-start.14 = (f32[2,32]{1,0:T(2,128)S(1)}, f32[2,32]{1,0:T(2,128)}, u32[]{:S(2)}) copy-start(f32[2,32]{1,0:T(2,128)} %constant.45.clone.circle) | copy-start | bytes 772
  19.5 33.9 %copy-start.3 = (f32[16,16,128]{2,1,0:T(8,128)S(1)}, f32[16,16,128]{2,1,0:T(8,128)}, u32[]{:S(2)}) copy-start(f32[16,16,128]{2,1,0:T(8,128)} %constant.51.clone.turns) | copy-start | bytes 393220
  19.5 33.9 %copy-start.8 = (f32[3,4,8,128]{3,2,1,0:T(8,128)S(1)}, f32[3,4,8,128]{3,2,1,0:T(8,128)}, u32[]{:S(2)}) copy-start(f32[3,4,8,128]{3,2,1,0:T(8,128)} %constant.52.clone.places) | copy-start | bytes 147460
  38.6 41.3 %copy-start.9 = (f32[128,64]{1,0:T(8,128)S(1)}, f32[128,64]{1,0:T(8,128)}, u32[]{:S(2)}) copy-start(f32[128,64]{1,0:T(8,128)} %constant.53.clone.graph) | copy-start | bytes 98308
  38.7 41.3 %copy-start.11 = (bf16[64,128]{1,0:T(8,128)(2,1)S(1)}, bf16[64,128]{1,0:T(8,128)(2,1)}, u32[]{:S(2)}) copy-start(bf16[64,128]{1,0:T(8,128)(2,1)} %constant.54.clone.turned) | copy-start | bytes 49156
  54.3 25.6 %all-to-all-start.2 = ((f32[16,8,128]{2,1,0:T(8,128)}), f32[16,8,128]{2,1,0:T(8,128)S(1)}, u32[]{:S(2)}, u32[]{:S(2)}) async-start(f32[16,8,128]{2,1,0:T(8,128)} %shard_map.188.ignored), calls=%async_computation.2 | async-start | bytes 131072 | tf_op jit(solution)/shard_map/all_to_all | solution.py:604
  69.1 5.0 %collective-permute-start.2 = (f32[9,8,128]{2,1,0:T(8,128)S(1)}, f32[9,8,128]{2,1,0:T(8,128)S(1)}, u32[]{:S(2)}, u32[]{:S(2)}) collective-permute-start(f32[9,8,128]{2,1,0:T(8,128)S(1)} %shard_map.189.mine), channel_id=1, source_target_pairs={{32,0},{64,32},{96,64},{128,96},{160,128},{192,160},{224,192},{256... | collective-permute-start | bytes 110600 | tf_op jit(solution)/shard_map/ppermute | solution.py:603
